TPU v7x, 256 devices: a whole 4x4x8 slice. The times are simulated.
256 devices in a mesh: head: 4 (over z_lo), blk: 64 (over x, z_hi, y, core).
Axes of the slice: x: 4, y: 4, z: 8 (z_hi: 2, z_lo: 4; z = z_hi * 4 + z_lo), core: 2. Of those that a mesh axis runs over, the one named last changes fastest.
Arguments:
- queries: bfloat16 [16384, 2048], P(('blk', 'head')), may hold values from -30 to 30
- keys: bfloat16 [16384, 256], P(('blk', 'head')), may hold values from -30 to 30
- values: bfloat16 [16384, 256], P(('blk', 'head')), may hold values from -6 to 6
- outputs: bfloat16 [16384, 2048], P(('blk', 'head')), may hold values from -6 to 6
- out_grad: bfloat16 [16384, 2048], P(('blk', 'head')), may hold values from -6 to 6
- order: int32 [128], replicated, may hold values from 0 to 127, as said below
Outputs:
- query_grad: bfloat16 [16384, 2048], P(('blk', 'head'))
- key_grad: bfloat16 [16384, 256], P(('blk', 'head'))
- value_grad: bfloat16 [16384, 256], P(('blk', 'head'))
Inputs may be any that keep to these rules, and one draw needn't show every extreme that they name: Layout block p holds rows p * 128 to (p + 1) * 128 - 1 and the tokens of sequence block order[p]; for every p < 64, order[2 * p] = m and order[2 * p + 1] = 127 - m, where the m of the pairs run over a permutation of 0 to 63.
All inputs are finite; a program needn't handle non-finite values.
Results may differ from a plain program's by a relative error of at most 0.017.
Values may be sent and summed in bfloat16 or wider, within the bound.
No kernel may reach another device: no remote copies, remote signals or barrier semaphores. Data moves between devices by JAX's collectives and lax.ppermute only.
A program may use at most 64 MiB of HBM per device.

v0:
```python
from functools import partial
import math

import jax
import jax.numpy as jnp
from jax import lax
from jax.sharding import PartitionSpec as P

HEAD_DIM = 128


def passed_along(value, axis, steps):
    count = lax.axis_size(axis)
    pairs = [(source, (source + steps) % count) for source in range(count)]
    return lax.ppermute(value, axis, pairs)


def lookup(table, wanted):
    places = jnp.arange(table.shape[0], dtype=jnp.int32)
    return jnp.sum(jnp.where(wanted[:, None] == places[None, :], table[None, :], 0), axis=1)


def dot_rows(left, right):
    return lax.dot_general(
        left, right, (((1,), (1,)), ((), ())), preferred_element_type=jnp.float32
    )


def dot_columns(left, right):
    return lax.dot_general(
        left, right, (((0,), (0,)), ((), ())), preferred_element_type=jnp.float32
    )


def body(queries, keys, values, outputs, out_grad, order):
    factor = HEAD_DIM ** (-0.5)
    n_blk = lax.axis_size("blk")
    n_head = lax.axis_size("head")
    position = lax.axis_index("blk")
    head_index = lax.axis_index("head")
    kv_count = keys.shape[1] // HEAD_DIM
    grouped = n_head // kv_count
    local_q, local_out, local_grad = (
        lax.all_to_all(queries, "head", split_axis=1, concat_axis=0, tiled=True),
        lax.all_to_all(outputs, "head", split_axis=1, concat_axis=0, tiled=True),
        lax.all_to_all(out_grad, "head", split_axis=1, concat_axis=0, tiled=True),
    )
    row_count = local_q.shape[0]
    head_count = local_q.shape[1] // HEAD_DIM
    block_len = row_count // 2
    all_keys, all_values = (
        lax.all_gather(keys, "head", axis=0, tiled=True),
        lax.all_gather(values, "head", axis=0, tiled=True),
    )
    offset = head_index // grouped * HEAD_DIM
    key_rows = lax.dynamic_slice_in_dim(all_keys, offset, HEAD_DIM, 1)
    value_rows = lax.dynamic_slice_in_dim(all_values, offset, HEAD_DIM, 1)
    flat_q = local_q.reshape(row_count * head_count, HEAD_DIM)
    flat_grad = local_grad.reshape(row_count * head_count, HEAD_DIM)
    flat_out = local_out.reshape(row_count * head_count, HEAD_DIM)
    row_delta = jnp.sum(flat_grad.astype(jnp.float32) * flat_out.astype(jnp.float32), axis=1)
    own_blocks = lookup(order, 2 * position + jnp.arange(2, dtype=jnp.int32))
    token_pos = (
        jnp.repeat(own_blocks, block_len) * block_len
        + jnp.arange(row_count, dtype=jnp.int32) % block_len
    )
    row_pos = jnp.repeat(token_pos, head_count)
    latest = jnp.max(token_pos)
    start_max = jnp.full((row_count * head_count,), -1e30, jnp.float32)
    start_sum = jnp.zeros((row_count * head_count,), jnp.float32)
    loop_state = (start_max, start_sum)
    piece = lax.all_gather(key_rows, "blk", axis=0, tiled=True)
    piece_rows = piece.shape[0]
    step_rows = math.gcd(piece_rows, 2 * block_len)

    def one_block(step_index, loop_state):
        key_block = lax.dynamic_slice_in_dim(piece, step_index * step_rows, step_rows, 0)
        row_index = step_index * step_rows + jnp.arange(step_rows, dtype=jnp.int32)
        key_pos = lookup(order, row_index // block_len) * block_len + row_index % block_len

        def update(loop_state):
            running_max, running_sum = loop_state
            scores = dot_rows(flat_q, key_block) * factor
            valid_mask = key_pos[None, :] <= row_pos[:, None]
            new_max = jnp.maximum(
                running_max, jnp.max(jnp.where(valid_mask, scores, -1e30), axis=1)
            )
            running_sum = running_sum * jnp.exp(running_max - new_max) + jnp.sum(
                jnp.where(valid_mask, jnp.exp(scores - new_max[:, None]), 0.0), axis=1
            )
            return (new_max, running_sum)

        return lax.cond(jnp.min(key_pos) <= latest, update, lambda unchanged: unchanged, loop_state)

    running_max, running_sum = lax.fori_loop(0, piece_rows // step_rows, one_block, loop_state)
    lse = running_max + jnp.log(running_sum)
    part_rows = block_len * head_count
    query_pieces = [
        flat_q[slot_index * part_rows : (slot_index + 1) * part_rows] for slot_index in range(2)
    ]
    grad_pieces = [
        flat_grad[slot_index * part_rows : (slot_index + 1) * part_rows] for slot_index in range(2)
    ]
    lse_pieces = [
        lse[slot_index * part_rows : (slot_index + 1) * part_rows] for slot_index in range(2)
    ]
    delta_pieces = [
        row_delta[slot_index * part_rows : (slot_index + 1) * part_rows] for slot_index in range(2)
    ]
    pos_pieces = [
        row_pos[slot_index * part_rows : (slot_index + 1) * part_rows] for slot_index in range(2)
    ]

    def tile_grads(query_slot, key_block, value_block, block_id, tile_state):
        query_part, key_acc, value_acc = tile_state
        key_pos = block_id * block_len + jnp.arange(block_len, dtype=jnp.int32)
        scores = dot_rows(query_pieces[query_slot], key_block) * factor
        valid_mask = key_pos[None, :] <= pos_pieces[query_slot][:, None]
        weights = jnp.where(valid_mask, jnp.exp(scores - lse_pieces[query_slot][:, None]), 0.0)
        weights_b = weights.astype(jnp.bfloat16)
        value_acc = value_acc + dot_columns(weights_b, grad_pieces[query_slot])
        dprob = dot_rows(grad_pieces[query_slot], value_block)
        score_grad = (weights * (dprob - delta_pieces[query_slot][:, None]) * factor).astype(
            jnp.bfloat16
        )
        query_part = query_part + jnp.dot(score_grad, key_block, preferred_element_type=jnp.float32)
        key_acc = key_acc + dot_columns(score_grad, query_pieces[query_slot])
        return (query_part, key_acc, value_acc)

    def visit_keys(query_parts, key_block, value_block, block_id, key_acc, value_acc):
        query_parts = list(query_parts)
        for query_slot in range(2):
            tile_state = (query_parts[query_slot], key_acc, value_acc)
            tile_state = lax.cond(
                own_blocks[query_slot] >= block_id,
                partial(tile_grads, query_slot, key_block, value_block, block_id),
                lambda unchanged: unchanged,
                tile_state,
            )
            query_parts[query_slot], key_acc, value_acc = tile_state
        return (query_parts, key_acc, value_acc)

    def work_turn(block_ids, loop_state):
        keys_now, values_now, key_grads, value_grads, first_q, second_q = loop_state
        query_parts = [first_q, second_q]
        key_accs = []
        value_accs = []
        for key_slot in range(2):
            query_parts, key_acc, value_acc = visit_keys(
                query_parts,
                keys_now[key_slot],
                values_now[key_slot],
                block_ids[key_slot],
                key_grads[key_slot],
                value_grads[key_slot],
            )
            key_accs.append(key_acc)
            value_accs.append(value_acc)
        return (query_parts, key_accs, value_accs)

    key_state = key_rows.reshape(2, block_len, HEAD_DIM)
    value_state = value_rows.reshape(2, block_len, HEAD_DIM)
    zero_grads = jnp.zeros((2, block_len, HEAD_DIM), jnp.float32)
    zero_query = jnp.zeros((part_rows, HEAD_DIM), jnp.float32)
    slot_offsets = jnp.arange(2, dtype=jnp.int32)

    def advance(step_index, loop_state):
        keys_now, values_now = (loop_state[0], loop_state[1])
        root = (position - step_index) % n_blk
        block_ids = lookup(order, 2 * root + slot_offsets)
        query_parts, key_accs, value_accs = work_turn(block_ids, loop_state)
        next_keys, next_values = passed_along((keys_now, values_now), "blk", 1)
        next_kgrad, next_vgrad = passed_along(
            (jnp.stack(key_accs), jnp.stack(value_accs)), "blk", 1
        )
        return (next_keys, next_values, next_kgrad, next_vgrad, query_parts[0], query_parts[1])

    start_state = (key_state, value_state, zero_grads, zero_grads, zero_query, zero_query)
    final_state = lax.fori_loop(0, n_blk, advance, start_state)
    key_grads, value_grads, first_q, second_q = (
        final_state[2],
        final_state[3],
        final_state[4],
        final_state[5],
    )
    query_local = (
        jnp.concatenate([first_q, second_q], axis=0)
        .astype(jnp.bfloat16)
        .reshape(row_count, head_count * HEAD_DIM)
    )
    query_grad = lax.all_to_all(query_local, "head", split_axis=0, concat_axis=1, tiled=True)
    key_back, value_back = (
        lax.all_to_all(
            key_grads.reshape(row_count, HEAD_DIM).astype(jnp.bfloat16),
            "head",
            split_axis=0,
            concat_axis=1,
            tiled=True,
        ).astype(jnp.float32),
        lax.all_to_all(
            value_grads.reshape(row_count, HEAD_DIM).astype(jnp.bfloat16),
            "head",
            split_axis=0,
            concat_axis=1,
            tiled=True,
        ).astype(jnp.float32),
    )
    token_rows = key_back.shape[0]

    def fold_groups(matrix):
        return (
            matrix.reshape(token_rows, kv_count, grouped, HEAD_DIM)
            .sum(axis=2)
            .reshape(token_rows, kv_count * HEAD_DIM)
            .astype(jnp.bfloat16)
        )

    return (query_grad, fold_groups(key_back), fold_groups(value_back))


def solution(mesh):
    return jax.shard_map(
        body,
        mesh=mesh,
        in_specs=(
            P(("blk", "head"), None),
            P(("blk", "head"), None),
            P(("blk", "head"), None),
            P(("blk", "head"), None),
            P(("blk", "head"), None),
            P(),
        ),
        out_specs=(P(("blk", "head"), None), P(("blk", "head"), None), P(("blk", "head"), None)),
        check_vma=False,
    )
```

profile of v0, /device:TPU:32, one launch (start us, length us, event | category | flops | bytes accessed | tf_op | source)
XLA Modules:
  0.0 2077.0 jit_solution(4288057238504518007)
XLA Ops:
  7.2 14.8 all_gather.9
  72.4 43.9 %all-gather.2.cloned.1.call-done = bf16[16384,128]{1,0:T(8,128)(2,1)} async-done(((bf16[256,128]{1,0:T(8,128)(2,1)}), bf16[16384,128]{1,0:T(8,128)(2,1)}) %all-gather.2.cloned.1.call-update) | async-done | bytes 4194320 | tf_op jit(solution)/shard_map/all_gather | solution.py:72
  116.3 250.1 %while.44 = (s32[]{:T(128)}, f32[1024]{0:T(1024)S(1)}, f32[1024]{0:T(1024)S(1)}, s32[128]{0:T(128)S(1)}, s32[]{:T(128)}, /*index=5*/bf16[16384,128]{1,0:T(8,128)...) while((s32[]{:T(128)}, f32[1024]{0:T(1024)S(1)}, ...), condition=%wide.region_9.10_spmd.clone, body=%wide.region_2.9_spmd.clone.sunk | while | flops 69314048 | bytes 2507537 | solution.py:95
  366.5 1673.0 %while.45 = (s32[]{:T(128)}, bf16[2,128,128]{2,1,0:T(8,128)(2,1)S(1)}, bf16[2,128,128]{2,1,0:T(8,128)(2,1)S(1)}, f32[2,128,128]{2,1,0:T(8,128)S(1)}, f32[2,128,1...) while((s32[]{:T(128)}, ...), condition=%wide.region_21.22_spmd.clone, body=%wide.region_11.21_spmd.clone.sunk | while | flops 338363648 | bytes 13544166 | solution.py:179
  380.6 15.0 collective-permute-done
  407.2 18.5 collective-permute-done
  437.2 16.5 collective-permute-done
  465.3 14.5 collective-permute-done
  491.3 14.4 collective-permute-done
  517.4 14.4 collective-permute-done
  543.4 14.4 collective-permute-done
  569.5 14.4 collective-permute-done
  595.5 14.4 collective-permute-done
  621.6 14.4 collective-permute-done
  647.5 14.4 collective-permute-done
  673.5 14.4 collective-permute-done
  699.5 14.4 collective-permute-done
  725.6 14.4 collective-permute-done
  751.5 14.4 collective-permute-done
  777.4 14.4 collective-permute-done
  803.4 14.4 collective-permute-done
  829.3 14.4 collective-permute-done
  855.4 14.4 collective-permute-done
  881.3 14.4 collective-permute-done
  907.2 14.4 collective-permute-done
  933.3 14.4 collective-permute-done
  959.2 14.4 collective-permute-done
  985.2 14.4 collective-permute-done
  1011.2 14.4 collective-permute-done
  1037.2 14.4 collective-permute-done
  1063.1 14.4 collective-permute-done
  1089.2 14.4 collective-permute-done
  1115.2 14.4 collective-permute-done
  1141.2 14.4 collective-permute-done
  1167.1 14.4 collective-permute-done
  1193.0 14.4 collective-permute-done
  1219.0 14.4 collective-permute-done
  1244.9 14.4 collective-permute-done
  1270.8 14.4 collective-permute-done
  1296.9 14.4 collective-permute-done
  1322.8 14.4 collective-permute-done
  1348.7 14.4 collective-permute-done
  1374.8 14.4 collective-permute-done
  1400.8 14.4 collective-permute-done
  1738.5 14.4 collective-permute-done
  1920.3 14.4 collective-permute-done
  1972.3 14.4 collective-permute-done
  2024.3 14.5 collective-permute-done
  (3158 shorter events, 1190.0 us)
Async XLA Ops:
  7.2 109.2 %all-gather.2.cloned.1.call-start = ((), (), s32[]{:S(2)}) async-start(), calls=%async_computation.6 | async-start | bytes 4259840 | tf_op jit(solution)/shard_map/all_gather | solution.py:72
  24.3 23.2 %all-to-all-start = ((bf16[64,4,512]{2,0,1:T(8,128)(2,1)}), bf16[64,4,512]{2,0,1:T(8,128)(2,1)S(1)}, u32[]{:S(2)}, u32[]{:S(2)}) async-start(bf16[64,4,512]{2,0,1:T(8,128)(2,1)} %bitcast.114), calls=%async_computation | async-start | bytes 524288 | tf_op jit(solution)/shard_map/all_to_all | solution.py:44
  378.8 17.6 collective-permute-start.3
  379.1 17.2 collective-permute-start.2
  379.3 16.3 collective-permute-start
  379.6 16.8 collective-permute-start.1
  406.8 19.6 collective-permute-start.3
  406.9 19.5 collective-permute-start.2
  407.0 18.7 collective-permute-start
  407.1 19.3 collective-permute-start.1
  436.8 17.6 collective-permute-start.3
  436.9 17.5 collective-permute-start.2
  437.0 16.6 collective-permute-start
  437.1 17.3 collective-permute-start.1
  464.9 15.6 collective-permute-start.3
  490.9 15.5 collective-permute-start.3
  517.0 15.5 collective-permute-start.3
  543.0 15.5 collective-permute-start.3
  569.1 15.5 collective-permute-start.3
  595.2 15.5 collective-permute-start.3
  621.2 15.5 collective-permute-start.3
  725.2 15.5 collective-permute-start.3
  777.0 15.5 collective-permute-start.3
  855.0 15.5 collective-permute-start.3
  880.9 15.5 collective-permute-start.3
  932.9 15.5 collective-permute-start.3
  958.8 15.5 collective-permute-start.3
  984.9 15.5 collective-permute-start.3
  1010.8 15.5 collective-permute-start.3
  1036.8 15.5 collective-permute-start.3
  1140.8 15.5 collective-permute-start.3
  1192.6 15.5 collective-permute-start.3
  1218.6 15.5 collective-permute-start.3
  1270.4 15.5 collective-permute-start.3
  1348.3 15.5 collective-permute-start.3
  1426.4 15.5 collective-permute-start.3
  1556.4 15.5 collective-permute-start.3
  1582.3 15.5 collective-permute-start.3
  1634.3 15.5 collective-permute-start.3
  1660.2 15.5 collective-permute-start.3
  1712.2 15.5 collective-permute-start.3
  1738.2 15.5 collective-permute-start.3
  1842.0 15.5 collective-permute-start.3
  1868.1 15.5 collective-permute-start.3
  1919.9 15.5 collective-permute-start.3
  1971.9 15.5 collective-permute-start.3
  2023.9 15.7 collective-permute-start.3
  2024.0 15.5 collective-permute-start.2
  (217 other events, 3572.9 us)
Sparse Core Ops, SparseCore 0:
  22.8 93.5 all-gather.1
where the time goes:
time: 2090 us; the launch traced here: 2080 us
  waiting for transfers between devices  1040 us (50%)
  loops' own time  504 us (24%)
  matrix products  212 us (10%)
  local copies, waits for them, and re-layouts  130 us (6%)
  other arithmetic  91 us (4%)
  starting transfers between devices  52.6 us (3%)
  blocking collectives  28.5 us (1%)
    ppermute x256, waiting for transfers between devices, passed_along(): return lax.ppermute(value, axis, pairs)  975 us
    another operation x1, loops' own time, body(): final_state = lax.fori_loop(0, n_blk, advance, start_state)  331 us
    dot_general x322, matrix products, dot_rows(): lax.dot_general(left, right, (((1,), (1,)), ((), ())), preferred_element_...  128 us
    another operation x256, loops' own time, visit_keys(): lax.cond(own_blocks[query_slot] >= block_id, partial(tile_grads, query_sl...  84.9 us
    another operation x1, loops' own time, body(): lax.fori_loop(0, piece_rows // step_rows, one_block, loop_state)  84.5 us
    dot_general x258, matrix products, dot_columns(): lax.dot_general(left, right, (((0,), (0,)), ((), ())), preferred_element_...  61 us
    reduce_min x64, other arithmetic, one_block(): jnp.min(key_pos) <= latest  45.9 us
    all_gather x1, waiting for transfers between devices, body(): piece = lax.all_gather(key_rows, 'blk', axis=0, tiled=True)  43.9 us
  transfers between devices with their start and end apart: 263, of which 134 were waited for; matrix products, arithmetic and copies ran while one was open for 1% of the time, Pallas kernels for 0%

commit v1 on v0

v1 whole, which is shorter than its diff:
```python
from functools import partial
import math

import jax
import jax.numpy as jnp
from jax import lax
from jax.experimental import pallas as pl
from jax.experimental.pallas import tpu as pltpu
from jax.sharding import Mesh, PartitionSpec as P

HEAD_DIM = 128
BLOCK = 128
HEADS_HERE = 4
ROWS = BLOCK * HEADS_HERE
CHUNK_BLOCKS = 4
CHUNK = CHUNK_BLOCKS * BLOCK
SLOTS = 64
CHUNKS = SLOTS // CHUNK_BLOCKS
PIECE = 2048
FACTOR = HEAD_DIM ** (-0.5)
LOG2E = math.log2(math.e)
SCALE2 = FACTOR * LOG2E
NEG = -1e30
VMEM_BYTES = 48 * 1024 * 1024
PIECE_ROWS = (PIECE, PIECE, PIECE, PIECE // 2, PIECE // 2)
PIECE_START = (0, PIECE, 2 * PIECE, 3 * PIECE, 3 * PIECE + PIECE // 2)


def ring_pairs(steps):
    return [(source, (source + steps) % 4) for source in range(4)]


def send(value, axis, steps):
    return lax.ppermute(value, axis, ring_pairs(steps))


def swap_core(value):
    return lax.ppermute(value, "core", [(0, 1), (1, 0)])


def gather_ring(own, axis):
    half = own.shape[0] // 2
    left = send(own, axis, 1)
    right = send(own, axis, -1)
    far_first = send(left[:half], axis, 1)
    far_second = send(right[half:], axis, -1)
    return [own, left, right, far_first, far_second]


def add(first, second):
    return (first.astype(jnp.float32) + second.astype(jnp.float32)).astype(jnp.bfloat16)


def reduce_ring(pieces, axis):
    own, left, right, far_first, far_second = pieces
    half = own.shape[0] // 2
    from_right = send(far_first, axis, -1)
    from_left = send(far_second, axis, 1)
    left = jnp.concatenate([add(left[:half], from_right), left[half:]], axis=0)
    right = jnp.concatenate([right[:half], add(right[half:], from_left)], axis=0)
    first = send(left, axis, -1)
    second = send(right, axis, 1)
    return (
        own.astype(jnp.float32) + first.astype(jnp.float32) + second.astype(jnp.float32)
    ).astype(jnp.bfloat16)


def split_pieces(rows):
    step = rows.shape[0] // 4
    half = step // 2
    return [
        rows[:step],
        rows[step : 2 * step],
        rows[2 * step : 3 * step],
        rows[3 * step : 3 * step + half],
        rows[3 * step + half :],
    ]


def copy_pieces(sources, target, sems):
    copies = []
    for index, source in enumerate(sources):
        copy = pltpu.make_async_copy(
            source, target.at[pl.ds(PIECE_START[index], PIECE_ROWS[index])], sems.at[index]
        )
        copy.start()
        copies.append(copy)
    return copies


def spread_heads(source, base, target):
    for pair in range(2):
        for head in range(HEADS_HERE):
            target[base + pair, pl.ds(head * BLOCK, BLOCK), :] = source[
                pl.ds(pair * BLOCK, BLOCK), pl.ds(head * HEAD_DIM, HEAD_DIM)
            ]


def load_chunk(source, slot_ref, chunk):
    return jnp.concatenate(
        [
            source[pl.ds(pl.multiple_of(slot_ref[chunk * CHUNK_BLOCKS + j] * BLOCK, BLOCK), BLOCK), :]
            for j in range(CHUNK_BLOCKS)
        ],
        axis=0,
    )


def dot_rows(left, right):
    return lax.dot_general(
        left, right, (((1,), (1,)), ((), ())), preferred_element_type=jnp.float32
    )


def dot_columns(left, right):
    return lax.dot_general(
        left, right, (((0,), (0,)), ((), ())), preferred_element_type=jnp.float32
    )


def masked(value, fill, ids_ref, chunk, query_id):
    rows = lax.broadcasted_iota(jnp.int32, (BLOCK, ROWS), 0)
    lanes = lax.broadcasted_iota(jnp.int32, (BLOCK, ROWS), 1) % BLOCK
    ahead = rows - lanes
    parts = []
    for j in range(CHUNK_BLOCKS):
        limit = (query_id - ids_ref[chunk * CHUNK_BLOCKS + j]) * BLOCK
        parts.append(jnp.where(ahead <= limit, value[j * BLOCK : (j + 1) * BLOCK], fill))
    return jnp.concatenate(parts, axis=0)


def for_tiles(chunk, query, count_ref, tile):
    count = count_ref[query]
    full = count // CHUNK_BLOCKS

    @pl.when(chunk < full)
    def _():
        tile(chunk, query, False)

    @pl.when((chunk >= full) & (chunk * CHUNK_BLOCKS < count_ref[query + 4]))
    def _():
        tile(chunk, query, True)


def lse_kernel(
    slot_ref, ids_ref, count_ref, qid_ref, q_own, q_other, k0, k1, k2, k3, k4,
    max_ref, sum_ref, keys, queries, max_acc, sum_acc, sems,
):
    copies = copy_pieces((k0, k1, k2, k3, k4), keys, sems)
    spread_heads(q_own, 0, queries)
    spread_heads(q_other, 2, queries)
    max_acc[...] = jnp.full(max_acc.shape, NEG, jnp.float32)
    sum_acc[...] = jnp.zeros(sum_acc.shape, jnp.float32)
    for copy in copies:
        copy.wait()

    def tile(chunk, query, use_mask):
        scores = dot_rows(load_chunk(keys, slot_ref, chunk), queries[query])
        if use_mask:
            scores = masked(scores, NEG, ids_ref, chunk, qid_ref[query])
        grouped = scores.reshape(CHUNK // 8, 8, ROWS)
        old_max = max_acc[query]
        new_max = jnp.maximum(old_max, jnp.max(grouped, axis=0))
        weights = jnp.exp2((grouped - new_max[None]) * SCALE2)
        sum_acc[query] = sum_acc[query] * jnp.exp2((old_max - new_max) * SCALE2) + jnp.sum(
            weights, axis=0
        )
        max_acc[query] = new_max

    def step(index, carry):
        for_tiles(index // 4, index % 4, count_ref, tile)
        return carry

    lax.fori_loop(0, CHUNKS * 4, step, 0)
    for query in range(4):
        part_max = max_acc[query]
        top = jnp.max(part_max, axis=0, keepdims=True)
        max_ref[query] = top
        sum_ref[query] = jnp.sum(
            sum_acc[query] * jnp.exp2((part_max - top) * SCALE2), axis=0, keepdims=True
        )


def grad_kernel(
    slot_k_ref, slot_v_ref, ids_ref, count_ref, qid_ref,
    q_own, q_other, g_own, g_other, max_mine, sum_mine, max_theirs, sum_theirs,
    delta_own, delta_other,
    k0, k1, k2, k3, k4, v0, v1, v2, v3, v4,
    dq_own, dq_other, dk0, dk1, dk2, dk3, dk4, dv0, dv1, dv2, dv3, dv4,
    keys, values, queries, grads, lse, delta, dk_all, dv_all, dk_acc, dv_acc, dq_acc,
    sems_k, sems_v,
):
    copies = copy_pieces((k0, k1, k2, k3, k4), keys, sems_k)
    copies += copy_pieces((v0, v1, v2, v3, v4), values, sems_v)
    spread_heads(q_own, 0, queries)
    spread_heads(q_other, 2, queries)
    spread_heads(g_own, 0, grads)
    spread_heads(g_other, 2, grads)
    for query in range(4):
        top_mine = max_mine[query]
        top_theirs = max_theirs[(query + 2) % 4]
        top = jnp.maximum(top_mine, top_theirs)
        total = sum_mine[query] * jnp.exp2((top_mine - top) * SCALE2) + sum_theirs[
            (query + 2) % 4
        ] * jnp.exp2((top_theirs - top) * SCALE2)
        lse[query] = top * SCALE2 + jnp.log2(total)
        delta[query] = (delta_own if query < 2 else delta_other)[query % 2]
    dq_acc[...] = jnp.zeros(dq_acc.shape, jnp.float32)
    for copy in copies:
        copy.wait()

    def tile(chunk, query, use_mask):
        key_part = load_chunk(keys, slot_k_ref, chunk)
        value_part = load_chunk(values, slot_v_ref, chunk)
        query_part = queries[query]
        grad_part = grads[query]
        scores = dot_rows(key_part, query_part)
        weights = jnp.exp2(scores * SCALE2 - lse[query])
        if use_mask:
            weights = masked(weights, 0.0, ids_ref, chunk, qid_ref[query])
        dv_acc[...] += jnp.dot(
            weights.astype(jnp.bfloat16), grad_part, preferred_element_type=jnp.float32
        )
        dprob = dot_rows(value_part, grad_part)
        score_grad = (weights * (dprob - delta[query])).astype(jnp.bfloat16)
        dk_acc[...] += jnp.dot(score_grad, query_part, preferred_element_type=jnp.float32)
        dq_acc[query] += dot_columns(key_part, score_grad)

    def chunk_step(chunk, carry):
        dk_acc[...] = jnp.zeros(dk_acc.shape, jnp.float32)
        dv_acc[...] = jnp.zeros(dv_acc.shape, jnp.float32)

        def query_step(query, inner):
            for_tiles(chunk, query, count_ref, tile)
            return inner

        lax.fori_loop(0, 4, query_step, 0)
        for j in range(CHUNK_BLOCKS):
            place = chunk * CHUNK_BLOCKS + j
            rows = pl.ds(j * BLOCK, BLOCK)
            start_k = pl.multiple_of(slot_k_ref[place] * BLOCK, BLOCK)
            start_v = pl.multiple_of(slot_v_ref[place] * BLOCK, BLOCK)
            dk_all[pl.ds(start_k, BLOCK), :] = (dk_acc[rows, :] * FACTOR).astype(jnp.bfloat16)
            dv_all[pl.ds(start_v, BLOCK), :] = dv_acc[rows, :].astype(jnp.bfloat16)
        return carry

    lax.fori_loop(0, CHUNKS, chunk_step, 0)
    outs = []
    for source, targets, sems in (
        (dk_all, (dk0, dk1, dk2, dk3, dk4), sems_k),
        (dv_all, (dv0, dv1, dv2, dv3, dv4), sems_v),
    ):
        for index, target in enumerate(targets):
            copy = pltpu.make_async_copy(
                source.at[pl.ds(PIECE_START[index], PIECE_ROWS[index])], target, sems.at[index]
            )
            copy.start()
            outs.append(copy)
    for query in range(4):
        target = dq_own if query < 2 else dq_other
        for head in range(HEADS_HERE):
            part = dq_acc[query, :, pl.ds(head * BLOCK, BLOCK)] * FACTOR
            target[pl.ds((query % 2) * BLOCK, BLOCK), pl.ds(head * HEAD_DIM, HEAD_DIM)] = (
                part.T.astype(target.dtype)
            )
    for copy in outs:
        copy.wait()


SMEM = pl.BlockSpec(memory_space=pltpu.SMEM)
VMEM = pl.BlockSpec(memory_space=pltpu.VMEM)
ANY = pl.BlockSpec(memory_space=pl.ANY)
PAIRS = SLOTS * 2 + 1


def call_lse(slots, ids, counts, qids, q_own, q_other, key_pieces):
    stat = jax.ShapeDtypeStruct((4, 1, ROWS), jnp.float32)
    work = PAIRS * BLOCK * ROWS
    return pl.pallas_call(
        lse_kernel,
        out_shape=(stat, stat),
        in_specs=[SMEM] * 4 + [VMEM] * 2 + [ANY] * 5,
        out_specs=(VMEM, VMEM),
        scratch_shapes=[
            pltpu.VMEM((SLOTS * BLOCK, HEAD_DIM), jnp.bfloat16),
            pltpu.VMEM((4, ROWS, HEAD_DIM), jnp.bfloat16),
            pltpu.VMEM((4, 8, ROWS), jnp.float32),
            pltpu.VMEM((4, 8, ROWS), jnp.float32),
            pltpu.SemaphoreType.DMA((5,)),
        ],
        compiler_params=pltpu.CompilerParams(vmem_limit_bytes=VMEM_BYTES),
        cost_estimate=pl.CostEstimate(
            flops=8 * work * HEAD_DIM, bytes_accessed=3 << 20, transcendentals=work
        ),
        name="lse",
    )(slots, ids, counts, qids, q_own, q_other, *key_pieces)


def call_grads(tables, rows, key_pieces, value_pieces):
    pieces = tuple(jax.ShapeDtypeStruct((n, HEAD_DIM), jnp.bfloat16) for n in PIECE_ROWS)
    work = PAIRS * BLOCK * ROWS
    flat = jax.ShapeDtypeStruct((2 * BLOCK, ROWS), jnp.float32)
    return pl.pallas_call(
        grad_kernel,
        out_shape=(flat, jax.ShapeDtypeStruct(flat.shape, jnp.bfloat16)) + pieces + pieces,
        in_specs=[SMEM] * 5 + [VMEM] * 10 + [ANY] * 10,
        out_specs=(VMEM, VMEM) + (ANY,) * 10,
        scratch_shapes=[
            pltpu.VMEM((SLOTS * BLOCK, HEAD_DIM), jnp.bfloat16),
            pltpu.VMEM((SLOTS * BLOCK, HEAD_DIM), jnp.bfloat16),
            pltpu.VMEM((4, ROWS, HEAD_DIM), jnp.bfloat16),
            pltpu.VMEM((4, ROWS, HEAD_DIM), jnp.bfloat16),
            pltpu.VMEM((4, 1, ROWS), jnp.float32),
            pltpu.VMEM((4, 1, ROWS), jnp.float32),
            pltpu.VMEM((SLOTS * BLOCK, HEAD_DIM), jnp.bfloat16),
            pltpu.VMEM((SLOTS * BLOCK, HEAD_DIM), jnp.bfloat16),
            pltpu.VMEM((CHUNK, HEAD_DIM), jnp.float32),
            pltpu.VMEM((CHUNK, HEAD_DIM), jnp.float32),
            pltpu.VMEM((4, HEAD_DIM, ROWS), jnp.float32),
            pltpu.SemaphoreType.DMA((5,)),
            pltpu.SemaphoreType.DMA((5,)),
        ],
        compiler_params=pltpu.CompilerParams(vmem_limit_bytes=VMEM_BYTES),
        cost_estimate=pl.CostEstimate(
            flops=16 * work * HEAD_DIM, bytes_accessed=10 << 20, transcendentals=work
        ),
        name="grads",
    )(*tables, *rows, *key_pieces, *value_pieces)


def lookup(table, wanted):
    places = jnp.arange(table.shape[0], dtype=jnp.int32)
    return jnp.sum(jnp.where(wanted[:, None] == places[None, :], table[None, :], 0), axis=1)


def plan(order):
    x, y, zh, core = (lax.axis_index(name) for name in ("x", "y", "zh", "core"))
    offsets = (0, -1, 1, 2)
    offset_table = jnp.array(offsets, jnp.int32)
    slot = jnp.arange(SLOTS, dtype=jnp.int32)
    outer, inner, pair = slot // 16, slot // 4 % 4, slot % 4

    def block_of(dx, dy):
        blk = ((x + dx) % 4) * 16 + (pair // 2) * 8 + ((y + dy) % 4) * 2 + core
        return lookup(order, 2 * blk + pair % 2)

    outer, inner = lookup(offset_table, outer), lookup(offset_table, inner)
    ids_k, ids_v = block_of(outer, inner), block_of(inner, outer)
    own = ((x * 2 + zh) * 4 + y) * 2 + core
    other = own + 1 - 2 * core
    ends = jnp.arange(2, dtype=jnp.int32)
    query_ids = lookup(order, jnp.concatenate([2 * own + ends, 2 * other + ends]))

    def in_sequence(ids):
        rank = jnp.sum((ids[None, :] < ids[:, None]).astype(jnp.int32), axis=1)
        hit = rank[None, :] == slot[:, None]
        return (
            jnp.sum(jnp.where(hit, slot[None, :], 0), axis=1),
            jnp.sum(jnp.where(hit, ids[None, :], 0), axis=1),
        )

    slots_k, ids = in_sequence(ids_k)
    slots_v, _ = in_sequence(ids_v)
    before = jnp.sum((ids[None, :] < query_ids[:, None]).astype(jnp.int32), axis=1)
    upto = jnp.sum((ids[None, :] <= query_ids[:, None]).astype(jnp.int32), axis=1)
    return slots_k, slots_v, ids, jnp.concatenate([before, upto]), query_ids


def to_heads(rows):
    parts = rows.reshape(rows.shape[0], 4, -1).transpose(1, 0, 2)
    parts = lax.all_to_all(parts, "head", split_axis=0, concat_axis=0, tiled=True)
    return parts.reshape(4 * rows.shape[0], -1)


def body(queries, keys, values, outputs, out_grad, order):
    tokens = queries.shape[0]
    slots_k, slots_v, ids, counts, query_ids = plan(order)

    both = jnp.stack(
        [keys.reshape(tokens, 2, HEAD_DIM), values.reshape(tokens, 2, HEAD_DIM)], axis=0
    ).transpose(2, 0, 1, 3)
    outgoing = jnp.broadcast_to(
        both[None, :, None], (2, 2, 2) + both.shape[1:]
    ).reshape(8, 2, tokens, HEAD_DIM)
    arrived = lax.all_to_all(outgoing, ("zh", "head"), split_axis=0, concat_axis=0, tiled=True)
    key_pieces = gather_ring(
        jnp.concatenate(gather_ring(arrived[:, 0].reshape(8 * tokens, HEAD_DIM), "y")), "x"
    )
    value_pieces = gather_ring(
        jnp.concatenate(gather_ring(arrived[:, 1].reshape(8 * tokens, HEAD_DIM), "x")), "y"
    )

    q_own = to_heads(queries)
    g_own = to_heads(out_grad)
    row_delta = jnp.sum(
        (out_grad.astype(jnp.float32) * outputs.astype(jnp.float32)).reshape(tokens, 16, HEAD_DIM),
        axis=2,
    )
    delta = lax.all_to_all(
        row_delta.T.reshape(4, 4, tokens), "head", split_axis=0, concat_axis=0, tiled=True
    )
    delta_own = delta.reshape(2, 2, 4, tokens).transpose(0, 2, 1, 3).reshape(2, 1, ROWS)
    q_other, g_other, delta_other = swap_core(q_own), swap_core(g_own), swap_core(delta_own)

    max_mine, sum_mine = call_lse(slots_k, ids, counts, query_ids, q_own, q_other, key_pieces)
    max_theirs, sum_theirs = swap_core(max_mine), swap_core(sum_mine)
    results = call_grads(
        (slots_k, slots_v, ids, counts, query_ids),
        (
            q_own, q_other, g_own, g_other, max_mine, sum_mine, max_theirs, sum_theirs,
            delta_own, delta_other,
        ),
        key_pieces,
        value_pieces,
    )
    dq_own, dq_other = results[0], results[1]
    dq = (dq_own + swap_core(dq_other).astype(jnp.float32)).astype(jnp.bfloat16)
    dq = lax.all_to_all(
        dq.reshape(4, tokens, ROWS), "head", split_axis=0, concat_axis=0, tiled=True
    )
    query_grad = dq.transpose(1, 0, 2).reshape(tokens, 4 * ROWS)

    dk = reduce_ring(split_pieces(reduce_ring(results[2:7], "x")), "y")
    dv = reduce_ring(split_pieces(reduce_ring(results[7:12], "y")), "x")
    back = jnp.stack(
        [dk.reshape(8, tokens, HEAD_DIM), dv.reshape(8, tokens, HEAD_DIM)], axis=1
    )
    back = lax.all_to_all(back, ("zh", "head"), split_axis=0, concat_axis=0, tiled=True)
    summed = jnp.sum(
        back.reshape(2, 2, 2, 2, tokens, HEAD_DIM).astype(jnp.float32), axis=(0, 2)
    )
    folded = summed.transpose(1, 2, 0, 3).reshape(2, tokens, 2 * HEAD_DIM).astype(jnp.bfloat16)
    return query_grad, folded[0], folded[1]


def solution(mesh):
    fine = Mesh(
        mesh.devices.reshape(4, 4, 2, 4, 2), ("head", "x", "zh", "y", "core")
    )
    rows = P(("x", "zh", "y", "core", "head"), None)
    return jax.shard_map(
        body,
        mesh=fine,
        in_specs=(rows, rows, rows, rows, rows, P()),
        out_specs=(rows, rows, rows),
        check_vma=False,
    )
```

time: 2090 us -> 197 us (0.09)
  waiting for transfers between devices: 1040 us -> 30.4 us
  loops' own time: 504 us -> 0 us
  matrix products: 212 us -> 0 us
  local copies, waits for them, and re-layouts: 130 us -> 20.2 us
  other arithmetic: 91 us -> 8.93 us
  Pallas kernels: 0 us -> 52 us
  blocking collectives: 28.5 us -> 0 us
  starting transfers between devices: 52.6 us -> 80.6 us
    ppermute x256 -> x38, waiting for transfers between devices: 975 us -> 14.9 us  [the longest x32 14.2 us: send(): return lax.ppermute(value, axis, ring_pairs(steps))]
    another operation x322 -> x0, loops' own time: 504 us -> none  [the longest x1 331 us: body(): final_state = lax.fori_loop(0, n_blk, advance, start_state)]
    dot_general x709 -> x0, matrix products: 212 us -> none  [the longest x322 128 us: dot_rows(): lax.dot_general(left, right, (((1,), (1,)), ((), ())), preferred_element_...]
    slice x265 -> x18, local copies, waits for them, and re-layouts: 96.1 us -> 5.02 us  [the longest x4 1.7 us: gather_ring(): far_second = send(right[half:], axis, -1)]
    pallas_call x0 -> x2, Pallas kernels: none -> 52 us  [the longest x1 33.2 us: call_grads(): pl.pallas_call(grad_kernel, out_shape=(flat, jax.ShapeDtypeStruct(flat.sh...]
    reduce_min x64 -> x0, other arithmetic: 45.9 us -> none  [one_block(): jnp.min(key_pos) <= latest]
    all_gather x1 -> x0, waiting for transfers between devices: 43.9 us -> none  [body(): piece = lax.all_gather(key_rows, 'blk', axis=0, tiled=True)]
    all_gather x2 -> x0, blocking collectives: 28.5 us -> none  [the longest x1 14.8 us: body(): lax.all_gather(keys, 'head', axis=0, tiled=True)]
  transfers between devices with their start and end apart: 263 -> 44, of which waited for: 134 -> 14; matrix products, arithmetic and copies ran while one was open for 1% -> 11% of each run, Pallas kernels for 0% -> 10%
where the time goes in v1:
time: 197 us; the launch traced here: 193 us
  starting transfers between devices  80.6 us (41%)
  Pallas kernels  52 us (26%)
  waiting for transfers between devices  30.4 us (15%)
  local copies, waits for them, and re-layouts  20.2 us (10%)
  other arithmetic  8.93 us (5%)
    ppermute x32, starting transfers between devices, send(): return lax.ppermute(value, axis, ring_pairs(steps))  46.3 us
    pallas_call x1, Pallas kernels, call_grads(): pl.pallas_call(grad_kernel, out_shape=(flat, jax.ShapeDtypeStruct(flat.sh...  33.2 us
    pallas_call x1, Pallas kernels, call_lse(): pl.pallas_call(lse_kernel, out_shape=(stat, stat), in_specs=[SMEM] * 4 +...  18.8 us
    ppermute x32, waiting for transfers between devices, send(): return lax.ppermute(value, axis, ring_pairs(steps))  14.2 us
    unnamed x54, local copies, waits for them, and re-layouts  10.1 us
    all_to_all x2, starting transfers between devices, to_heads(): lax.all_to_all(parts, 'head', split_axis=0, concat_axis=0, tiled=True)  9.09 us
    all_to_all x1, starting transfers between devices, body(): lax.all_to_all(outgoing, ('zh', 'head'), split_axis=0, concat_axis=0, til...  8.7 us
    all_to_all x1, waiting for transfers between devices, body(): lax.all_to_all(back, ('zh', 'head'), split_axis=0, concat_axis=0, tiled=T...  8.3 us
  transfers between devices with their start and end apart: 44, of which 14 were waited for; matrix products, arithmetic and copies ran while one was open for 11% of the time, Pallas kernels for 10%

profile of v1, /device:TPU:32, one launch (start us, length us, event | category | flops | bytes accessed | tf_op | source)
XLA Modules:
  0.0 193.4 jit_solution(10199719274407420372)
XLA Ops:
  2.3 8.7 %all-to-all-start.2 = ((bf16[8,2,64,128]{3,2,1,0:T(8,128)(2,1)}), bf16[8,2,64,128]{3,2,1,0:T(8,128)(2,1)S(1)}, u32[]{:S(2)}, u32[]{:S(2)}) async-start(bf16[8,2,64,128]{3,2,1,0:T(8,128)(2,1)} %bitcast.5), calls=%async_computation.2 | async-start | bytes 524288 | tf_op jit(solution)/shard_map/all_to_all | solution.py:385
  12.0 0.9 copy-done.14
  16.3 5.2 %all-to-all-done.2 = bf16[8,2,64,128]{3,2,1,0:T(8,128)(2,1)S(1)} async-done(((bf16[8,2,64,128]{3,2,1,0:T(8,128)(2,1)}), bf16[8,2,64,128]{3,2,1,0:T(8,128)(2,1)S(1)}, u32[]{:S(2)}, u32[]{:S(2)}) %all-to-all-start.2) | async-done | bytes 262176 | tf_op jit(solution)/shard_map/all_to_all | solution.py:385
  21.4 4.7 %all-to-all-start.3 = ((f32[4,1,256]{2,1,0:T(1,128)}), f32[4,1,256]{2,1,0:T(1,128)S(1)}, u32[]{:S(2)}, u32[]{:S(2)}) async-start(f32[4,1,256]{2,1,0:T(1,128)} %reshape.214), calls=%async_computation.3 | async-start | bytes 8192 | tf_op jit(solution)/shard_map/all_to_all | solution.py:399
  26.1 3.1 %collective-permute-start.3 = (bf16[512,128]{1,0:T(8,128)(2,1)S(1)}, bf16[512,128]{1,0:T(8,128)(2,1)S(1)}, u32[]{:S(2)}, u32[]{:S(2)}) collective-permute-start(bf16[512,128]{1,0:T(8,128)(2,1)S(1)} %bitcast.65), channel_id=1, source_target_pairs={{0,6},{2,0},{4,2},{6,4},{1,7},{3,1},{5,3},{7,5},{8,14},{10,8},{12,... | collective-permute-start | bytes 393224 | tf_op jit(solution)/shard_map/ppermute | solution.py:34
  29.2 2.8 %collective-permute-start.14 = (bf16[512,128]{1,0:T(8,128)(2,1)S(1)}, bf16[512,128]{1,0:T(8,128)(2,1)S(1)}, u32[]{:S(2)}, u32[]{:S(2)}) collective-permute-start(bf16[512,128]{1,0:T(8,128)(2,1)S(1)} %bitcast.62), channel_id=1, source_target_pairs={{0,48},{16,0},{32,16},{48,32},{1,49},{17,1},{33,17},{49,33},{2,50}... | collective-permute-start | bytes 393224 | tf_op jit(solution)/shard_map/ppermute | solution.py:34
  32.7 3.3 %collective-permute-start.5 = (bf16[256,128]{1,0:T(8,128)(2,1)S(1)}, bf16[256,128]{1,0:T(8,128)(2,1)S(1)}, u32[]{:S(2)}, u32[]{:S(2)}) collective-permute-start(bf16[256,128]{1,0:T(8,128)(2,1)S(1)} %slice.152), channel_id=1, source_target_pairs={{0,6},{2,0},{4,2},{6,4},{1,7},{3,1},{5,3},{7,5},{8,14},{10,8},{12,... | collective-permute-start | bytes 196616 | tf_op jit(solution)/shard_map/ppermute | solution.py:34
  36.1 3.3 %collective-permute-start.16 = (bf16[256,128]{1,0:T(8,128)(2,1)S(1)}, bf16[256,128]{1,0:T(8,128)(2,1)S(1)}, u32[]{:S(2)}, u32[]{:S(2)}) collective-permute-start(bf16[256,128]{1,0:T(8,128)(2,1)S(1)} %slice.157), channel_id=1, source_target_pairs={{0,48},{16,0},{32,16},{48,32},{1,49},{17,1},{33,17},{49,33},{2,50}... | collective-permute-start | bytes 196616 | tf_op jit(solution)/shard_map/ppermute | solution.py:34
  40.3 1.3 collective-permute-done.4
  41.6 3.3 %collective-permute-start.7 = (bf16[2048,128]{1,0:T(8,128)(2,1)S(1)}, bf16[2048,128]{1,0:T(8,128)(2,1)S(1)}, u32[]{:S(2)}, u32[]{:S(2)}) collective-permute-start(bf16[2048,128]{1,0:T(8,128)(2,1)S(1)} %constant_dynamic-update-slice_fusion.k0), channel_id=1, source_target_pairs={{0,48},{16,0},{32,16},{48,32},{1,49},{17,1},{33,17},{49,33},{2,50}... | collective-permute-start | bytes 1572872 | tf_op jit(solution)/shard_map/ppermute | solution.py:34
  44.9 5.1 %all-to-all-start = ((bf16[4,64,512]{2,1,0:T(8,128)(2,1)}), bf16[4,64,512]{2,1,0:T(8,128)(2,1)S(1)}, u32[]{:S(2)}, u32[]{:S(2)}) async-start(bf16[4,64,512]{2,1,0:T(8,128)(2,1)} %bitcast.49), calls=%async_computation | async-start | bytes 524288 | tf_op jit(solution)/shard_map/all_to_all | solution.py:371
  52.0 1.9 collective-permute-start.18
  54.2 2.1 %all-to-all-done = bf16[4,64,512]{2,1,0:T(8,128)(2,1)S(1)} async-done(((bf16[4,64,512]{2,1,0:T(8,128)(2,1)}), bf16[4,64,512]{2,1,0:T(8,128)(2,1)S(1)}, u32[]{:S(2)}, u32[]{:S(2)}) %all-to-all-start) | async-done | bytes 262176 | tf_op jit(solution)/shard_map/all_to_all | solution.py:371
  56.2 4.0 %all-to-all-start.1 = ((bf16[4,64,512]{2,1,0:T(8,128)(2,1)}), bf16[4,64,512]{2,1,0:T(8,128)(2,1)S(1)}, u32[]{:S(2)}, u32[]{:S(2)}) async-start(bf16[4,64,512]{2,1,0:T(8,128)(2,1)} %bitcast.47), calls=%async_computation.1 | async-start | bytes 524288 | tf_op jit(solution)/shard_map/all_to_all | solution.py:371
  60.5 3.5 %collective-permute-start.9 = (bf16[1024,128]{1,0:T(8,128)(2,1)S(1)}, bf16[1024,128]{1,0:T(8,128)(2,1)S(1)}, u32[]{:S(2)}, u32[]{:S(2)}) collective-permute-start(bf16[1024,128]{1,0:T(8,128)(2,1)S(1)} %slice.154), channel_id=1, source_target_pairs={{0,48},{16,0},{32,16},{48,32},{1,49},{17,1},{33,17},{49,33},{2,50}... | collective-permute-start | bytes 786440 | tf_op jit(solution)/shard_map/ppermute | solution.py:34
  66.2 1.7 slice.159
  68.2 1.0 slice.158
  69.2 2.2 %collective-permute-start.20 = (bf16[1024,128]{1,0:T(8,128)(2,1)S(1)}, bf16[1024,128]{1,0:T(8,128)(2,1)S(1)}, u32[]{:S(2)}, u32[]{:S(2)}) collective-permute-start(bf16[1024,128]{1,0:T(8,128)(2,1)S(1)} %copy-done.15), channel_id=1, source_target_pairs={{0,6},{2,0},{4,2},{6,4},{1,7},{3,1},{5,3},{7,5},{8,14},{10,8},{12,... | collective-permute-start | bytes 786440 | tf_op jit(solution)/shard_map/ppermute | solution.py:34
  71.5 2.3 %collective-permute-done.8.k3 = bf16[1024,128]{1,0:T(8,128)(2,1)S(1)} collective-permute-done((bf16[1024,128]{1,0:T(8,128)(2,1)S(1)}, bf16[1024,128]{1,0:T(8,128)(2,1)S(1)}, u32[]{:S(2)}, u32[]{:S(2)}) %collective-permute-start.8) | collective-permute-done | bytes 262176 | tf_op jit(solution)/shard_map/ppermute | solution.py:34
  73.8 18.8 %lse.1 = (f32[4,1,512]{2,1,0:T(1,128)S(1)}, f32[4,1,512]{2,1,0:T(1,128)S(1)}) custom-call(s32[64]{0:T(128)S(1)} %get-tuple-element.34.slot_ref.slot_k_ref, s32[64]{0:T(128)S(1)} %get-tuple-element.33.ids_ref, s32[8]{0:T(128)S(1)} %pad_add_fusion.1.count_ref, s32[4]{0:T(128)S(1)} %select_reduce_fusion.5.qid_ref, bf16[256,512]{1,0:T(8,128)(2,1)S(1)} %bitcast.54, ...), custom_call_target="tpu_custom_call" | custom-call | flops 8657043456 | bytes 3145728 | tf_op jit(solution)/shard_map/lse/pallas_call | solution.py:279
  94.0 0.9 copy-done.4
  94.9 0.9 copy-done.6
  95.9 33.2 %grads.1 = (f32[256,512]{1,0:T(8,128)S(1)}, bf16[256,512]{1,0:T(8,128)(2,1)S(1)}, bf16[2048,128]{1,0:T(8,128)(2,1)S(1)}, bf16[2048,128]{1,0:T(8,128)(2,1)S(1)}, ...) custom-call(s32[64]{0:T(128)S(1)} %get-tuple-element.34.slot_ref.slo, ...), custom_call_target="tpu_custom_call" | custom-call | flops 17314086912 | bytes 10485760 | tf_op jit(solution)/shard_map/grads/pallas_call | solution.py:303
  132.1 1.0 collective-permute-start.22
  133.1 1.0 collective-permute-start.24
  134.1 3.2 %collective-permute-start.30 = (bf16[1024,128]{1,0:T(8,128)(2,1)}, bf16[1024,128]{1,0:T(8,128)(2,1)}, u32[]{:S(2)}, u32[]{:S(2)}) collective-permute-start(bf16[1024,128]{1,0:T(8,128)(2,1)} %get-tuple-element.28), channel_id=1, source_target_pairs={{0,6},{2,0},{4,2},{6,4},{1,7},{3,1},{5,3},{7,5},{8,14},{10,8},{12,... | collective-permute-start | bytes 786440 | tf_op jit(solution)/shard_map/ppermute | solution.py:34
  138.1 5.1 %all-to-all-start.4 = ((bf16[4,64,512]{2,1,0:T(8,128)(2,1)}), bf16[4,64,512]{2,1,0:T(8,128)(2,1)S(1)}, u32[]{:S(2)}, u32[]{:S(2)}) async-start(bf16[4,64,512]{2,1,0:T(8,128)(2,1)} %bitcast.12), calls=%async_computation.4 | async-start | bytes 524288 | tf_op jit(solution)/shard_map/all_to_all | solution.py:418
  143.2 1.1 add_convert_fusion.2
  144.6 0.9 copy-done.12
  145.4 1.0 add_convert_fusion.3
  146.5 2.4 %collective-permute-start.31 = (bf16[2048,128]{1,0:T(8,128)(2,1)S(1)}, bf16[2048,128]{1,0:T(8,128)(2,1)S(1)}, u32[]{:S(2)}, u32[]{:S(2)}) collective-permute-start(bf16[2048,128]{1,0:T(8,128)(2,1)S(1)} %pad_maximum_fusion.2), channel_id=1, source_target_pairs={{0,6},{2,0},{4,2},{6,4},{1,7},{3,1},{5,3},{7,5},{8,14},{10,8},{12,... | collective-permute-start | bytes 1572872 | tf_op jit(solution)/shard_map/ppermute | solution.py:34
  149.0 1.0 add_convert_fusion.4
  150.1 1.0 add_convert_fusion.5
  151.2 3.3 %collective-permute-start.23 = (bf16[2048,128]{1,0:T(8,128)(2,1)S(1)}, bf16[2048,128]{1,0:T(8,128)(2,1)S(1)}, u32[]{:S(2)}, u32[]{:S(2)}) collective-permute-start(bf16[2048,128]{1,0:T(8,128)(2,1)S(1)} %pad_maximum_fusion), channel_id=1, source_target_pairs={{0,48},{16,0},{32,16},{48,32},{1,49},{17,1},{33,17},{49,33},{2,50}... | collective-permute-start | bytes 1572872 | tf_op jit(solution)/shard_map/ppermute | solution.py:34
  154.5 3.6 %collective-permute-done.33 = bf16[2048,128]{1,0:T(8,128)(2,1)S(1)} collective-permute-done((bf16[2048,128]{1,0:T(8,128)(2,1)S(1)}, bf16[2048,128]{1,0:T(8,128)(2,1)S(1)}, u32[]{:S(2)}, u32[]{:S(2)}) %collective-permute-start.33) | collective-permute-done | bytes 524320 | tf_op jit(solution)/shard_map/ppermute | solution.py:34
  158.1 0.9 collective-permute-done.31
  159.2 2.5 %collective-permute-start.34 = (bf16[256,128]{1,0:T(8,128)(2,1)S(1)}, bf16[256,128]{1,0:T(8,128)(2,1)S(1)}, u32[]{:S(2)}, u32[]{:S(2)}) collective-permute-start(bf16[256,128]{1,0:T(8,128)(2,1)S(1)} %get-tuple-element.47), channel_id=1, source_target_pairs={{0,48},{16,0},{32,16},{48,32},{1,49},{17,1},{33,17},{49,33},{2,50}... | collective-permute-start | bytes 196616 | tf_op jit(solution)/shard_map/ppermute | solution.py:34
  161.6 1.6 collective-permute-done.25
  163.2 1.0 collective-permute-done.23
  164.4 0.8 collective-permute-start.26
  165.2 1.3 collective-permute-start.28
  167.2 0.8 collective-permute-start.37
  168.0 2.6 %collective-permute-start.35 = (bf16[512,128]{1,0:T(8,128)(2,1)S(1)}, bf16[512,128]{1,0:T(8,128)(2,1)S(1)}, u32[]{:S(2)}, u32[]{:S(2)}) collective-permute-start(bf16[512,128]{1,0:T(8,128)(2,1)S(1)} %pad_maximum_fusion.7), channel_id=1, source_target_pairs={{0,48},{16,0},{32,16},{48,32},{1,49},{17,1},{33,17},{49,33},{2,50}... | collective-permute-start | bytes 393224 | tf_op jit(solution)/shard_map/ppermute | solution.py:34
  170.8 0.8 collective-permute-start.29
  171.7 2.6 %collective-permute-start.27 = (bf16[512,128]{1,0:T(8,128)(2,1)S(1)}, bf16[512,128]{1,0:T(8,128)(2,1)S(1)}, u32[]{:S(2)}, u32[]{:S(2)}) collective-permute-start(bf16[512,128]{1,0:T(8,128)(2,1)S(1)} %pad_maximum_fusion.5), channel_id=1, source_target_pairs={{0,6},{2,0},{4,2},{6,4},{1,7},{3,1},{5,3},{7,5},{8,14},{10,8},{12,... | collective-permute-start | bytes 393224 | tf_op jit(solution)/shard_map/ppermute | solution.py:34
  174.3 2.8 %collective-permute-done.29 = bf16[512,128]{1,0:T(8,128)(2,1)S(1)} collective-permute-done((bf16[512,128]{1,0:T(8,128)(2,1)S(1)}, bf16[512,128]{1,0:T(8,128)(2,1)S(1)}, u32[]{:S(2)}, u32[]{:S(2)}) %collective-permute-start.29) | collective-permute-done | bytes 131104 | tf_op jit(solution)/shard_map/ppermute | solution.py:34
  177.9 5.1 %all-to-all-start.5 = ((bf16[8,2,64,128]{3,2,1,0:T(8,128)(2,1)}), bf16[8,2,64,128]{3,2,1,0:T(8,128)(2,1)S(1)}, u32[]{:S(2)}, u32[]{:S(2)}) async-start(bf16[8,2,64,128]{3,2,1,0:T(8,128)(2,1)} %pad_maximum_fusion.4), calls=%async_computation.5 | async-start | bytes 524288 | tf_op jit(solution)/shard_map/all_to_all | solution.py:428
  183.7 8.3 %all-to-all-done.5 = bf16[8,2,64,128]{3,2,1,0:T(8,128)(2,1)S(1)} async-done(((bf16[8,2,64,128]{3,2,1,0:T(8,128)(2,1)}), bf16[8,2,64,128]{3,2,1,0:T(8,128)(2,1)S(1)}, u32[]{:S(2)}, u32[]{:S(2)}) %all-to-all-start.5) | async-done | bytes 262176 | tf_op jit(solution)/shard_map/all_to_all | solution.py:428
  (165 shorter events, 22.5 us)
Async XLA Ops:
  2.3 19.1 %all-to-all-start.2 = ((bf16[8,2,64,128]{3,2,1,0:T(8,128)(2,1)}), bf16[8,2,64,128]{3,2,1,0:T(8,128)(2,1)S(1)}, u32[]{:S(2)}, u32[]{:S(2)}) async-start(bf16[8,2,64,128]{3,2,1,0:T(8,128)(2,1)} %bitcast.5), calls=%async_computation.2 | async-start | bytes 524288 | tf_op jit(solution)/shard_map/all_to_all | solution.py:385
  21.4 23.5 %all-to-all-start.3 = ((f32[4,1,256]{2,1,0:T(1,128)}), f32[4,1,256]{2,1,0:T(1,128)S(1)}, u32[]{:S(2)}, u32[]{:S(2)}) async-start(f32[4,1,256]{2,1,0:T(1,128)} %reshape.214), calls=%async_computation.3 | async-start | bytes 8192 | tf_op jit(solution)/shard_map/all_to_all | solution.py:399
  26.1 6.5 %collective-permute-start.3 = (bf16[512,128]{1,0:T(8,128)(2,1)S(1)}, bf16[512,128]{1,0:T(8,128)(2,1)S(1)}, u32[]{:S(2)}, u32[]{:S(2)}) collective-permute-start(bf16[512,128]{1,0:T(8,128)(2,1)S(1)} %bitcast.65), channel_id=1, source_target_pairs={{0,6},{2,0},{4,2},{6,4},{1,7},{3,1},{5,3},{7,5},{8,14},{10,8},{12,... | collective-permute-start | bytes 393224 | tf_op jit(solution)/shard_map/ppermute | solution.py:34
  29.2 6.8 %collective-permute-start.2 = (bf16[512,128]{1,0:T(8,128)(2,1)S(1)}, bf16[512,128]{1,0:T(8,128)(2,1)S(1)}, u32[]{:S(2)}, u32[]{:S(2)}) collective-permute-start(bf16[512,128]{1,0:T(8,128)(2,1)S(1)} %bitcast.66), channel_id=1, source_target_pairs={{0,2},{2,4},{4,6},{6,0},{1,3},{3,5},{5,7},{7,1},{8,10},{10,12},{12... | collective-permute-start | bytes 393224 | tf_op jit(solution)/shard_map/ppermute | solution.py:34
  29.2 6.9 %collective-permute-start.14 = (bf16[512,128]{1,0:T(8,128)(2,1)S(1)}, bf16[512,128]{1,0:T(8,128)(2,1)S(1)}, u32[]{:S(2)}, u32[]{:S(2)}) collective-permute-start(bf16[512,128]{1,0:T(8,128)(2,1)S(1)} %bitcast.62), channel_id=1, source_target_pairs={{0,48},{16,0},{32,16},{48,32},{1,49},{17,1},{33,17},{49,33},{2,50}... | collective-permute-start | bytes 393224 | tf_op jit(solution)/shard_map/ppermute | solution.py:34
  32.0 7.4 %collective-permute-start.13 = (bf16[512,128]{1,0:T(8,128)(2,1)S(1)}, bf16[512,128]{1,0:T(8,128)(2,1)S(1)}, u32[]{:S(2)}, u32[]{:S(2)}) collective-permute-start(bf16[512,128]{1,0:T(8,128)(2,1)S(1)} %bitcast.63), channel_id=1, source_target_pairs={{0,16},{16,32},{32,48},{48,0},{1,17},{17,33},{33,49},{49,1},{2,18}... | collective-permute-start | bytes 393224 | tf_op jit(solution)/shard_map/ppermute | solution.py:34
  32.7 8.9 %collective-permute-start.5 = (bf16[256,128]{1,0:T(8,128)(2,1)S(1)}, bf16[256,128]{1,0:T(8,128)(2,1)S(1)}, u32[]{:S(2)}, u32[]{:S(2)}) collective-permute-start(bf16[256,128]{1,0:T(8,128)(2,1)S(1)} %slice.152), channel_id=1, source_target_pairs={{0,6},{2,0},{4,2},{6,4},{1,7},{3,1},{5,3},{7,5},{8,14},{10,8},{12,... | collective-permute-start | bytes 196616 | tf_op jit(solution)/shard_map/ppermute | solution.py:34
  36.0 5.6 %collective-permute-start.4 = (bf16[256,128]{1,0:T(8,128)(2,1)S(1)}, bf16[256,128]{1,0:T(8,128)(2,1)S(1)}, u32[]{:S(2)}, u32[]{:S(2)}) collective-permute-start(bf16[256,128]{1,0:T(8,128)(2,1)S(1)} %slice.151), channel_id=1, source_target_pairs={{0,2},{2,4},{4,6},{6,0},{1,3},{3,5},{5,7},{7,1},{8,10},{10,12},{12... | collective-permute-start | bytes 196616 | tf_op jit(solution)/shard_map/ppermute | solution.py:34
  36.1 15.2 %collective-permute-start.16 = (bf16[256,128]{1,0:T(8,128)(2,1)S(1)}, bf16[256,128]{1,0:T(8,128)(2,1)S(1)}, u32[]{:S(2)}, u32[]{:S(2)}) collective-permute-start(bf16[256,128]{1,0:T(8,128)(2,1)S(1)} %slice.157), channel_id=1, source_target_pairs={{0,48},{16,0},{32,16},{48,32},{1,49},{17,1},{33,17},{49,33},{2,50}... | collective-permute-start | bytes 196616 | tf_op jit(solution)/shard_map/ppermute | solution.py:34
  39.4 11.2 %collective-permute-start.15 = (bf16[256,128]{1,0:T(8,128)(2,1)S(1)}, bf16[256,128]{1,0:T(8,128)(2,1)S(1)}, u32[]{:S(2)}, u32[]{:S(2)}) collective-permute-start(bf16[256,128]{1,0:T(8,128)(2,1)S(1)} %slice.156), channel_id=1, source_target_pairs={{0,16},{16,32},{32,48},{48,0},{1,17},{17,33},{33,49},{49,1},{2,18}... | collective-permute-start | bytes 196616 | tf_op jit(solution)/shard_map/ppermute | solution.py:34
  41.6 32.1 %copy-start.2 = (bf16[2048,128]{1,0:T(8,128)(2,1)}, bf16[2048,128]{1,0:T(8,128)(2,1)S(1)}, u32[]{:S(2)}) copy-start(bf16[2048,128]{1,0:T(8,128)(2,1)S(1)} %constant_dynamic-update-slice_fusion.k0) | copy-start | bytes 1572868
  41.6 18.8 %collective-permute-start.7 = (bf16[2048,128]{1,0:T(8,128)(2,1)S(1)}, bf16[2048,128]{1,0:T(8,128)(2,1)S(1)}, u32[]{:S(2)}, u32[]{:S(2)}) collective-permute-start(bf16[2048,128]{1,0:T(8,128)(2,1)S(1)} %constant_dynamic-update-slice_fusion.k0), channel_id=1, source_target_pairs={{0,48},{16,0},{32,16},{48,32},{1,49},{17,1},{33,17},{49,33},{2,50}... | collective-permute-start | bytes 1572872 | tf_op jit(solution)/shard_map/ppermute | solution.py:34
  44.9 19.1 %collective-permute-start.6 = (bf16[2048,128]{1,0:T(8,128)(2,1)S(1)}, bf16[2048,128]{1,0:T(8,128)(2,1)S(1)}, u32[]{:S(2)}, u32[]{:S(2)}) collective-permute-start(bf16[2048,128]{1,0:T(8,128)(2,1)S(1)} %constant_dynamic-update-slice_fusion.k0), channel_id=1, source_target_pairs={{0,16},{16,32},{32,48},{48,0},{1,17},{17,33},{33,49},{49,1},{2,18}... | collective-permute-start | bytes 1572872 | tf_op jit(solution)/shard_map/ppermute | solution.py:34
  44.9 11.3 %all-to-all-start = ((bf16[4,64,512]{2,1,0:T(8,128)(2,1)}), bf16[4,64,512]{2,1,0:T(8,128)(2,1)S(1)}, u32[]{:S(2)}, u32[]{:S(2)}) async-start(bf16[4,64,512]{2,1,0:T(8,128)(2,1)} %bitcast.49), calls=%async_computation | async-start | bytes 524288 | tf_op jit(solution)/shard_map/all_to_all | solution.py:371
  52.0 14.0 %collective-permute-start.18 = (bf16[2048,128]{1,0:T(8,128)(2,1)}, bf16[2048,128]{1,0:T(8,128)(2,1)}, u32[]{:S(2)}, u32[]{:S(2)}) collective-permute-start(bf16[2048,128]{1,0:T(8,128)(2,1)} %constant_dynamic-update-slice_fusion.5.v0), channel_id=1, source_target_pairs={{0,6},{2,0},{4,2},{6,4},{1,7},{3,1},{5,3},{7,5},{8,14},{10,8},{12,... | collective-permute-start | bytes 1572872 | tf_op jit(solution)/shard_map/ppermute | solution.py:34
  53.9 14.0 %collective-permute-start.17 = (bf16[2048,128]{1,0:T(8,128)(2,1)}, bf16[2048,128]{1,0:T(8,128)(2,1)}, u32[]{:S(2)}, u32[]{:S(2)}) collective-permute-start(bf16[2048,128]{1,0:T(8,128)(2,1)} %constant_dynamic-update-slice_fusion.5.v0), channel_id=1, source_target_pairs={{0,2},{2,4},{4,6},{6,0},{1,3},{3,5},{5,7},{7,1},{8,10},{10,12},{12... | collective-permute-start | bytes 1572872 | tf_op jit(solution)/shard_map/ppermute | solution.py:34
  56.2 11.6 %all-to-all-start.1 = ((bf16[4,64,512]{2,1,0:T(8,128)(2,1)}), bf16[4,64,512]{2,1,0:T(8,128)(2,1)S(1)}, u32[]{:S(2)}, u32[]{:S(2)}) async-start(bf16[4,64,512]{2,1,0:T(8,128)(2,1)} %bitcast.47), calls=%async_computation.1 | async-start | bytes 524288 | tf_op jit(solution)/shard_map/all_to_all | solution.py:371
  60.3 8.9 %collective-permute-start = (bf16[256,512]{1,0:T(8,128)(2,1)S(1)}, bf16[256,512]{1,0:T(8,128)(2,1)S(1)}, u32[]{:S(2)}, u32[]{:S(2)}) collective-permute-start(bf16[256,512]{1,0:T(8,128)(2,1)S(1)} %bitcast.53), channel_id=1, source_target_pairs={{0,1},{1,0},{2,3},{3,2},{4,5},{5,4},{6,7},{7,6},{8,9},{9,8},{10,11... | collective-permute-start | bytes 786440 | tf_op jit(solution)/shard_map/ppermute | solution.py:38
  60.5 13.3 %copy-start = (bf16[2048,128]{1,0:T(8,128)(2,1)}, bf16[2048,128]{1,0:T(8,128)(2,1)S(1)}, u32[]{:S(2)}) copy-start(bf16[2048,128]{1,0:T(8,128)(2,1)S(1)} %collective-permute-done.7.k2) | copy-start | bytes 1572868
  60.5 11.0 %collective-permute-start.9 = (bf16[1024,128]{1,0:T(8,128)(2,1)S(1)}, bf16[1024,128]{1,0:T(8,128)(2,1)S(1)}, u32[]{:S(2)}, u32[]{:S(2)}) collective-permute-start(bf16[1024,128]{1,0:T(8,128)(2,1)S(1)} %slice.154), channel_id=1, source_target_pairs={{0,48},{16,0},{32,16},{48,32},{1,49},{17,1},{33,17},{49,33},{2,50}... | collective-permute-start | bytes 786440 | tf_op jit(solution)/shard_map/ppermute | solution.py:34
  64.0 9.7 %collective-permute-start.8 = (bf16[1024,128]{1,0:T(8,128)(2,1)S(1)}, bf16[1024,128]{1,0:T(8,128)(2,1)S(1)}, u32[]{:S(2)}, u32[]{:S(2)}) collective-permute-start(bf16[1024,128]{1,0:T(8,128)(2,1)S(1)} %slice.153), channel_id=1, source_target_pairs={{0,16},{16,32},{32,48},{48,0},{1,17},{17,33},{33,49},{49,1},{2,18}... | collective-permute-start | bytes 786440 | tf_op jit(solution)/shard_map/ppermute | solution.py:34
  65.9 26.7 %collective-permute-start.12 = (f32[2,1,512]{2,1,0:T(1,128)S(1)}, f32[2,1,512]{2,1,0:T(1,128)S(1)}, u32[]{:S(2)}, u32[]{:S(2)}) collective-permute-start(f32[2,1,512]{2,1,0:T(1,128)S(1)} %reshape.211.delta_own), channel_id=1, source_target_pairs={{0,1},{1,0},{2,3},{3,2},{4,5},{5,4},{6,7},{7,6},{8,9},{9,8},{10,11... | collective-permute-start | bytes 12296 | tf_op jit(solution)/shard_map/ppermute | solution.py:38
  67.8 25.4 %collective-permute-start.1 = (bf16[256,512]{1,0:T(8,128)(2,1)S(1)}, bf16[256,512]{1,0:T(8,128)(2,1)S(1)}, u32[]{:S(2)}, u32[]{:S(2)}) collective-permute-start(bf16[256,512]{1,0:T(8,128)(2,1)S(1)} %bitcast.56), channel_id=1, source_target_pairs={{0,1},{1,0},{2,3},{3,2},{4,5},{5,4},{6,7},{7,6},{8,9},{9,8},{10,11... | collective-permute-start | bytes 786440 | tf_op jit(solution)/shard_map/ppermute | solution.py:38
  69.2 24.0 %collective-permute-start.20 = (bf16[1024,128]{1,0:T(8,128)(2,1)S(1)}, bf16[1024,128]{1,0:T(8,128)(2,1)S(1)}, u32[]{:S(2)}, u32[]{:S(2)}) collective-permute-start(bf16[1024,128]{1,0:T(8,128)(2,1)S(1)} %copy-done.15), channel_id=1, source_target_pairs={{0,6},{2,0},{4,2},{6,4},{1,7},{3,1},{5,3},{7,5},{8,14},{10,8},{12,... | collective-permute-start | bytes 786440 | tf_op jit(solution)/shard_map/ppermute | solution.py:34
  71.4 21.1 %copy-start.3 = (bf16[1024,128]{1,0:T(8,128)(2,1)}, bf16[1024,128]{1,0:T(8,128)(2,1)S(1)}, u32[]{:S(2)}) copy-start(bf16[1024,128]{1,0:T(8,128)(2,1)S(1)} %collective-permute-done.9.k4) | copy-start | bytes 786436
  71.4 21.8 %collective-permute-start.19 = (bf16[1024,128]{1,0:T(8,128)(2,1)S(1)}, bf16[1024,128]{1,0:T(8,128)(2,1)S(1)}, u32[]{:S(2)}, u32[]{:S(2)}) collective-permute-start(bf16[1024,128]{1,0:T(8,128)(2,1)S(1)} %slice.158), channel_id=1, source_target_pairs={{0,2},{2,4},{4,6},{6,0},{1,3},{3,5},{5,7},{7,1},{8,10},{10,12},{12... | collective-permute-start | bytes 786440 | tf_op jit(solution)/shard_map/ppermute | solution.py:34
  73.7 18.8 %copy-start.5 = (bf16[1024,128]{1,0:T(8,128)(2,1)}, bf16[1024,128]{1,0:T(8,128)(2,1)S(1)}, u32[]{:S(2)}) copy-start(bf16[1024,128]{1,0:T(8,128)(2,1)S(1)} %collective-permute-done.8.k3) | copy-start | bytes 786436
  92.5 1.3 collective-permute-start.10
  92.7 1.3 collective-permute-start.11
  129.1 8.3 %collective-permute-start.21 = (bf16[256,512]{1,0:T(8,128)(2,1)S(1)}, bf16[256,512]{1,0:T(8,128)(2,1)S(1)}, u32[]{:S(2)}, u32[]{:S(2)}) collective-permute-start(bf16[256,512]{1,0:T(8,128)(2,1)S(1)} %get-tuple-element.20), channel_id=1, source_target_pairs={{0,1},{1,0},{2,3},{3,2},{4,5},{5,4},{6,7},{7,6},{8,9},{9,8},{10,11... | collective-permute-start | bytes 786440 | tf_op jit(solution)/shard_map/ppermute | solution.py:38
  129.5 13.7 %collective-permute-start.32 = (bf16[1024,128]{1,0:T(8,128)(2,1)}, bf16[1024,128]{1,0:T(8,128)(2,1)}, u32[]{:S(2)}, u32[]{:S(2)}) collective-permute-start(bf16[1024,128]{1,0:T(8,128)(2,1)} %get-tuple-element.30), channel_id=1, source_target_pairs={{0,2},{2,4},{4,6},{6,0},{1,3},{3,5},{5,7},{7,1},{8,10},{10,12},{12... | collective-permute-start | bytes 786440 | tf_op jit(solution)/shard_map/ppermute | solution.py:34
  132.1 18.0 %collective-permute-start.22 = (bf16[1024,128]{1,0:T(8,128)(2,1)S(1)}, bf16[1024,128]{1,0:T(8,128)(2,1)}, u32[]{:S(2)}, u32[]{:S(2)}) collective-permute-start(bf16[1024,128]{1,0:T(8,128)(2,1)S(1)} %get-tuple-element.23), channel_id=1, source_target_pairs={{0,48},{16,0},{32,16},{48,32},{1,49},{17,1},{33,17},{49,33},{2,50}... | collective-permute-start | bytes 786440 | tf_op jit(solution)/shard_map/ppermute | solution.py:34
  133.1 15.9 %collective-permute-start.24 = (bf16[1024,128]{1,0:T(8,128)(2,1)S(1)}, bf16[1024,128]{1,0:T(8,128)(2,1)}, u32[]{:S(2)}, u32[]{:S(2)}) collective-permute-start(bf16[1024,128]{1,0:T(8,128)(2,1)S(1)} %get-tuple-element.25), channel_id=1, source_target_pairs={{0,16},{16,32},{32,48},{48,0},{1,17},{17,33},{33,49},{49,1},{2,18}... | collective-permute-start | bytes 786440 | tf_op jit(solution)/shard_map/ppermute | solution.py:34
  134.1 10.4 %collective-permute-start.30 = (bf16[1024,128]{1,0:T(8,128)(2,1)}, bf16[1024,128]{1,0:T(8,128)(2,1)}, u32[]{:S(2)}, u32[]{:S(2)}) collective-permute-start(bf16[1024,128]{1,0:T(8,128)(2,1)} %get-tuple-element.28), channel_id=1, source_target_pairs={{0,6},{2,0},{4,2},{6,4},{1,7},{3,1},{5,3},{7,5},{8,14},{10,8},{12,... | collective-permute-start | bytes 786440 | tf_op jit(solution)/shard_map/ppermute | solution.py:34
  138.1 39.7 %all-to-all-start.4 = ((bf16[4,64,512]{2,1,0:T(8,128)(2,1)}), bf16[4,64,512]{2,1,0:T(8,128)(2,1)S(1)}, u32[]{:S(2)}, u32[]{:S(2)}) async-start(bf16[4,64,512]{2,1,0:T(8,128)(2,1)} %bitcast.12), calls=%async_computation.4 | async-start | bytes 524288 | tf_op jit(solution)/shard_map/all_to_all | solution.py:418
  144.5 13.6 %collective-permute-start.33 = (bf16[2048,128]{1,0:T(8,128)(2,1)S(1)}, bf16[2048,128]{1,0:T(8,128)(2,1)S(1)}, u32[]{:S(2)}, u32[]{:S(2)}) collective-permute-start(bf16[2048,128]{1,0:T(8,128)(2,1)S(1)} %pad_maximum_fusion.3), channel_id=1, source_target_pairs={{0,2},{2,4},{4,6},{6,0},{1,3},{3,5},{5,7},{7,1},{8,10},{10,12},{12... | collective-permute-start | bytes 1572872 | tf_op jit(solution)/shard_map/ppermute | solution.py:34
  146.5 12.4 %collective-permute-start.31 = (bf16[2048,128]{1,0:T(8,128)(2,1)S(1)}, bf16[2048,128]{1,0:T(8,128)(2,1)S(1)}, u32[]{:S(2)}, u32[]{:S(2)}) collective-permute-start(bf16[2048,128]{1,0:T(8,128)(2,1)S(1)} %pad_maximum_fusion.2), channel_id=1, source_target_pairs={{0,6},{2,0},{4,2},{6,4},{1,7},{3,1},{5,3},{7,5},{8,14},{10,8},{12,... | collective-permute-start | bytes 1572872 | tf_op jit(solution)/shard_map/ppermute | solution.py:34
  150.0 13.2 %collective-permute-start.25 = (bf16[2048,128]{1,0:T(8,128)(2,1)S(1)}, bf16[2048,128]{1,0:T(8,128)(2,1)S(1)}, u32[]{:S(2)}, u32[]{:S(2)}) collective-permute-start(bf16[2048,128]{1,0:T(8,128)(2,1)S(1)} %pad_maximum_fusion.1), channel_id=1, source_target_pairs={{0,16},{16,32},{32,48},{48,0},{1,17},{17,33},{33,49},{49,1},{2,18}... | collective-permute-start | bytes 1572872 | tf_op jit(solution)/shard_map/ppermute | solution.py:34
  151.2 13.0 %collective-permute-start.23 = (bf16[2048,128]{1,0:T(8,128)(2,1)S(1)}, bf16[2048,128]{1,0:T(8,128)(2,1)S(1)}, u32[]{:S(2)}, u32[]{:S(2)}) collective-permute-start(bf16[2048,128]{1,0:T(8,128)(2,1)S(1)} %pad_maximum_fusion), channel_id=1, source_target_pairs={{0,48},{16,0},{32,16},{48,32},{1,49},{17,1},{33,17},{49,33},{2,50}... | collective-permute-start | bytes 1572872 | tf_op jit(solution)/shard_map/ppermute | solution.py:34
  159.2 7.4 %collective-permute-start.34 = (bf16[256,128]{1,0:T(8,128)(2,1)S(1)}, bf16[256,128]{1,0:T(8,128)(2,1)S(1)}, u32[]{:S(2)}, u32[]{:S(2)}) collective-permute-start(bf16[256,128]{1,0:T(8,128)(2,1)S(1)} %get-tuple-element.47), channel_id=1, source_target_pairs={{0,48},{16,0},{32,16},{48,32},{1,49},{17,1},{33,17},{49,33},{2,50}... | collective-permute-start | bytes 196616 | tf_op jit(solution)/shard_map/ppermute | solution.py:34
  161.6 5.5 %collective-permute-start.36 = (bf16[256,128]{1,0:T(8,128)(2,1)S(1)}, bf16[256,128]{1,0:T(8,128)(2,1)S(1)}, u32[]{:S(2)}, u32[]{:S(2)}) collective-permute-start(bf16[256,128]{1,0:T(8,128)(2,1)S(1)} %get-tuple-element.48), channel_id=1, source_target_pairs={{0,16},{16,32},{32,48},{48,0},{1,17},{17,33},{33,49},{49,1},{2,18}... | collective-permute-start | bytes 196616 | tf_op jit(solution)/shard_map/ppermute | solution.py:34
  164.4 6.1 %collective-permute-start.26 = (bf16[256,128]{1,0:T(8,128)(2,1)S(1)}, bf16[256,128]{1,0:T(8,128)(2,1)S(1)}, u32[]{:S(2)}, u32[]{:S(2)}) collective-permute-start(bf16[256,128]{1,0:T(8,128)(2,1)S(1)} %get-tuple-element.41), channel_id=1, source_target_pairs={{0,6},{2,0},{4,2},{6,4},{1,7},{3,1},{5,3},{7,5},{8,14},{10,8},{12,... | collective-permute-start | bytes 196616 | tf_op jit(solution)/shard_map/ppermute | solution.py:34
  165.2 5.5 %collective-permute-start.28 = (bf16[256,128]{1,0:T(8,128)(2,1)S(1)}, bf16[256,128]{1,0:T(8,128)(2,1)S(1)}, u32[]{:S(2)}, u32[]{:S(2)}) collective-permute-start(bf16[256,128]{1,0:T(8,128)(2,1)S(1)} %get-tuple-element.42), channel_id=1, source_target_pairs={{0,2},{2,4},{4,6},{6,0},{1,3},{3,5},{5,7},{7,1},{8,10},{10,12},{12... | collective-permute-start | bytes 196616 | tf_op jit(solution)/shard_map/ppermute | solution.py:34
  167.2 7.1 %collective-permute-start.37 = (bf16[512,128]{1,0:T(8,128)(2,1)S(1)}, bf16[512,128]{1,0:T(8,128)(2,1)S(1)}, u32[]{:S(2)}, u32[]{:S(2)}) collective-permute-start(bf16[512,128]{1,0:T(8,128)(2,1)S(1)} %pad_maximum_fusion.8), channel_id=1, source_target_pairs={{0,16},{16,32},{32,48},{48,0},{1,17},{17,33},{33,49},{49,1},{2,18}... | collective-permute-start | bytes 393224 | tf_op jit(solution)/shard_map/ppermute | solution.py:34
  168.0 6.2 %collective-permute-start.35 = (bf16[512,128]{1,0:T(8,128)(2,1)S(1)}, bf16[512,128]{1,0:T(8,128)(2,1)S(1)}, u32[]{:S(2)}, u32[]{:S(2)}) collective-permute-start(bf16[512,128]{1,0:T(8,128)(2,1)S(1)} %pad_maximum_fusion.7), channel_id=1, source_target_pairs={{0,48},{16,0},{32,16},{48,32},{1,49},{17,1},{33,17},{49,33},{2,50}... | collective-permute-start | bytes 393224 | tf_op jit(solution)/shard_map/ppermute | solution.py:34
  170.8 6.3 %collective-permute-start.29 = (bf16[512,128]{1,0:T(8,128)(2,1)S(1)}, bf16[512,128]{1,0:T(8,128)(2,1)S(1)}, u32[]{:S(2)}, u32[]{:S(2)}) collective-permute-start(bf16[512,128]{1,0:T(8,128)(2,1)S(1)} %pad_maximum_fusion.6), channel_id=1, source_target_pairs={{0,2},{2,4},{4,6},{6,0},{1,3},{3,5},{5,7},{7,1},{8,10},{10,12},{12... | collective-permute-start | bytes 393224 | tf_op jit(solution)/shard_map/ppermute | solution.py:34
  171.7 5.4 %collective-permute-start.27 = (bf16[512,128]{1,0:T(8,128)(2,1)S(1)}, bf16[512,128]{1,0:T(8,128)(2,1)S(1)}, u32[]{:S(2)}, u32[]{:S(2)}) collective-permute-start(bf16[512,128]{1,0:T(8,128)(2,1)S(1)} %pad_maximum_fusion.5), channel_id=1, source_target_pairs={{0,6},{2,0},{4,2},{6,4},{1,7},{3,1},{5,3},{7,5},{8,14},{10,8},{12,... | collective-permute-start | bytes 393224 | tf_op jit(solution)/shard_map/ppermute | solution.py:34
  177.9 14.1 %all-to-all-start.5 = ((bf16[8,2,64,128]{3,2,1,0:T(8,128)(2,1)}), bf16[8,2,64,128]{3,2,1,0:T(8,128)(2,1)S(1)}, u32[]{:S(2)}, u32[]{:S(2)}) async-start(bf16[8,2,64,128]{3,2,1,0:T(8,128)(2,1)} %pad_maximum_fusion.4), calls=%async_computation.5 | async-start | bytes 524288 | tf_op jit(solution)/shard_map/all_to_all | solution.py:428
  (16 other events, 45.8 us)

commit v2 on v1

v2 whole, which is shorter than its diff:
```python
from functools import partial
import math

import jax
import jax.numpy as jnp
from jax import lax
from jax.experimental import pallas as pl
from jax.experimental.pallas import tpu as pltpu
from jax.sharding import Mesh, PartitionSpec as P

HEAD_DIM = 128
BLOCK = 128
TOKENS = 64
HEADS_HERE = 8
ROWS = TOKENS * HEADS_HERE
WIDE = HEADS_HERE * HEAD_DIM
CHUNK_BLOCKS = 4
CHUNK = CHUNK_BLOCKS * BLOCK
SLOTS = 32
TILES = 8
CHUNKS = SLOTS // CHUNK_BLOCKS
PIECE = 512
PIECES = 4
OTHER = PIECES * PIECE
PAIR = 2 * HEAD_DIM
OFFSETS = (0, -1, 1, 2)
PIECE_AT = {offset % 4: index for index, offset in enumerate(OFFSETS)}
FACTOR = HEAD_DIM ** (-0.5)
LOG2E = math.log2(math.e)
SCALE2 = FACTOR * LOG2E
NEG = -1e30
VMEM_BYTES = 48 * 1024 * 1024

def ring_pairs(steps):
    return [(source, (source + steps) % 4) for source in range(4)]


def send(value, axis, steps):
    return lax.ppermute(value, axis, ring_pairs(steps))


def swap_core(value):
    return lax.ppermute(value, "core", [(0, 1), (1, 0)])


def swap_group(value):
    return lax.ppermute(value, "head", [(source, source ^ 2) for source in range(4)])


def swap_half(value):
    return lax.ppermute(value, "head", [(source, source ^ 1) for source in range(4)])


def swap_z(value):
    return lax.ppermute(value, "zh", [(0, 1), (1, 0)])


def swap_both(value):
    return lax.ppermute(value, ("head", "zh"), [(source, source ^ 5) for source in range(8)])


def gather_direct(own, axis):
    return [own] + [send(own, axis, -offset) for offset in OFFSETS[1:]]


def wide(value):
    return value.astype(jnp.float32)


def add(*values):
    total = wide(values[0])
    for value in values[1:]:
        total = total + wide(value)
    return total.astype(jnp.bfloat16)


def reduce_direct(pieces, axis):
    arrived = [send(piece, axis, offset) for piece, offset in zip(pieces[1:], OFFSETS[1:])]
    return add(pieces[0], *arrived)


def kv_copies(pieces, other, gathered, sems, outward):
    copies = []
    for index in range(PIECES + 1):
        outside = other if index == PIECES else pieces[index]
        inside = gathered.at[pl.ds(index * PIECE, outside.shape[0])]
        ends = (inside, outside) if outward else (outside, inside)
        copy = pltpu.make_async_copy(*ends, sems.at[index])
        copy.start()
        copies.append(copy)
    return copies


def spread_heads(sources, target):
    for tile in range(TILES):
        for head in range(HEADS_HERE):
            target[tile, pl.ds(head * TOKENS, TOKENS), :] = sources[tile // 2][
                pl.ds(tile % 2 * TOKENS, TOKENS), pl.ds(head * HEAD_DIM, HEAD_DIM)
            ]


def load_chunk(source, slot_ref, chunk, column):
    return jnp.concatenate(
        [
            source[pl.ds(pl.multiple_of(slot_ref[chunk * CHUNK_BLOCKS + j] * BLOCK, BLOCK), BLOCK),
                pl.ds(column, HEAD_DIM),
            ]
            for j in range(CHUNK_BLOCKS)
        ],
        axis=0,
    )


def dot_rows(left, right):
    return lax.dot_general(
        left, right, (((1,), (1,)), ((), ())), preferred_element_type=jnp.float32
    )


def dot_columns(left, right):
    return lax.dot_general(
        left, right, (((0,), (0,)), ((), ())), preferred_element_type=jnp.float32
    )


def masked(value, fill, ids_ref, chunk, query_start):
    rows = lax.broadcasted_iota(jnp.int32, (BLOCK, ROWS), 0)
    lanes = lax.broadcasted_iota(jnp.int32, (BLOCK, ROWS), 1) % TOKENS
    ahead = rows - lanes
    parts = []
    for j in range(CHUNK_BLOCKS):
        limit = query_start - ids_ref[chunk * CHUNK_BLOCKS + j] * BLOCK
        parts.append(jnp.where(ahead <= limit, value[j * BLOCK : (j + 1) * BLOCK], fill))
    return jnp.concatenate(parts, axis=0)


def for_tiles(chunk, query, count_ref, tile):
    count = count_ref[query]
    full = count // CHUNK_BLOCKS

    @pl.when(chunk < full)
    def _():
        tile(chunk, query, False)

    @pl.when((chunk >= full) & (chunk * CHUNK_BLOCKS < count_ref[query + TILES]))
    def _():
        tile(chunk, query, True)


def lse_kernel(slot_ref, ids_ref, count_ref, start_ref, delta_ref, *refs):
    rows, pieces, other = refs[:4], refs[4 : 4 + PIECES], refs[4 + PIECES]
    stat_ref, gathered, queries, max_acc, sum_acc, sems = refs[5 + PIECES :]
    copies = kv_copies(pieces, other, gathered, sems, False)
    spread_heads(rows, queries)
    max_acc[...] = jnp.full(max_acc.shape, NEG, jnp.float32)
    sum_acc[...] = jnp.zeros(sum_acc.shape, jnp.float32)
    for copy in copies:
        copy.wait()

    def tile(chunk, query, use_mask):
        scores = dot_rows(load_chunk(gathered, slot_ref, chunk, 0), queries[query])
        if use_mask:
            scores = masked(scores, NEG, ids_ref, chunk, start_ref[query])
        grouped = scores.reshape(CHUNK // 8, 8, ROWS)
        old_max = max_acc[query]
        new_max = jnp.maximum(old_max, jnp.max(grouped, axis=0))
        weights = jnp.exp2((grouped - new_max[None]) * SCALE2)
        sum_acc[query] = sum_acc[query] * jnp.exp2((old_max - new_max) * SCALE2) + jnp.sum(
            weights, axis=0
        )
        max_acc[query] = new_max

    def step(index, carry):
        for_tiles(index // TILES, index % TILES, count_ref, tile)
        return carry

    lax.fori_loop(0, CHUNKS * TILES, step, 0)
    for query in range(2):
        stat_ref[2 * TILES + query] = delta_ref[query]
    for query in range(TILES):
        part_max = max_acc[query]
        top = jnp.max(part_max, axis=0, keepdims=True)
        stat_ref[query] = top
        stat_ref[TILES + query] = jnp.sum(
            sum_acc[query] * jnp.exp2((part_max - top) * SCALE2), axis=0, keepdims=True
        )


def grad_kernel(slot_ref, ids_ref, count_ref, start_ref, *refs):
    q_rows, g_rows, stats = refs[:4], refs[4:8], refs[8:12]
    pieces, other = refs[12 : 12 + PIECES], refs[12 + PIECES]
    refs = refs[13 + PIECES :]
    dq_pieces, d_pieces, d_other = refs[:4], refs[4 : 4 + PIECES], refs[4 + PIECES]
    gathered, queries, grads, lse, delta, d_all, dk_acc, dv_acc, dq_acc, sems = refs[5 + PIECES :]
    copies = kv_copies(pieces, other, gathered, sems, False)
    spread_heads(q_rows, queries)
    spread_heads(g_rows, grads)
    for query in range(TILES):
        offset = OFFSETS[query // 2]
        places = [2 * PIECE_AT[(offset - source) % 4] + query % 2 for source in OFFSETS]
        tops = [stat[place] for stat, place in zip(stats, places)]
        top = jnp.maximum(jnp.maximum(tops[0], tops[1]), jnp.maximum(tops[2], tops[3]))
        total = jnp.zeros_like(top)
        for stat, place, part in zip(stats, places, tops):
            total += stat[TILES + place] * jnp.exp2((part - top) * SCALE2)
        lse[query] = top * SCALE2 + jnp.log2(total)
        delta[query] = stats[query // 2][2 * TILES + query % 2]
    dq_acc[...] = jnp.zeros(dq_acc.shape, jnp.float32)
    for copy in copies:
        copy.wait()

    def tile(chunk, query, use_mask):
        key_part = load_chunk(gathered, slot_ref, chunk, 0)
        value_part = load_chunk(gathered, slot_ref, chunk, HEAD_DIM)
        query_part = queries[query]
        grad_part = grads[query]
        scores = dot_rows(key_part, query_part)
        weights = jnp.exp2(scores * SCALE2 - lse[query])
        if use_mask:
            weights = masked(weights, 0.0, ids_ref, chunk, start_ref[query])
        dv_acc[...] += jnp.dot(
            weights.astype(jnp.bfloat16), grad_part, preferred_element_type=jnp.float32
        )
        dprob = dot_rows(value_part, grad_part)
        score_grad = (weights * (dprob - delta[query])).astype(jnp.bfloat16)
        dk_acc[...] += jnp.dot(score_grad, query_part, preferred_element_type=jnp.float32)
        dq_acc[query] += dot_columns(key_part, score_grad)

    def chunk_step(chunk, carry):
        dk_acc[...] = jnp.zeros(dk_acc.shape, jnp.float32)
        dv_acc[...] = jnp.zeros(dv_acc.shape, jnp.float32)

        def query_step(query, inner):
            for_tiles(chunk, query, count_ref, tile)
            return inner

        lax.fori_loop(0, TILES, query_step, 0)
        for j in range(CHUNK_BLOCKS):
            place = chunk * CHUNK_BLOCKS + j
            rows = pl.ds(j * BLOCK, BLOCK)
            target = pl.ds(pl.multiple_of(slot_ref[place] * BLOCK, BLOCK), BLOCK)
            d_all[target, pl.ds(0, HEAD_DIM)] = (dk_acc[rows, :] * FACTOR).astype(jnp.bfloat16)
            d_all[target, pl.ds(HEAD_DIM, HEAD_DIM)] = dv_acc[rows, :].astype(jnp.bfloat16)
        return carry

    lax.fori_loop(0, CHUNKS, chunk_step, 0)
    outs = kv_copies(d_pieces, d_other, d_all, sems, True)
    for query in range(TILES):
        target = dq_pieces[query // 2]
        for head in range(0, HEADS_HERE, 2):
            pair = (dq_acc[query, :, pl.ds(head * TOKENS, 2 * TOKENS)] * FACTOR).T
            for half in range(2):
                target[
                    pl.ds((query % 2) * TOKENS, TOKENS),
                    pl.ds((head + half) * HEAD_DIM, HEAD_DIM),
                ] = pair[half * TOKENS : (half + 1) * TOKENS].astype(target.dtype)
    for copy in outs:
        copy.wait()


SMEM = pl.BlockSpec(memory_space=pltpu.SMEM)
VMEM = pl.BlockSpec(memory_space=pltpu.VMEM)
ANY = pl.BlockSpec(memory_space=pl.ANY)
PAIRS = (SLOTS + 2) * TILES // 2


def call_lse(tables, delta, rows, pieces):
    work = PAIRS * BLOCK * ROWS
    return pl.pallas_call(
        lse_kernel,
        out_shape=jax.ShapeDtypeStruct((2 * TILES + 2, 1, ROWS), jnp.float32),
        in_specs=[SMEM] * 4 + [VMEM] * 5 + [ANY] * (PIECES + 1),
        out_specs=VMEM,
        scratch_shapes=[
            pltpu.VMEM((SLOTS * BLOCK, PAIR), jnp.bfloat16),
            pltpu.VMEM((TILES, ROWS, HEAD_DIM), jnp.bfloat16),
            pltpu.VMEM((TILES, 8, ROWS), jnp.float32),
            pltpu.VMEM((TILES, 8, ROWS), jnp.float32),
            pltpu.SemaphoreType.DMA((PIECES + 1,)),
        ],
        compiler_params=pltpu.CompilerParams(vmem_limit_bytes=VMEM_BYTES),
        cost_estimate=pl.CostEstimate(
            flops=8 * work * HEAD_DIM, bytes_accessed=4 << 20, transcendentals=work
        ),
        name="lse",
    )(*tables, delta, *rows, *pieces)


def call_grads(tables, q_rows, g_rows, stats, pieces):
    work = PAIRS * BLOCK * ROWS
    flat = jax.ShapeDtypeStruct((2 * TOKENS, WIDE), jnp.bfloat16)
    piece = jax.ShapeDtypeStruct((PIECE, PAIR), jnp.bfloat16)
    other = jax.ShapeDtypeStruct((OTHER, PAIR), jnp.bfloat16)
    results = pl.pallas_call(
        grad_kernel,
        out_shape=(flat,) * 4 + (piece,) * PIECES + (other,),
        in_specs=[SMEM] * 4 + [VMEM] * 12 + [ANY] * (PIECES + 1),
        out_specs=(VMEM,) * 4 + (ANY,) * (PIECES + 1),
        scratch_shapes=[
            pltpu.VMEM((SLOTS * BLOCK, PAIR), jnp.bfloat16),
            pltpu.VMEM((TILES, ROWS, HEAD_DIM), jnp.bfloat16),
            pltpu.VMEM((TILES, ROWS, HEAD_DIM), jnp.bfloat16),
            pltpu.VMEM((TILES, 1, ROWS), jnp.float32),
            pltpu.VMEM((TILES, 1, ROWS), jnp.float32),
            pltpu.VMEM((SLOTS * BLOCK, PAIR), jnp.bfloat16),
            pltpu.VMEM((CHUNK, HEAD_DIM), jnp.float32),
            pltpu.VMEM((CHUNK, HEAD_DIM), jnp.float32),
            pltpu.VMEM((TILES, HEAD_DIM, ROWS), jnp.float32),
            pltpu.SemaphoreType.DMA((PIECES + 1,)),
        ],
        compiler_params=pltpu.CompilerParams(vmem_limit_bytes=VMEM_BYTES),
        cost_estimate=pl.CostEstimate(
            flops=16 * work * HEAD_DIM, bytes_accessed=8 << 20, transcendentals=work
        ),
        name="grads",
    )(*tables, *q_rows, *g_rows, *stats, *pieces)
    return results[:4], results[4 : 4 + PIECES], results[4 + PIECES]


def lookup(table, wanted):
    places = jnp.arange(table.shape[0], dtype=jnp.int32)
    return jnp.sum(jnp.where(wanted[:, None] == places[None, :], table[None, :], 0), axis=1)


def plan(order):
    x, y, zh, core, head = (lax.axis_index(name) for name in ("x", "y", "zh", "core", "head"))
    group, half = head // 2, head % 2
    offsets = jnp.array(OFFSETS, jnp.int32)
    slot = jnp.arange(SLOTS, dtype=jnp.int32)
    piece, pair = slot // 4 % 4, slot % 4
    blk = (
        x * 16
        + (zh + pair // 2) % 2 * 8
        + (y + lookup(offsets, piece)) % 4 * 2
        + (core + slot // 16) % 2
    )
    ids = lookup(order, 2 * blk + (group + pair) % 2)
    tile = jnp.arange(TILES, dtype=jnp.int32)
    blk = (x + lookup(offsets, tile // 2)) % 4 * 16 + zh * 8 + y * 2 + core
    query_ids = lookup(order, 2 * blk + (group + tile) % 2)
    before = jnp.sum((ids[None, :] < query_ids[:, None]).astype(jnp.int32), axis=1)
    upto = jnp.sum((ids[None, :] <= query_ids[:, None]).astype(jnp.int32), axis=1)
    rank = jnp.sum((ids[None, :] < ids[:, None]).astype(jnp.int32), axis=1)
    hit = rank[None, :] == slot[:, None]
    slots = jnp.sum(jnp.where(hit, slot[None, :], 0), axis=1)
    sorted_ids = jnp.sum(jnp.where(hit, ids[None, :], 0), axis=1)
    counts = jnp.concatenate([before, upto])
    return slots, sorted_ids, counts, query_ids * BLOCK + half * TOKENS


def choose(first, second, swap):
    return jnp.where(swap, second, first), jnp.where(swap, first, second)


def columns(rows, group):
    width = rows.shape[1] // 2
    return choose(rows[:, :width], rows[:, width:], group == 1)


def body(queries, keys, values, outputs, out_grad, order):
    head = lax.axis_index("head")
    group, half = head // 2, head % 2
    tables = plan(order)

    my_keys, their_keys = columns(keys, group)
    my_values, their_values = columns(values, group)
    mine = jnp.concatenate([my_keys, my_values], axis=1)
    theirs = jnp.concatenate([their_keys, their_values], axis=1)
    near = jnp.stack([mine, swap_group(theirs), swap_z(mine), swap_both(theirs)])
    blocks = jnp.concatenate(choose(near, swap_half(near), half == 1), axis=1)
    my_q, their_q = columns(queries, group)
    my_g, their_g = columns(out_grad, group)
    q_rows = jnp.concatenate([my_q, swap_group(their_q)])
    g_rows = jnp.concatenate([my_g, swap_group(their_g)])
    pieces = gather_direct(blocks.reshape(PIECE, PAIR), "y")
    q_rows = gather_direct(q_rows, "x")
    across = jnp.concatenate(pieces)
    across, g_rows, *q_rows = lax.optimization_barrier((across, g_rows, *q_rows))
    pieces.append(swap_core(across))
    row_delta = jnp.sum(
        (wide(out_grad) * wide(outputs)).reshape(TOKENS, 2 * HEADS_HERE, HEAD_DIM), axis=2
    ).T.reshape(2, 1, ROWS)
    my_delta, their_delta = choose(row_delta[0], row_delta[1], group == 1)
    g_rows = gather_direct(g_rows, "x")
    delta = jnp.stack([my_delta, swap_group(their_delta)])

    stats = call_lse(tables, delta, q_rows, pieces)
    dq_pieces, d_pieces, d_other = call_grads(
        tables, q_rows, g_rows, gather_direct(stats, "x"), pieces
    )

    dq = reduce_direct(dq_pieces, "x")
    query_grad = jnp.concatenate(
        choose(dq[:TOKENS], swap_group(dq[TOKENS:]), group == 1), axis=1
    )

    arrived = swap_core(d_other)
    both = reduce_direct(
        [add(piece, arrived[i * PIECE : (i + 1) * PIECE]) for i, piece in enumerate(d_pieces)], "y"
    )
    both = both.reshape(4, 2, TOKENS, PAIR)
    kept, sent = choose(both[:, 0], both[:, 1], half == 1)
    near = add(kept, swap_half(sent))
    my_part = add(near[0], swap_z(near[2]))
    their_part = add(swap_group(near[1]), swap_both(near[3]))
    first, second = choose(my_part, their_part, group == 1)
    key_grad = jnp.concatenate([first[:, :HEAD_DIM], second[:, :HEAD_DIM]], axis=1)
    value_grad = jnp.concatenate([first[:, HEAD_DIM:], second[:, HEAD_DIM:]], axis=1)
    return query_grad, key_grad, value_grad


def solution(mesh):
    fine = Mesh(
        mesh.devices.reshape(4, 4, 2, 4, 2), ("head", "x", "zh", "y", "core")
    )
    rows = P(("x", "zh", "y", "core", "head"), None)
    return jax.shard_map(
        body,
        mesh=fine,
        in_specs=(rows, rows, rows, rows, rows, P()),
        out_specs=(rows, rows, rows),
        check_vma=False,
    )
```

time: 197 us -> 148 us (0.75); the launches traced: 193 us -> 148 us
  starting transfers between devices: 80.6 us -> 50.4 us
  local copies, waits for them, and re-layouts: 20.2 us -> 0.67 us
  waiting for transfers between devices: 30.4 us -> 35.5 us
    all_to_all x6 -> x0, starting transfers between devices: 32.6 us -> none  [the longest x2 9.09 us: to_heads(): lax.all_to_all(parts, 'head', split_axis=0, concat_axis=0, tiled=True)]
    ppermute x0 -> x12, starting transfers between devices: none -> 26.2 us  [the longest x2 10.7 us: swap_both(): lax.ppermute(value, ('head', 'zh'), [(source, source ^ 5) for source in r...]
    ppermute x32 -> x18, starting transfers between devices: 46.3 us -> 24.2 us  [send(): return lax.ppermute(value, axis, ring_pairs(steps))]
    ppermute x0 -> x12, waiting for transfers between devices: none -> 16.9 us  [the longest x2 10.2 us: swap_half(): lax.ppermute(value, 'head', [(source, source ^ 1) for source in range(4)])]
    all_to_all x6 -> x0, waiting for transfers between devices: 15.5 us -> none  [the longest x1 8.3 us: body(): lax.all_to_all(back, ('zh', 'head'), split_axis=0, concat_axis=0, tiled=T...]
    unnamed x54 -> x11, local copies, waits for them, and re-layouts: 10.1 us -> 0.36 us
    convert_element_type x11 -> x4, other arithmetic: 5.58 us -> 0.58 us  [add(): return total.astype(jnp.bfloat16)]
    slice x18 -> x3, local copies, waits for them, and re-layouts: 5.02 us -> 0.02 us  [the longest x1 0.01 us: body(): dq[TOKENS:]]
  transfers between devices with their start and end apart: 44 -> 32, of which waited for: 14 -> 17; matrix products, arithmetic and copies ran while one was open for 11% -> 4% of each run, Pallas kernels for 10% -> 13%
where the time goes in v2:
time: 148 us
  Pallas kernels  53.4 us (36%)
  starting transfers between devices  50.4 us (34%)
  waiting for transfers between devices  35.5 us (24%)
  other arithmetic  7.12 us (5%)
    pallas_call x1, Pallas kernels, call_grads(): pl.pallas_call(grad_kernel, out_shape=(flat,) * 4 + (piece,) * PIECES + (...  33.6 us
    ppermute x18, starting transfers between devices, send(): return lax.ppermute(value, axis, ring_pairs(steps))  24.2 us
    pallas_call x1, Pallas kernels, call_lse(): pl.pallas_call(lse_kernel, out_shape=jax.ShapeDtypeStruct((2 * TILES + 2,...  19.8 us
    ppermute x18, waiting for transfers between devices, send(): return lax.ppermute(value, axis, ring_pairs(steps))  18.4 us
    ppermute x2, starting transfers between devices, swap_both(): lax.ppermute(value, ('head', 'zh'), [(source, source ^ 5) for source in r...  10.7 us
    ppermute x2, waiting for transfers between devices, swap_half(): lax.ppermute(value, 'head', [(source, source ^ 1) for source in range(4)])  10.2 us
    ppermute x6, starting transfers between devices, swap_group(): lax.ppermute(value, 'head', [(source, source ^ 2) for source in range(4)])  9.42 us
    ppermute x2, starting transfers between devices, swap_half(): lax.ppermute(value, 'head', [(source, source ^ 1) for source in range(4)])  3.5 us
  transfers between devices with their start and end apart: 32, of which 17 were waited for; matrix products, arithmetic and copies ran while one was open for 4% of the time, Pallas kernels for 13%

profile of v2, /device:TPU:32, one launch (start us, length us, event | category | flops | bytes accessed | tf_op | source)
XLA Modules:
  0.0 148.1 jit_solution(2236542677079108234)
XLA Ops:
  0.7 0.8 broadcast_select_fusion.12
  1.5 5.5 %collective-permute-start.2 = (bf16[64,256]{1,0:T(8,128)(2,1)S(1)}, bf16[64,256]{1,0:T(8,128)(2,1)S(1)}, u32[]{:S(2)}, u32[]{:S(2)}) collective-permute-start(bf16[64,256]{1,0:T(8,128)(2,1)S(1)} %pad_maximum_fusion.7), channel_id=1, source_target_pairs={{0,136},{8,128},{64,200},{72,192},{128,8},{136,0},{192,72},{200,64... | collective-permute-start | bytes 98312 | tf_op jit(solution)/shard_map/ppermute | solution.py:59
  7.0 1.5 collective-permute-start
  8.5 1.0 collective-permute-start.1
  9.5 1.0 broadcast_select_fusion.5
  10.5 2.0 %collective-permute-start.8 = (bf16[64,1024]{1,0:T(8,128)(2,1)S(1)}, bf16[64,1024]{1,0:T(8,128)(2,1)S(1)}, u32[]{:S(2)}, u32[]{:S(2)}) collective-permute-start(bf16[64,1024]{1,0:T(8,128)(2,1)S(1)} %get-tuple-element.43), channel_id=1, source_target_pairs={{0,128},{64,192},{128,0},{192,64},{1,129},{65,193},{129,1},{193,65... | collective-permute-start | bytes 393224 | tf_op jit(solution)/shard_map/ppermute | solution.py:47
  12.5 1.1 collective-permute-start.7
  14.4 2.0 %collective-permute-done.1 = bf16[64,256]{1,0:T(8,128)(2,1)S(1)} collective-permute-done((bf16[64,256]{1,0:T(8,128)(2,1)S(1)}, bf16[64,256]{1,0:T(8,128)(2,1)S(1)}, u32[]{:S(2)}, u32[]{:S(2)}) %collective-permute-start.1) | collective-permute-done | bytes 32800 | tf_op jit(solution)/shard_map/ppermute | solution.py:55
  16.5 1.0 collective-permute-start.3
  17.6 7.2 %collective-permute-done.3 = bf16[4,64,256]{2,1,0:T(8,128)(2,1)S(1)} collective-permute-done((bf16[4,64,256]{2,1,0:T(8,128)(2,1)S(1)}, bf16[4,64,256]{2,1,0:T(8,128)(2,1)S(1)}, u32[]{:S(2)}, u32[]{:S(2)}) %collective-permute-start.3) | collective-permute-done | bytes 131104 | tf_op jit(solution)/shard_map/ppermute | solution.py:51
  24.9 3.3 %collective-permute-start.6 = (bf16[512,256]{1,0:T(8,128)(2,1)S(1)}, bf16[512,256]{1,0:T(8,128)(2,1)S(1)}, u32[]{:S(2)}, u32[]{:S(2)}) collective-permute-start(bf16[512,256]{1,0:T(8,128)(2,1)S(1)} %bitcast.44), channel_id=1, source_target_pairs={{0,4},{2,6},{4,0},{6,2},{1,5},{3,7},{5,1},{7,3},{8,12},{10,14},{12... | collective-permute-start | bytes 786440 | tf_op jit(solution)/shard_map/ppermute | solution.py:39
  28.3 1.1 collective-permute-start.5
  29.5 1.0 collective-permute-start.4
  30.7 3.1 %collective-permute-start.11 = (bf16[128,1024]{1,0:T(8,128)(2,1)S(1)}, bf16[128,1024]{1,0:T(8,128)(2,1)S(1)}, u32[]{:S(2)}, u32[]{:S(2)}) collective-permute-start(bf16[128,1024]{1,0:T(8,128)(2,1)S(1)} %pad_maximum_fusion.3.refs_0_), channel_id=1, source_target_pairs={{0,32},{16,48},{32,0},{48,16},{1,33},{17,49},{33,1},{49,17},{2,34}... | collective-permute-start | bytes 786440 | tf_op jit(solution)/shard_map/ppermute | solution.py:39
  33.8 1.1 collective-permute-start.10
  35.0 0.9 collective-permute-start.9
  35.9 0.8 collective-permute-done.5.refs_6_.refs_14_
  36.7 2.0 %collective-permute-start.15 = (f32[1,512]{1,0:T(1,128)S(1)}, f32[1,512]{1,0:T(1,128)S(1)}, u32[]{:S(2)}, u32[]{:S(2)}) collective-permute-start(f32[1,512]{1,0:T(1,128)S(1)} %select_n.297), channel_id=1, source_target_pairs={{0,128},{64,192},{128,0},{192,64},{1,129},{65,193},{129,1},{193,65... | collective-permute-start | bytes 6152 | tf_op jit(solution)/shard_map/ppermute | solution.py:47
  38.7 1.1 pad_maximum_fusion
  39.8 1.8 %collective-permute-done.10.refs_2_ = bf16[128,1024]{1,0:T(8,128)(2,1)S(1)} collective-permute-done((bf16[128,1024]{1,0:T(8,128)(2,1)S(1)}, bf16[128,1024]{1,0:T(8,128)(2,1)S(1)}, u32[]{:S(2)}, u32[]{:S(2)}) %collective-permute-start.10) | collective-permute-done | bytes 262176 | tf_op jit(solution)/shard_map/ppermute | solution.py:39
  41.6 1.0 collective-permute-done.9.refs_1_
  43.3 2.0 %collective-permute-start.14 = (bf16[128,1024]{1,0:T(8,128)(2,1)S(1)}, bf16[128,1024]{1,0:T(8,128)(2,1)S(1)}, u32[]{:S(2)}, u32[]{:S(2)}) collective-permute-start(bf16[128,1024]{1,0:T(8,128)(2,1)S(1)} %pad_maximum_fusion.2.refs_4_), channel_id=1, source_target_pairs={{0,32},{16,48},{32,0},{48,16},{1,33},{17,49},{33,1},{49,17},{2,34}... | collective-permute-start | bytes 786440 | tf_op jit(solution)/shard_map/ppermute | solution.py:39
  45.3 1.2 collective-permute-start.13
  46.5 0.8 collective-permute-start.12
  47.4 19.8 %lse.1.refs_8_ = f32[18,1,512]{2,1,0:T(1,128)S(1)} custom-call(s32[32]{0:T(128)S(1)} %get-tuple-element.36.slot_ref, s32[32]{0:T(128)S(1)} %get-tuple-element.35.ids_ref, s32[16]{0:T(128)S(1)} %pad_add_fusion.count_ref, s32[8]{0:T(128)S(1)} %multiply_add_fusion.start_ref, f32[2,1,512]{2,1,0:T(1,128)S(1)} %pad_maximum_fusion.10.delta_ref, ...), custom_call_target="tpu_custom_call" | custom-call | flops 9126805504 | bytes 4194304 | tf_op jit(solution)/shard_map/lse/pallas_call | solution.py:269
  67.2 1.2 collective-permute-start.19
  68.4 1.7 %collective-permute-start.18 = (f32[18,1,512]{2,1,0:T(1,128)S(1)}, f32[18,1,512]{2,1,0:T(1,128)S(1)}, u32[]{:S(2)}, u32[]{:S(2)}) collective-permute-start(f32[18,1,512]{2,1,0:T(1,128)S(1)} %lse.1.refs_8_), channel_id=1, source_target_pairs={{0,48},{16,0},{32,16},{48,32},{1,49},{17,1},{33,17},{49,33},{2,50}... | collective-permute-start | bytes 110600 | tf_op jit(solution)/shard_map/ppermute | solution.py:39
  70.6 2.2 %collective-permute-done.19.refs_11_ = f32[18,1,512]{2,1,0:T(1,128)S(1)} collective-permute-done((f32[18,1,512]{2,1,0:T(1,128)S(1)}, f32[18,1,512]{2,1,0:T(1,128)S(1)}, u32[]{:S(2)}, u32[]{:S(2)}) %collective-permute-start.19) | collective-permute-done | bytes 36896 | tf_op jit(solution)/shard_map/ppermute | solution.py:39
  72.9 2.4 %collective-permute-done.17.refs_9_ = f32[18,1,512]{2,1,0:T(1,128)S(1)} collective-permute-done((f32[18,1,512]{2,1,0:T(1,128)S(1)}, f32[18,1,512]{2,1,0:T(1,128)S(1)}, u32[]{:S(2)}, u32[]{:S(2)}) %collective-permute-start.17) | collective-permute-done | bytes 36896 | tf_op jit(solution)/shard_map/ppermute | solution.py:39
  75.2 33.6 %grads.1 = (bf16[128,1024]{1,0:T(8,128)(2,1)S(1)}, bf16[128,1024]{1,0:T(8,128)(2,1)S(1)}, bf16[128,1024]{1,0:T(8,128)(2,1)S(1)}, bf16[128,1024]{1,0:T(8,128)(2,1...) custom-call(s32[32]{0:T(128)S(1)} %get-tuple-element.36.slot_ref, ...), custom_call_target="tpu_custom_call" | custom-call | flops 18253611008 | bytes 8388608 | tf_op jit(solution)/shard_map/grads/pallas_call | solution.py:294
  109.4 1.7 %collective-permute-start.21 = (bf16[128,1024]{1,0:T(8,128)(2,1)S(1)}, bf16[128,1024]{1,0:T(8,128)(2,1)S(1)}, u32[]{:S(2)}, u32[]{:S(2)}) collective-permute-start(bf16[128,1024]{1,0:T(8,128)(2,1)S(1)} %get-tuple-element.26), channel_id=1, source_target_pairs={{0,16},{16,32},{32,48},{48,0},{1,17},{17,33},{33,49},{49,1},{2,18}... | collective-permute-start | bytes 786440 | tf_op jit(solution)/shard_map/ppermute | solution.py:39
  112.0 1.6 %collective-permute-start.25 = (bf16[512,256]{1,0:T(8,128)(2,1)S(1)}, bf16[512,256]{1,0:T(8,128)(2,1)S(1)}, u32[]{:S(2)}, u32[]{:S(2)}) collective-permute-start(bf16[512,256]{1,0:T(8,128)(2,1)S(1)} %get-tuple-element.37), channel_id=1, source_target_pairs={{0,6},{2,0},{4,2},{6,4},{1,7},{3,1},{5,3},{7,5},{8,14},{10,8},{12,... | collective-permute-start | bytes 786440 | tf_op jit(solution)/shard_map/ppermute | solution.py:39
  113.6 1.3 collective-permute-start.27
  114.9 3.3 %collective-permute-done.20 = bf16[128,1024]{1,0:T(8,128)(2,1)S(1)} collective-permute-done((bf16[128,1024]{1,0:T(8,128)(2,1)S(1)}, bf16[128,1024]{1,0:T(8,128)(2,1)S(1)}, u32[]{:S(2)}, u32[]{:S(2)}) %collective-permute-start.20) | collective-permute-done | bytes 262176 | tf_op jit(solution)/shard_map/ppermute | solution.py:39
  118.1 0.7 collective-permute-start.26
  118.9 5.7 %collective-permute-done.21 = bf16[128,1024]{1,0:T(8,128)(2,1)S(1)} collective-permute-done((bf16[128,1024]{1,0:T(8,128)(2,1)S(1)}, bf16[128,1024]{1,0:T(8,128)(2,1)S(1)}, u32[]{:S(2)}, u32[]{:S(2)}) %collective-permute-start.21) | collective-permute-done | bytes 262176 | tf_op jit(solution)/shard_map/ppermute | solution.py:39
  124.7 2.8 %collective-permute-start.23 = (bf16[64,1024]{1,0:T(8,128)(2,1)S(1)}, bf16[64,1024]{1,0:T(8,128)(2,1)S(1)}, u32[]{:S(2)}, u32[]{:S(2)}) collective-permute-start(bf16[64,1024]{1,0:T(8,128)(2,1)S(1)} %slice.108), channel_id=1, source_target_pairs={{0,128},{64,192},{128,0},{192,64},{1,129},{65,193},{129,1},{193,65... | collective-permute-start | bytes 393224 | tf_op jit(solution)/shard_map/ppermute | solution.py:47
  127.6 1.2 collective-permute-done.26
  129.0 2.5 %collective-permute-start.28 = (bf16[4,64,256]{2,1,0:T(8,128)(2,1)S(1)}, bf16[4,64,256]{2,1,0:T(8,128)(2,1)S(1)}, u32[]{:S(2)}, u32[]{:S(2)}) collective-permute-start(bf16[4,64,256]{2,1,0:T(8,128)(2,1)S(1)} %select_bitcast_fusion), channel_id=1, source_target_pairs={{0,64},{64,0},{128,192},{192,128},{1,65},{65,1},{129,193},{193,129... | collective-permute-start | bytes 393224 | tf_op jit(solution)/shard_map/ppermute | solution.py:51
  132.1 3.1 %collective-permute-done.28 = bf16[4,64,256]{2,1,0:T(8,128)(2,1)S(1)} collective-permute-done((bf16[4,64,256]{2,1,0:T(8,128)(2,1)S(1)}, bf16[4,64,256]{2,1,0:T(8,128)(2,1)S(1)}, u32[]{:S(2)}, u32[]{:S(2)}) %collective-permute-start.28) | collective-permute-done | bytes 131104 | tf_op jit(solution)/shard_map/ppermute | solution.py:51
  135.2 1.6 %collective-permute-start.31 = (bf16[64,256]{1,0:T(8,128)(2,1)S(1)}, bf16[64,256]{1,0:T(8,128)(2,1)S(1)}, u32[]{:S(2)}, u32[]{:S(2)}) collective-permute-start(bf16[64,256]{1,0:T(8,128)(2,1)S(1)} %get-tuple-element.50), channel_id=1, source_target_pairs={{0,8},{8,0},{1,9},{9,1},{2,10},{10,2},{3,11},{11,3},{4,12},{12,4},... | collective-permute-start | bytes 98312 | tf_op jit(solution)/shard_map/ppermute | solution.py:55
  136.8 5.2 %collective-permute-start.30 = (bf16[64,256]{1,0:T(8,128)(2,1)S(1)}, bf16[64,256]{1,0:T(8,128)(2,1)S(1)}, u32[]{:S(2)}, u32[]{:S(2)}) collective-permute-start(bf16[64,256]{1,0:T(8,128)(2,1)S(1)} %get-tuple-element.51), channel_id=1, source_target_pairs={{0,136},{8,128},{64,200},{72,192},{128,8},{136,0},{192,72},{200,64... | collective-permute-start | bytes 98312 | tf_op jit(solution)/shard_map/ppermute | solution.py:59
  142.0 0.7 pad_maximum_fusion.4
  142.7 0.8 collective-permute-done.31
  143.5 0.7 collective-permute-done.30
  144.3 2.5 %collective-permute-done.29 = bf16[64,256]{1,0:T(8,128)(2,1)S(1)} collective-permute-done((bf16[64,256]{1,0:T(8,128)(2,1)S(1)}, bf16[64,256]{1,0:T(8,128)(2,1)S(1)}, u32[]{:S(2)}, u32[]{:S(2)}) %collective-permute-start.29) | collective-permute-done | bytes 32800 | tf_op jit(solution)/shard_map/ppermute | solution.py:47
  146.8 0.6 pad_maximum_fusion.9
  147.5 0.6 pad_maximum_fusion.8
  (75 shorter events, 5.4 us)
Async XLA Ops:
  0.6 11.8 %copy-start.1 = (bf16[64,2048]{1,0:T(8,128)(2,1)S(1)}, bf16[64,2048]{1,0:T(8,128)(2,1)}, u32[]{:S(2)}) copy-start(bf16[64,2048]{1,0:T(8,128)(2,1)} %param.11) | copy-start | bytes 786436
  0.6 13.0 %copy-start.2 = (bf16[64,2048]{1,0:T(8,128)(2,1)S(1)}, bf16[64,2048]{1,0:T(8,128)(2,1)}, u32[]{:S(2)}) copy-start(bf16[64,2048]{1,0:T(8,128)(2,1)} %param.10) | copy-start | bytes 786436
  1.5 14.9 %collective-permute-start.2 = (bf16[64,256]{1,0:T(8,128)(2,1)S(1)}, bf16[64,256]{1,0:T(8,128)(2,1)S(1)}, u32[]{:S(2)}, u32[]{:S(2)}) collective-permute-start(bf16[64,256]{1,0:T(8,128)(2,1)S(1)} %pad_maximum_fusion.7), channel_id=1, source_target_pairs={{0,136},{8,128},{64,200},{72,192},{128,8},{136,0},{192,72},{200,64... | collective-permute-start | bytes 98312 | tf_op jit(solution)/shard_map/ppermute | solution.py:59
  7.0 9.4 %collective-permute-start = (bf16[64,256]{1,0:T(8,128)(2,1)S(1)}, bf16[64,256]{1,0:T(8,128)(2,1)S(1)}, u32[]{:S(2)}, u32[]{:S(2)}) collective-permute-start(bf16[64,256]{1,0:T(8,128)(2,1)S(1)} %pad_maximum_fusion.7), channel_id=1, source_target_pairs={{0,128},{64,192},{128,0},{192,64},{1,129},{65,193},{129,1},{193,65... | collective-permute-start | bytes 98312 | tf_op jit(solution)/shard_map/ppermute | solution.py:47
  8.5 8.0 %collective-permute-start.1 = (bf16[64,256]{1,0:T(8,128)(2,1)S(1)}, bf16[64,256]{1,0:T(8,128)(2,1)S(1)}, u32[]{:S(2)}, u32[]{:S(2)}) collective-permute-start(bf16[64,256]{1,0:T(8,128)(2,1)S(1)} %get-tuple-element.60), channel_id=1, source_target_pairs={{0,8},{8,0},{1,9},{9,1},{2,10},{10,2},{3,11},{11,3},{4,12},{12,4},... | collective-permute-start | bytes 98312 | tf_op jit(solution)/shard_map/ppermute | solution.py:55
  10.5 20.2 %collective-permute-start.8 = (bf16[64,1024]{1,0:T(8,128)(2,1)S(1)}, bf16[64,1024]{1,0:T(8,128)(2,1)S(1)}, u32[]{:S(2)}, u32[]{:S(2)}) collective-permute-start(bf16[64,1024]{1,0:T(8,128)(2,1)S(1)} %get-tuple-element.43), channel_id=1, source_target_pairs={{0,128},{64,192},{128,0},{192,64},{1,129},{65,193},{129,1},{193,65... | collective-permute-start | bytes 393224 | tf_op jit(solution)/shard_map/ppermute | solution.py:47
  12.5 21.4 %collective-permute-start.7 = (bf16[64,1024]{1,0:T(8,128)(2,1)S(1)}, bf16[64,1024]{1,0:T(8,128)(2,1)S(1)}, u32[]{:S(2)}, u32[]{:S(2)}) collective-permute-start(bf16[64,1024]{1,0:T(8,128)(2,1)S(1)} %get-tuple-element.45), channel_id=1, source_target_pairs={{0,128},{64,192},{128,0},{192,64},{1,129},{65,193},{129,1},{193,65... | collective-permute-start | bytes 393224 | tf_op jit(solution)/shard_map/ppermute | solution.py:47
  13.7 0.7 copy-start.4
  13.7 3.8 %copy-start.3 = (s32[128]{0:T(128)S(1)}, s32[128]{0:T(128)}, u32[]{:S(2)}) copy-start(s32[128]{0:T(128)} %param.12) | copy-start | bytes 1540
  16.5 8.3 %collective-permute-start.3 = (bf16[4,64,256]{2,1,0:T(8,128)(2,1)S(1)}, bf16[4,64,256]{2,1,0:T(8,128)(2,1)S(1)}, u32[]{:S(2)}, u32[]{:S(2)}) collective-permute-start(bf16[4,64,256]{2,1,0:T(8,128)(2,1)S(1)} %pad_maximum_fusion.5), channel_id=1, source_target_pairs={{0,64},{64,0},{128,192},{192,128},{1,65},{65,1},{129,193},{193,129... | collective-permute-start | bytes 393224 | tf_op jit(solution)/shard_map/ppermute | solution.py:51
  24.9 10.1 %collective-permute-start.6 = (bf16[512,256]{1,0:T(8,128)(2,1)S(1)}, bf16[512,256]{1,0:T(8,128)(2,1)S(1)}, u32[]{:S(2)}, u32[]{:S(2)}) collective-permute-start(bf16[512,256]{1,0:T(8,128)(2,1)S(1)} %bitcast.44), channel_id=1, source_target_pairs={{0,4},{2,6},{4,0},{6,2},{1,5},{3,7},{5,1},{7,3},{8,12},{10,14},{12... | collective-permute-start | bytes 786440 | tf_op jit(solution)/shard_map/ppermute | solution.py:39
  28.3 8.4 %collective-permute-start.5 = (bf16[512,256]{1,0:T(8,128)(2,1)S(1)}, bf16[512,256]{1,0:T(8,128)(2,1)S(1)}, u32[]{:S(2)}, u32[]{:S(2)}) collective-permute-start(bf16[512,256]{1,0:T(8,128)(2,1)S(1)} %bitcast.45), channel_id=1, source_target_pairs={{0,6},{2,0},{4,2},{6,4},{1,7},{3,1},{5,3},{7,5},{8,14},{10,8},{12,... | collective-permute-start | bytes 786440 | tf_op jit(solution)/shard_map/ppermute | solution.py:39
  29.5 9.3 %collective-permute-start.4 = (bf16[512,256]{1,0:T(8,128)(2,1)S(1)}, bf16[512,256]{1,0:T(8,128)(2,1)S(1)}, u32[]{:S(2)}, u32[]{:S(2)}) collective-permute-start(bf16[512,256]{1,0:T(8,128)(2,1)S(1)} %bitcast.46), channel_id=1, source_target_pairs={{0,2},{2,4},{4,6},{6,0},{1,3},{3,5},{5,7},{7,1},{8,10},{10,12},{12... | collective-permute-start | bytes 786440 | tf_op jit(solution)/shard_map/ppermute | solution.py:39
  30.7 9.1 %collective-permute-start.11 = (bf16[128,1024]{1,0:T(8,128)(2,1)S(1)}, bf16[128,1024]{1,0:T(8,128)(2,1)S(1)}, u32[]{:S(2)}, u32[]{:S(2)}) collective-permute-start(bf16[128,1024]{1,0:T(8,128)(2,1)S(1)} %pad_maximum_fusion.3.refs_0_), channel_id=1, source_target_pairs={{0,32},{16,48},{32,0},{48,16},{1,33},{17,49},{33,1},{49,17},{2,34}... | collective-permute-start | bytes 786440 | tf_op jit(solution)/shard_map/ppermute | solution.py:39
  33.8 7.8 %collective-permute-start.10 = (bf16[128,1024]{1,0:T(8,128)(2,1)S(1)}, bf16[128,1024]{1,0:T(8,128)(2,1)S(1)}, u32[]{:S(2)}, u32[]{:S(2)}) collective-permute-start(bf16[128,1024]{1,0:T(8,128)(2,1)S(1)} %pad_maximum_fusion.3.refs_0_), channel_id=1, source_target_pairs={{0,48},{16,0},{32,16},{48,32},{1,49},{17,1},{33,17},{49,33},{2,50}... | collective-permute-start | bytes 786440 | tf_op jit(solution)/shard_map/ppermute | solution.py:39
  35.0 7.6 %collective-permute-start.9 = (bf16[128,1024]{1,0:T(8,128)(2,1)S(1)}, bf16[128,1024]{1,0:T(8,128)(2,1)S(1)}, u32[]{:S(2)}, u32[]{:S(2)}) collective-permute-start(bf16[128,1024]{1,0:T(8,128)(2,1)S(1)} %pad_maximum_fusion.3.refs_0_), channel_id=1, source_target_pairs={{0,16},{16,32},{32,48},{48,0},{1,17},{17,33},{33,49},{49,1},{2,18}... | collective-permute-start | bytes 786440 | tf_op jit(solution)/shard_map/ppermute | solution.py:39
  36.7 6.6 %collective-permute-start.15 = (f32[1,512]{1,0:T(1,128)S(1)}, f32[1,512]{1,0:T(1,128)S(1)}, u32[]{:S(2)}, u32[]{:S(2)}) collective-permute-start(f32[1,512]{1,0:T(1,128)S(1)} %select_n.297), channel_id=1, source_target_pairs={{0,128},{64,192},{128,0},{192,64},{1,129},{65,193},{129,1},{193,65... | collective-permute-start | bytes 6152 | tf_op jit(solution)/shard_map/ppermute | solution.py:47
  42.6 4.8 %collective-permute-start.16 = (bf16[2048,256]{1,0:T(8,128)(2,1)}, bf16[2048,256]{1,0:T(8,128)(2,1)S(1)}, u32[]{:S(2)}, u32[]{:S(2)}) collective-permute-start(bf16[2048,256]{1,0:T(8,128)(2,1)} %pad_maximum_fusion), channel_id=1, source_target_pairs={{0,1},{1,0},{2,3},{3,2},{4,5},{5,4},{6,7},{7,6},{8,9},{9,8},{10,11... | collective-permute-start | bytes 3145736 | tf_op jit(solution)/shard_map/ppermute | solution.py:43
  43.3 26.8 %collective-permute-start.14 = (bf16[128,1024]{1,0:T(8,128)(2,1)S(1)}, bf16[128,1024]{1,0:T(8,128)(2,1)S(1)}, u32[]{:S(2)}, u32[]{:S(2)}) collective-permute-start(bf16[128,1024]{1,0:T(8,128)(2,1)S(1)} %pad_maximum_fusion.2.refs_4_), channel_id=1, source_target_pairs={{0,32},{16,48},{32,0},{48,16},{1,33},{17,49},{33,1},{49,17},{2,34}... | collective-permute-start | bytes 786440 | tf_op jit(solution)/shard_map/ppermute | solution.py:39
  45.3 25.2 %collective-permute-start.13 = (bf16[128,1024]{1,0:T(8,128)(2,1)S(1)}, bf16[128,1024]{1,0:T(8,128)(2,1)S(1)}, u32[]{:S(2)}, u32[]{:S(2)}) collective-permute-start(bf16[128,1024]{1,0:T(8,128)(2,1)S(1)} %pad_maximum_fusion.2.refs_4_), channel_id=1, source_target_pairs={{0,48},{16,0},{32,16},{48,32},{1,49},{17,1},{33,17},{49,33},{2,50}... | collective-permute-start | bytes 786440 | tf_op jit(solution)/shard_map/ppermute | solution.py:39
  46.5 24.0 %collective-permute-start.12 = (bf16[128,1024]{1,0:T(8,128)(2,1)S(1)}, bf16[128,1024]{1,0:T(8,128)(2,1)S(1)}, u32[]{:S(2)}, u32[]{:S(2)}) collective-permute-start(bf16[128,1024]{1,0:T(8,128)(2,1)S(1)} %pad_maximum_fusion.2.refs_4_), channel_id=1, source_target_pairs={{0,16},{16,32},{32,48},{48,0},{1,17},{17,33},{33,49},{49,1},{2,18}... | collective-permute-start | bytes 786440 | tf_op jit(solution)/shard_map/ppermute | solution.py:39
  47.4 19.8 %copy-start = (bf16[2048,256]{1,0:T(8,128)(2,1)}, bf16[2048,256]{1,0:T(8,128)(2,1)S(1)}, u32[]{:S(2)}) copy-start(bf16[2048,256]{1,0:T(8,128)(2,1)S(1)} %collective-permute-done.16.refs_8_.refs_16_) | copy-start | bytes 3145732
  67.2 5.5 %collective-permute-start.19 = (f32[18,1,512]{2,1,0:T(1,128)S(1)}, f32[18,1,512]{2,1,0:T(1,128)S(1)}, u32[]{:S(2)}, u32[]{:S(2)}) collective-permute-start(f32[18,1,512]{2,1,0:T(1,128)S(1)} %lse.1.refs_8_), channel_id=1, source_target_pairs={{0,32},{16,48},{32,0},{48,16},{1,33},{17,49},{33,1},{49,17},{2,34}... | collective-permute-start | bytes 110600 | tf_op jit(solution)/shard_map/ppermute | solution.py:39
  68.4 4.5 %collective-permute-start.18 = (f32[18,1,512]{2,1,0:T(1,128)S(1)}, f32[18,1,512]{2,1,0:T(1,128)S(1)}, u32[]{:S(2)}, u32[]{:S(2)}) collective-permute-start(f32[18,1,512]{2,1,0:T(1,128)S(1)} %lse.1.refs_8_), channel_id=1, source_target_pairs={{0,48},{16,0},{32,16},{48,32},{1,49},{17,1},{33,17},{49,33},{2,50}... | collective-permute-start | bytes 110600 | tf_op jit(solution)/shard_map/ppermute | solution.py:39
  70.1 5.2 %collective-permute-start.17 = (f32[18,1,512]{2,1,0:T(1,128)S(1)}, f32[18,1,512]{2,1,0:T(1,128)S(1)}, u32[]{:S(2)}, u32[]{:S(2)}) collective-permute-start(f32[18,1,512]{2,1,0:T(1,128)S(1)} %lse.1.refs_8_), channel_id=1, source_target_pairs={{0,16},{16,32},{32,48},{48,0},{1,17},{17,33},{33,49},{49,1},{2,18}... | collective-permute-start | bytes 110600 | tf_op jit(solution)/shard_map/ppermute | solution.py:39
  108.9 3.0 %collective-permute-start.24 = (bf16[2048,256]{1,0:T(8,128)(2,1)}, bf16[2048,256]{1,0:T(8,128)(2,1)S(1)}, u32[]{:S(2)}, u32[]{:S(2)}) collective-permute-start(bf16[2048,256]{1,0:T(8,128)(2,1)} %get-tuple-element.29), channel_id=1, source_target_pairs={{0,1},{1,0},{2,3},{3,2},{4,5},{5,4},{6,7},{7,6},{8,9},{9,8},{10,11... | collective-permute-start | bytes 3145736 | tf_op jit(solution)/shard_map/ppermute | solution.py:43
  109.0 9.2 %collective-permute-start.20 = (bf16[128,1024]{1,0:T(8,128)(2,1)S(1)}, bf16[128,1024]{1,0:T(8,128)(2,1)S(1)}, u32[]{:S(2)}, u32[]{:S(2)}) collective-permute-start(bf16[128,1024]{1,0:T(8,128)(2,1)S(1)} %get-tuple-element.25), channel_id=1, source_target_pairs={{0,48},{16,0},{32,16},{48,32},{1,49},{17,1},{33,17},{49,33},{2,50}... | collective-permute-start | bytes 786440 | tf_op jit(solution)/shard_map/ppermute | solution.py:39
  109.4 15.2 %collective-permute-start.21 = (bf16[128,1024]{1,0:T(8,128)(2,1)S(1)}, bf16[128,1024]{1,0:T(8,128)(2,1)S(1)}, u32[]{:S(2)}, u32[]{:S(2)}) collective-permute-start(bf16[128,1024]{1,0:T(8,128)(2,1)S(1)} %get-tuple-element.26), channel_id=1, source_target_pairs={{0,16},{16,32},{32,48},{48,0},{1,17},{17,33},{33,49},{49,1},{2,18}... | collective-permute-start | bytes 786440 | tf_op jit(solution)/shard_map/ppermute | solution.py:39
  111.1 13.5 %collective-permute-start.22 = (bf16[128,1024]{1,0:T(8,128)(2,1)S(1)}, bf16[128,1024]{1,0:T(8,128)(2,1)S(1)}, u32[]{:S(2)}, u32[]{:S(2)}) collective-permute-start(bf16[128,1024]{1,0:T(8,128)(2,1)S(1)} %get-tuple-element.27), channel_id=1, source_target_pairs={{0,32},{16,48},{32,0},{48,16},{1,33},{17,49},{33,1},{49,17},{2,34}... | collective-permute-start | bytes 786440 | tf_op jit(solution)/shard_map/ppermute | solution.py:39
  112.0 15.6 %collective-permute-start.25 = (bf16[512,256]{1,0:T(8,128)(2,1)S(1)}, bf16[512,256]{1,0:T(8,128)(2,1)S(1)}, u32[]{:S(2)}, u32[]{:S(2)}) collective-permute-start(bf16[512,256]{1,0:T(8,128)(2,1)S(1)} %get-tuple-element.37), channel_id=1, source_target_pairs={{0,6},{2,0},{4,2},{6,4},{1,7},{3,1},{5,3},{7,5},{8,14},{10,8},{12,... | collective-permute-start | bytes 786440 | tf_op jit(solution)/shard_map/ppermute | solution.py:39
  113.6 14.0 %collective-permute-start.27 = (bf16[512,256]{1,0:T(8,128)(2,1)S(1)}, bf16[512,256]{1,0:T(8,128)(2,1)S(1)}, u32[]{:S(2)}, u32[]{:S(2)}) collective-permute-start(bf16[512,256]{1,0:T(8,128)(2,1)S(1)} %get-tuple-element.38), channel_id=1, source_target_pairs={{0,4},{2,6},{4,0},{6,2},{1,5},{3,7},{5,1},{7,3},{8,12},{10,14},{12... | collective-permute-start | bytes 786440 | tf_op jit(solution)/shard_map/ppermute | solution.py:39
  118.1 10.6 %collective-permute-start.26 = (bf16[512,256]{1,0:T(8,128)(2,1)S(1)}, bf16[512,256]{1,0:T(8,128)(2,1)S(1)}, u32[]{:S(2)}, u32[]{:S(2)}) collective-permute-start(bf16[512,256]{1,0:T(8,128)(2,1)S(1)} %get-tuple-element.39), channel_id=1, source_target_pairs={{0,2},{2,4},{4,6},{6,0},{1,3},{3,5},{5,7},{7,1},{8,10},{10,12},{12... | collective-permute-start | bytes 786440 | tf_op jit(solution)/shard_map/ppermute | solution.py:39
  124.7 7.3 %collective-permute-start.23 = (bf16[64,1024]{1,0:T(8,128)(2,1)S(1)}, bf16[64,1024]{1,0:T(8,128)(2,1)S(1)}, u32[]{:S(2)}, u32[]{:S(2)}) collective-permute-start(bf16[64,1024]{1,0:T(8,128)(2,1)S(1)} %slice.108), channel_id=1, source_target_pairs={{0,128},{64,192},{128,0},{192,64},{1,129},{65,193},{129,1},{193,65... | collective-permute-start | bytes 393224 | tf_op jit(solution)/shard_map/ppermute | solution.py:47
  129.0 6.2 %collective-permute-start.28 = (bf16[4,64,256]{2,1,0:T(8,128)(2,1)S(1)}, bf16[4,64,256]{2,1,0:T(8,128)(2,1)S(1)}, u32[]{:S(2)}, u32[]{:S(2)}) collective-permute-start(bf16[4,64,256]{2,1,0:T(8,128)(2,1)S(1)} %select_bitcast_fusion), channel_id=1, source_target_pairs={{0,64},{64,0},{128,192},{192,128},{1,65},{65,1},{129,193},{193,129... | collective-permute-start | bytes 393224 | tf_op jit(solution)/shard_map/ppermute | solution.py:51
  135.2 8.3 %collective-permute-start.31 = (bf16[64,256]{1,0:T(8,128)(2,1)S(1)}, bf16[64,256]{1,0:T(8,128)(2,1)S(1)}, u32[]{:S(2)}, u32[]{:S(2)}) collective-permute-start(bf16[64,256]{1,0:T(8,128)(2,1)S(1)} %get-tuple-element.50), channel_id=1, source_target_pairs={{0,8},{8,0},{1,9},{9,1},{2,10},{10,2},{3,11},{11,3},{4,12},{12,4},... | collective-permute-start | bytes 98312 | tf_op jit(solution)/shard_map/ppermute | solution.py:55
  136.8 7.5 %collective-permute-start.30 = (bf16[64,256]{1,0:T(8,128)(2,1)S(1)}, bf16[64,256]{1,0:T(8,128)(2,1)S(1)}, u32[]{:S(2)}, u32[]{:S(2)}) collective-permute-start(bf16[64,256]{1,0:T(8,128)(2,1)S(1)} %get-tuple-element.51), channel_id=1, source_target_pairs={{0,136},{8,128},{64,200},{72,192},{128,8},{136,0},{192,72},{200,64... | collective-permute-start | bytes 98312 | tf_op jit(solution)/shard_map/ppermute | solution.py:59
  142.0 4.8 %collective-permute-start.29 = (bf16[64,256]{1,0:T(8,128)(2,1)S(1)}, bf16[64,256]{1,0:T(8,128)(2,1)S(1)}, u32[]{:S(2)}, u32[]{:S(2)}) collective-permute-start(bf16[64,256]{1,0:T(8,128)(2,1)S(1)} %get-tuple-element.52), channel_id=1, source_target_pairs={{0,128},{64,192},{128,0},{192,64},{1,129},{65,193},{129,1},{193,65... | collective-permute-start | bytes 98312 | tf_op jit(solution)/shard_map/ppermute | solution.py:47

commit v3 on v2

--- a/solution.py
+++ b/solution.py
@@ -19,6 +19,8 @@
 SLOTS = 32
 TILES = 8
 CHUNKS = SLOTS // CHUNK_BLOCKS
+LOW_CHUNKS = CHUNKS // 2
+UNITS = LOW_CHUNKS + 1
 PIECE = 512
 PIECES = 4
 OTHER = PIECES * PIECE
@@ -92,11 +94,12 @@
 
 
 def spread_heads(sources, target):
-    for tile in range(TILES):
-        for head in range(HEADS_HERE):
-            target[tile, pl.ds(head * TOKENS, TOKENS), :] = sources[tile // 2][
-                pl.ds(tile % 2 * TOKENS, TOKENS), pl.ds(head * HEAD_DIM, HEAD_DIM)
-            ]
+    for place, source in enumerate(sources):
+        for kind in range(2):
+            for head in range(HEADS_HERE):
+                target[4 * kind + place, pl.ds(head * TOKENS, TOKENS), :] = source[
+                    pl.ds(kind * TOKENS, TOKENS), pl.ds(head * HEAD_DIM, HEAD_DIM)
+                ]
 
 
 def load_chunk(source, slot_ref, chunk, column):
@@ -134,20 +137,23 @@
     return jnp.concatenate(parts, axis=0)
 
 
-def for_tiles(chunk, query, count_ref, tile):
-    count = count_ref[query]
-    full = count // CHUNK_BLOCKS
-
-    @pl.when(chunk < full)
-    def _():
-        tile(chunk, query, False)
-
-    @pl.when((chunk >= full) & (chunk * CHUNK_BLOCKS < count_ref[query + TILES]))
-    def _():
-        tile(chunk, query, True)
-
-
-def lse_kernel(slot_ref, ids_ref, count_ref, start_ref, delta_ref, *refs):
+def for_steps(unit_refs, step):
+    tile_ref, chunk_ref, start_ref = unit_refs
+
+    def high(chunk, carry):
+        step([(4 + place, chunk, None) for place in range(4)])
+        return carry
+
+    def rest(index, carry):
+        units = [4 * index + place for place in range(4)]
+        step([(tile_ref[unit], chunk_ref[unit], start_ref[unit]) for unit in units])
+        return carry
+
+    lax.fori_loop(0, LOW_CHUNKS, high, 0)
+    lax.fori_loop(0, UNITS, rest, 0)
+
+
+def lse_kernel(slot_ref, ids_ref, tile_ref, chunk_ref, start_ref, delta_ref, *refs):
     rows, pieces, other = refs[:4], refs[4 : 4 + PIECES], refs[4 + PIECES]
     stat_ref, gathered, queries, max_acc, sum_acc, sems = refs[5 + PIECES :]
     copies = kv_copies(pieces, other, gathered, sems, False)
@@ -157,24 +163,23 @@
     for copy in copies:
         copy.wait()
 
-    def tile(chunk, query, use_mask):
-        scores = dot_rows(load_chunk(gathered, slot_ref, chunk, 0), queries[query])
-        if use_mask:
-            scores = masked(scores, NEG, ids_ref, chunk, start_ref[query])
-        grouped = scores.reshape(CHUNK // 8, 8, ROWS)
-        old_max = max_acc[query]
-        new_max = jnp.maximum(old_max, jnp.max(grouped, axis=0))
-        weights = jnp.exp2((grouped - new_max[None]) * SCALE2)
-        sum_acc[query] = sum_acc[query] * jnp.exp2((old_max - new_max) * SCALE2) + jnp.sum(
-            weights, axis=0
-        )
-        max_acc[query] = new_max
-
-    def step(index, carry):
-        for_tiles(index // TILES, index % TILES, count_ref, tile)
-        return carry
-
-    lax.fori_loop(0, CHUNKS * TILES, step, 0)
+    def step(units):
+        scores = []
+        for query, chunk, start in units:
+            part = dot_rows(load_chunk(gathered, slot_ref, chunk, 0), queries[query])
+            if start is not None:
+                part = masked(part, NEG, ids_ref, chunk, start)
+            scores.append(part.reshape(CHUNK // 8, 8, ROWS))
+        for (query, _, _), part in zip(units, scores):
+            old_max = max_acc[query]
+            new_max = jnp.maximum(old_max, jnp.max(part, axis=0))
+            weights = jnp.exp2((part - new_max[None]) * SCALE2)
+            sum_acc[query] = sum_acc[query] * jnp.exp2((old_max - new_max) * SCALE2) + jnp.sum(
+                weights, axis=0
+            )
+            max_acc[query] = new_max
+
+    for_steps((tile_ref, chunk_ref, start_ref), step)
     for query in range(2):
         stat_ref[2 * TILES + query] = delta_ref[query]
     for query in range(TILES):
@@ -186,7 +191,7 @@
         )
 
 
-def grad_kernel(slot_ref, ids_ref, count_ref, start_ref, *refs):
+def grad_kernel(slot_ref, ids_ref, tile_ref, chunk_ref, start_ref, *refs):
     q_rows, g_rows, stats = refs[:4], refs[4:8], refs[8:12]
     pieces, other = refs[12 : 12 + PIECES], refs[12 + PIECES]
     refs = refs[13 + PIECES :]
@@ -196,62 +201,96 @@
     spread_heads(q_rows, queries)
     spread_heads(g_rows, grads)
     for query in range(TILES):
-        offset = OFFSETS[query // 2]
-        places = [2 * PIECE_AT[(offset - source) % 4] + query % 2 for source in OFFSETS]
+        offset, kind = OFFSETS[query % 4], query // 4
+        places = [4 * kind + PIECE_AT[(offset - source) % 4] for source in OFFSETS]
         tops = [stat[place] for stat, place in zip(stats, places)]
         top = jnp.maximum(jnp.maximum(tops[0], tops[1]), jnp.maximum(tops[2], tops[3]))
         total = jnp.zeros_like(top)
         for stat, place, part in zip(stats, places, tops):
             total += stat[TILES + place] * jnp.exp2((part - top) * SCALE2)
         lse[query] = top * SCALE2 + jnp.log2(total)
-        delta[query] = stats[query // 2][2 * TILES + query % 2]
+        delta[query] = stats[query % 4][2 * TILES + kind]
     dq_acc[...] = jnp.zeros(dq_acc.shape, jnp.float32)
     for copy in copies:
         copy.wait()
 
-    def tile(chunk, query, use_mask):
+    for chunk in range(LOW_CHUNKS, CHUNKS):
+        dk_acc[chunk] = jnp.zeros((CHUNK, HEAD_DIM), jnp.float32)
+        dv_acc[chunk] = jnp.zeros((CHUNK, HEAD_DIM), jnp.float32)
+
+    def high_step(chunk):
         key_part = load_chunk(gathered, slot_ref, chunk, 0)
         value_part = load_chunk(gathered, slot_ref, chunk, HEAD_DIM)
-        query_part = queries[query]
-        grad_part = grads[query]
+        query_part = queries[4:].reshape(4 * ROWS, HEAD_DIM)
+        grad_part = grads[4:].reshape(4 * ROWS, HEAD_DIM)
         scores = dot_rows(key_part, query_part)
-        weights = jnp.exp2(scores * SCALE2 - lse[query])
-        if use_mask:
-            weights = masked(weights, 0.0, ids_ref, chunk, start_ref[query])
-        dv_acc[...] += jnp.dot(
+        dprob = dot_rows(value_part, grad_part)
+        row_lse = jnp.concatenate([lse[4 + place] for place in range(4)], axis=1)
+        row_delta = jnp.concatenate([delta[4 + place] for place in range(4)], axis=1)
+        weights = jnp.exp2(scores * SCALE2 - row_lse)
+        score_grad = (weights * (dprob - row_delta)).astype(jnp.bfloat16)
+        dk_acc[chunk] = jnp.dot(score_grad, query_part, preferred_element_type=jnp.float32)
+        dv_acc[chunk] = jnp.dot(
             weights.astype(jnp.bfloat16), grad_part, preferred_element_type=jnp.float32
         )
-        dprob = dot_rows(value_part, grad_part)
-        score_grad = (weights * (dprob - delta[query])).astype(jnp.bfloat16)
-        dk_acc[...] += jnp.dot(score_grad, query_part, preferred_element_type=jnp.float32)
-        dq_acc[query] += dot_columns(key_part, score_grad)
-
-    def chunk_step(chunk, carry):
-        dk_acc[...] = jnp.zeros(dk_acc.shape, jnp.float32)
-        dv_acc[...] = jnp.zeros(dv_acc.shape, jnp.float32)
-
-        def query_step(query, inner):
-            for_tiles(chunk, query, count_ref, tile)
-            return inner
-
-        lax.fori_loop(0, TILES, query_step, 0)
+        dq = dot_columns(key_part, score_grad)
+        for place in range(4):
+            dq_acc[4 + place] += dq[:, place * ROWS : (place + 1) * ROWS]
+
+    def products(query, chunk):
+        key_part = load_chunk(gathered, slot_ref, chunk, 0)
+        value_part = load_chunk(gathered, slot_ref, chunk, HEAD_DIM)
+        return key_part, dot_rows(key_part, queries[query]), dot_rows(value_part, grads[query])
+
+    def step(units):
+        if units[0][2] is None:
+            high_step(units[0][1])
+            return
+        parts = []
+        ahead = products(*units[0][:2])
+        for index, (query, chunk, start) in enumerate(units):
+            key_part, scores, dprob = ahead
+            if index + 1 < len(units):
+                ahead = products(*units[index + 1][:2])
+            weights = jnp.exp2(scores * SCALE2 - lse[query])
+            weights = masked(weights, 0.0, ids_ref, chunk, start)
+            score_grad = (weights * (dprob - delta[query])).astype(jnp.bfloat16)
+            parts.append((
+                dot_columns(key_part, score_grad),
+                jnp.dot(score_grad, queries[query], preferred_element_type=jnp.float32),
+                jnp.dot(
+                    weights.astype(jnp.bfloat16),
+                    grads[query],
+                    preferred_element_type=jnp.float32,
+                ),
+            ))
+        for (query, chunk, _), part in zip(units, parts):
+            dq_acc[query] += part[0]
+            dk_acc[chunk] += part[1]
+            dv_acc[chunk] += part[2]
+
+    for_steps((tile_ref, chunk_ref, start_ref), step)
+
+    def place_chunk(chunk, carry):
         for j in range(CHUNK_BLOCKS):
             place = chunk * CHUNK_BLOCKS + j
             rows = pl.ds(j * BLOCK, BLOCK)
             target = pl.ds(pl.multiple_of(slot_ref[place] * BLOCK, BLOCK), BLOCK)
-            d_all[target, pl.ds(0, HEAD_DIM)] = (dk_acc[rows, :] * FACTOR).astype(jnp.bfloat16)
-            d_all[target, pl.ds(HEAD_DIM, HEAD_DIM)] = dv_acc[rows, :].astype(jnp.bfloat16)
+            d_all[target, pl.ds(0, HEAD_DIM)] = (dk_acc[chunk, rows, :] * FACTOR).astype(
+                jnp.bfloat16
+            )
+            d_all[target, pl.ds(HEAD_DIM, HEAD_DIM)] = dv_acc[chunk, rows, :].astype(jnp.bfloat16)
         return carry
 
-    lax.fori_loop(0, CHUNKS, chunk_step, 0)
+    lax.fori_loop(0, CHUNKS, place_chunk, 0)
     outs = kv_copies(d_pieces, d_other, d_all, sems, True)
     for query in range(TILES):
-        target = dq_pieces[query // 2]
+        target = dq_pieces[query % 4]
         for head in range(0, HEADS_HERE, 2):
             pair = (dq_acc[query, :, pl.ds(head * TOKENS, 2 * TOKENS)] * FACTOR).T
             for half in range(2):
                 target[
-                    pl.ds((query % 2) * TOKENS, TOKENS),
+                    pl.ds(query // 4 * TOKENS, TOKENS),
                     pl.ds((head + half) * HEAD_DIM, HEAD_DIM),
                 ] = pair[half * TOKENS : (half + 1) * TOKENS].astype(target.dtype)
     for copy in outs:
@@ -269,7 +308,7 @@
     return pl.pallas_call(
         lse_kernel,
         out_shape=jax.ShapeDtypeStruct((2 * TILES + 2, 1, ROWS), jnp.float32),
-        in_specs=[SMEM] * 4 + [VMEM] * 5 + [ANY] * (PIECES + 1),
+        in_specs=[SMEM] * 5 + [VMEM] * 5 + [ANY] * (PIECES + 1),
         out_specs=VMEM,
         scratch_shapes=[
             pltpu.VMEM((SLOTS * BLOCK, PAIR), jnp.bfloat16),
@@ -294,7 +333,7 @@
     results = pl.pallas_call(
         grad_kernel,
         out_shape=(flat,) * 4 + (piece,) * PIECES + (other,),
-        in_specs=[SMEM] * 4 + [VMEM] * 12 + [ANY] * (PIECES + 1),
+        in_specs=[SMEM] * 5 + [VMEM] * 12 + [ANY] * (PIECES + 1),
         out_specs=(VMEM,) * 4 + (ANY,) * (PIECES + 1),
         scratch_shapes=[
             pltpu.VMEM((SLOTS * BLOCK, PAIR), jnp.bfloat16),
@@ -303,8 +342,8 @@
             pltpu.VMEM((TILES, 1, ROWS), jnp.float32),
             pltpu.VMEM((TILES, 1, ROWS), jnp.float32),
             pltpu.VMEM((SLOTS * BLOCK, PAIR), jnp.bfloat16),
-            pltpu.VMEM((CHUNK, HEAD_DIM), jnp.float32),
-            pltpu.VMEM((CHUNK, HEAD_DIM), jnp.float32),
+            pltpu.VMEM((CHUNKS, CHUNK, HEAD_DIM), jnp.float32),
+            pltpu.VMEM((CHUNKS, CHUNK, HEAD_DIM), jnp.float32),
             pltpu.VMEM((TILES, HEAD_DIM, ROWS), jnp.float32),
             pltpu.SemaphoreType.DMA((PIECES + 1,)),
         ],
@@ -336,16 +375,26 @@
     )
     ids = lookup(order, 2 * blk + (group + pair) % 2)
     tile = jnp.arange(TILES, dtype=jnp.int32)
-    blk = (x + lookup(offsets, tile // 2)) % 4 * 16 + zh * 8 + y * 2 + core
-    query_ids = lookup(order, 2 * blk + (group + tile) % 2)
-    before = jnp.sum((ids[None, :] < query_ids[:, None]).astype(jnp.int32), axis=1)
-    upto = jnp.sum((ids[None, :] <= query_ids[:, None]).astype(jnp.int32), axis=1)
+    blk = (x + lookup(offsets, tile % 4)) % 4 * 16 + zh * 8 + y * 2 + core
+    query_ids = lookup(order, 2 * blk + tile // 4)
+    seen = jnp.sum((ids[None, :] <= query_ids[:, None]).astype(jnp.int32), axis=1)
     rank = jnp.sum((ids[None, :] < ids[:, None]).astype(jnp.int32), axis=1)
     hit = rank[None, :] == slot[:, None]
     slots = jnp.sum(jnp.where(hit, slot[None, :], 0), axis=1)
     sorted_ids = jnp.sum(jnp.where(hit, ids[None, :], 0), axis=1)
-    counts = jnp.concatenate([before, upto])
-    return slots, sorted_ids, counts, query_ids * BLOCK + half * TOKENS
+    chunks = (seen + CHUNK_BLOCKS - 1) // CHUNK_BLOCKS
+    unit = jnp.arange(UNITS, dtype=jnp.int32)[:, None]
+    place = jnp.arange(4, dtype=jnp.int32)[None, :]
+    is_high = unit >= chunks[None, :4]
+    later = LOW_CHUNKS + unit - chunks[None, :4]
+    starts = query_ids * BLOCK + half * TOKENS
+    left = jnp.where(later < chunks[None, 4:], starts[None, 4:], -BLOCK)
+    unit_tiles = place + jnp.where(is_high, 4, 0)
+    unit_chunks = jnp.where(is_high, jnp.minimum(later, CHUNKS - 1), unit)
+    unit_starts = jnp.where(is_high, left, starts[None, :4])
+    return (
+        slots, sorted_ids, unit_tiles.reshape(-1), unit_chunks.reshape(-1), unit_starts.reshape(-1),
+    )
 
 
 def choose(first, second, swap):
@@ -370,8 +419,8 @@
     blocks = jnp.concatenate(choose(near, swap_half(near), half == 1), axis=1)
     my_q, their_q = columns(queries, group)
     my_g, their_g = columns(out_grad, group)
-    q_rows = jnp.concatenate([my_q, swap_group(their_q)])
-    g_rows = jnp.concatenate([my_g, swap_group(their_g)])
+    q_rows = jnp.concatenate(choose(my_q, swap_group(their_q), group == 1))
+    g_rows = jnp.concatenate(choose(my_g, swap_group(their_g), group == 1))
     pieces = gather_direct(blocks.reshape(PIECE, PAIR), "y")
     q_rows = gather_direct(q_rows, "x")
     across = jnp.concatenate(pieces)
@@ -382,7 +431,7 @@
     ).T.reshape(2, 1, ROWS)
     my_delta, their_delta = choose(row_delta[0], row_delta[1], group == 1)
     g_rows = gather_direct(g_rows, "x")
-    delta = jnp.stack([my_delta, swap_group(their_delta)])
+    delta = jnp.stack(choose(my_delta, swap_group(their_delta), group == 1))
 
     stats = call_lse(tables, delta, q_rows, pieces)
     dq_pieces, d_pieces, d_other = call_grads(
@@ -390,9 +439,8 @@
     )
 
     dq = reduce_direct(dq_pieces, "x")
-    query_grad = jnp.concatenate(
-        choose(dq[:TOKENS], swap_group(dq[TOKENS:]), group == 1), axis=1
-    )
+    my_dq, their_dq = choose(dq[:TOKENS], dq[TOKENS:], group == 1)
+    query_grad = jnp.concatenate(choose(my_dq, swap_group(their_dq), group == 1), axis=1)
 
     arrived = swap_core(d_other)
     both = reduce_direct(

time: 148 us -> 141 us (0.953)
  Pallas kernels: 53.4 us -> 42.2 us
  starting transfers between devices: 50.4 us -> 53.5 us
  waiting for transfers between devices: 35.5 us -> 34 us
    pallas_call x1, Pallas kernels: 19.8 us -> 13.4 us  [call_lse(): pl.pallas_call(lse_kernel, out_shape=jax.ShapeDtypeStruct((2 * TILES + 2,...]
    ppermute x2, waiting for transfers between devices: 10.2 us -> 4.94 us  [swap_half(): lax.ppermute(value, 'head', [(source, source ^ 1) for source in range(4)])]
    pallas_call x1, Pallas kernels: 33.6 us -> 28.8 us  [call_grads(): pl.pallas_call(grad_kernel, out_shape=(flat,) * 4 + (piece,) * PIECES + (...]
    ppermute x6, waiting for transfers between devices: 3.1 us -> 6.8 us  [swap_group(): lax.ppermute(value, 'head', [(source, source ^ 2) for source in range(4)])]
    ppermute x2, starting transfers between devices: 10.7 us -> 7.08 us  [swap_both(): lax.ppermute(value, ('head', 'zh'), [(source, source ^ 5) for source in r...]
    ppermute x18, starting transfers between devices: 24.2 us -> 26.6 us  [send(): return lax.ppermute(value, axis, ring_pairs(steps))]
    ppermute x2, starting transfers between devices: 2.57 us -> 4.79 us  [swap_z(): return lax.ppermute(value, 'zh', [(0, 1), (1, 0)])]
    ppermute x6, starting transfers between devices: 9.42 us -> 11.4 us  [swap_group(): lax.ppermute(value, 'head', [(source, source ^ 2) for source in range(4)])]
  transfers between devices with their start and end apart: 32 -> 32, of which waited for: 17 -> 13; matrix products, arithmetic and copies ran while one was open for 4% -> 5% of each run, Pallas kernels for 13% -> 10%
where the time goes in v3:
time: 141 us; the launch traced here: 140 us
  starting transfers between devices  53.5 us (38%)
  Pallas kernels  42.2 us (30%)
  waiting for transfers between devices  34 us (24%)
  other arithmetic  8.13 us (6%)
    pallas_call x1, Pallas kernels, call_grads(): pl.pallas_call(grad_kernel, out_shape=(flat,) * 4 + (piece,) * PIECES + (...  28.8 us
    ppermute x18, starting transfers between devices, send(): return lax.ppermute(value, axis, ring_pairs(steps))  26.6 us
    ppermute x18, waiting for transfers between devices, send(): return lax.ppermute(value, axis, ring_pairs(steps))  19.4 us
    pallas_call x1, Pallas kernels, call_lse(): pl.pallas_call(lse_kernel, out_shape=jax.ShapeDtypeStruct((2 * TILES + 2,...  13.4 us
    ppermute x6, starting transfers between devices, swap_group(): lax.ppermute(value, 'head', [(source, source ^ 2) for source in range(4)])  11.4 us
    ppermute x2, starting transfers between devices, swap_both(): lax.ppermute(value, ('head', 'zh'), [(source, source ^ 5) for source in r...  7.08 us
    ppermute x6, waiting for transfers between devices, swap_group(): lax.ppermute(value, 'head', [(source, source ^ 2) for source in range(4)])  6.8 us
    ppermute x2, waiting for transfers between devices, swap_half(): lax.ppermute(value, 'head', [(source, source ^ 1) for source in range(4)])  4.94 us
  transfers between devices with their start and end apart: 32, of which 13 were waited for; matrix products, arithmetic and copies ran while one was open for 5% of the time, Pallas kernels for 10%

profile of v3, /device:TPU:32, one launch (start us, length us, event | category | flops | bytes accessed | tf_op | source)
XLA Modules:
  0.0 140.1 jit_solution(1699756809783108161)
XLA Ops:
  0.7 0.8 broadcast_select_fusion.18
  1.5 5.5 %collective-permute-start.2 = (bf16[64,256]{1,0:T(8,128)(2,1)S(1)}, bf16[64,256]{1,0:T(8,128)(2,1)S(1)}, u32[]{:S(2)}, u32[]{:S(2)}) collective-permute-start(bf16[64,256]{1,0:T(8,128)(2,1)S(1)} %pad_maximum_fusion.7), channel_id=1, source_target_pairs={{0,136},{8,128},{64,200},{72,192},{128,8},{136,0},{192,72},{200,64... | collective-permute-start | bytes 98312 | tf_op jit(solution)/shard_map/ppermute | solution.py:61
  7.0 1.5 %collective-permute-start = (bf16[64,256]{1,0:T(8,128)(2,1)S(1)}, bf16[64,256]{1,0:T(8,128)(2,1)S(1)}, u32[]{:S(2)}, u32[]{:S(2)}) collective-permute-start(bf16[64,256]{1,0:T(8,128)(2,1)S(1)} %pad_maximum_fusion.7), channel_id=1, source_target_pairs={{0,128},{64,192},{128,0},{192,64},{1,129},{65,193},{129,1},{193,65... | collective-permute-start | bytes 98312 | tf_op jit(solution)/shard_map/ppermute | solution.py:49
  8.5 1.0 collective-permute-start.1
  9.5 1.0 broadcast_select_fusion.13
  10.5 2.0 %collective-permute-start.7 = (bf16[64,1024]{1,0:T(8,128)(2,1)S(1)}, bf16[64,1024]{1,0:T(8,128)(2,1)S(1)}, u32[]{:S(2)}, u32[]{:S(2)}) collective-permute-start(bf16[64,1024]{1,0:T(8,128)(2,1)S(1)} %broadcast_select_fusion.13), channel_id=1, source_target_pairs={{0,128},{64,192},{128,0},{192,64},{1,129},{65,193},{129,1},{193,65... | collective-permute-start | bytes 393224 | tf_op jit(solution)/shard_map/ppermute | solution.py:49
  12.5 1.0 broadcast_select_fusion.9
  13.5 1.1 collective-permute-start.8
  16.5 1.0 collective-permute-start.3
  17.5 6.1 %collective-permute-done.8 = bf16[64,1024]{1,0:T(8,128)(2,1)S(1)} collective-permute-done((bf16[64,1024]{1,0:T(8,128)(2,1)S(1)}, bf16[64,1024]{1,0:T(8,128)(2,1)S(1)}, u32[]{:S(2)}, u32[]{:S(2)}) %collective-permute-start.8) | collective-permute-done | bytes 131104 | tf_op jit(solution)/shard_map/ppermute | solution.py:49
  23.6 1.3 collective-permute-done.3
  24.9 3.3 %collective-permute-start.6 = (bf16[512,256]{1,0:T(8,128)(2,1)S(1)}, bf16[512,256]{1,0:T(8,128)(2,1)S(1)}, u32[]{:S(2)}, u32[]{:S(2)}) collective-permute-start(bf16[512,256]{1,0:T(8,128)(2,1)S(1)} %bitcast.47), channel_id=1, source_target_pairs={{0,4},{2,6},{4,0},{6,2},{1,5},{3,7},{5,1},{7,3},{8,12},{10,14},{12... | collective-permute-start | bytes 786440 | tf_op jit(solution)/shard_map/ppermute | solution.py:41
  28.3 3.1 %collective-permute-start.11 = (bf16[128,1024]{1,0:T(8,128)(2,1)S(1)}, bf16[128,1024]{1,0:T(8,128)(2,1)S(1)}, u32[]{:S(2)}, u32[]{:S(2)}) collective-permute-start(bf16[128,1024]{1,0:T(8,128)(2,1)S(1)} %pad_maximum_fusion.3.refs_0_), channel_id=1, source_target_pairs={{0,32},{16,48},{32,0},{48,16},{1,33},{17,49},{33,1},{49,17},{2,34}... | collective-permute-start | bytes 786440 | tf_op jit(solution)/shard_map/ppermute | solution.py:41
  31.4 1.1 collective-permute-start.10
  32.5 1.1 collective-permute-start.5
  33.6 1.0 collective-permute-start.4
  34.6 1.0 collective-permute-start.9
  35.6 3.5 %collective-permute-done.5.refs_6_.refs_14_ = bf16[512,256]{1,0:T(8,128)(2,1)S(1)} collective-permute-done((bf16[512,256]{1,0:T(8,128)(2,1)S(1)}, bf16[512,256]{1,0:T(8,128)(2,1)S(1)}, u32[]{:S(2)}, u32[]{:S(2)}) %collective-permute-start.5) | collective-permute-done | bytes 262176 | tf_op jit(solution)/shard_map/ppermute | solution.py:41
  39.1 3.4 %collective-permute-start.15 = (f32[1,512]{1,0:T(1,128)S(1)}, f32[1,512]{1,0:T(1,128)S(1)}, u32[]{:S(2)}, u32[]{:S(2)}) collective-permute-start(f32[1,512]{1,0:T(1,128)S(1)} %select_n.361), channel_id=1, source_target_pairs={{0,128},{64,192},{128,0},{192,64},{1,129},{65,193},{129,1},{193,65... | collective-permute-start | bytes 6152 | tf_op jit(solution)/shard_map/ppermute | solution.py:49
  42.5 1.1 pad_maximum_fusion
  44.8 3.1 %collective-permute-start.14 = (bf16[128,1024]{1,0:T(8,128)(2,1)S(1)}, bf16[128,1024]{1,0:T(8,128)(2,1)S(1)}, u32[]{:S(2)}, u32[]{:S(2)}) collective-permute-start(bf16[128,1024]{1,0:T(8,128)(2,1)S(1)} %pad_maximum_fusion.2.refs_4_), channel_id=1, source_target_pairs={{0,32},{16,48},{32,0},{48,16},{1,33},{17,49},{33,1},{49,17},{2,34}... | collective-permute-start | bytes 786440 | tf_op jit(solution)/shard_map/ppermute | solution.py:41
  47.9 1.1 collective-permute-start.13
  49.1 0.9 collective-permute-start.12
  50.0 13.4 %lse.1.refs_8_ = f32[18,1,512]{2,1,0:T(1,128)S(1)} custom-call(s32[32]{0:T(128)S(1)} %get-tuple-element.34.slot_ref, s32[32]{0:T(128)S(1)} %get-tuple-element.33.ids_ref, s32[20]{0:T(128)S(1)} %get-tuple-element.67.tile_ref, s32[20]{0:T(128)S(1)} %get-tuple-element.66.chunk_ref, s32[20]{0:T(128)S(1)} %get-tuple-element.65.start_ref, ...), custom_call_target="tpu_custom_call" | custom-call | flops 9126805504 | bytes 4194304 | tf_op jit(solution)/shard_map/lse/pallas_call | solution.py:308
  63.4 0.7 collective-permute-start.19
  64.1 2.6 %collective-permute-start.18 = (f32[18,1,512]{2,1,0:T(1,128)S(1)}, f32[18,1,512]{2,1,0:T(1,128)S(1)}, u32[]{:S(2)}, u32[]{:S(2)}) collective-permute-start(f32[18,1,512]{2,1,0:T(1,128)S(1)} %lse.1.refs_8_), channel_id=1, source_target_pairs={{0,48},{16,0},{32,16},{48,32},{1,49},{17,1},{33,17},{49,33},{2,50}... | collective-permute-start | bytes 110600 | tf_op jit(solution)/shard_map/ppermute | solution.py:41
  66.7 2.4 %collective-permute-done.19.refs_11_ = f32[18,1,512]{2,1,0:T(1,128)S(1)} collective-permute-done((f32[18,1,512]{2,1,0:T(1,128)S(1)}, f32[18,1,512]{2,1,0:T(1,128)S(1)}, u32[]{:S(2)}, u32[]{:S(2)}) %collective-permute-start.19) | collective-permute-done | bytes 36896 | tf_op jit(solution)/shard_map/ppermute | solution.py:41
  69.1 2.7 %collective-permute-done.17.refs_9_ = f32[18,1,512]{2,1,0:T(1,128)S(1)} collective-permute-done((f32[18,1,512]{2,1,0:T(1,128)S(1)}, f32[18,1,512]{2,1,0:T(1,128)S(1)}, u32[]{:S(2)}, u32[]{:S(2)}) %collective-permute-start.17) | collective-permute-done | bytes 36896 | tf_op jit(solution)/shard_map/ppermute | solution.py:41
  71.9 28.8 %grads.1 = (bf16[128,1024]{1,0:T(8,128)(2,1)S(1)}, bf16[128,1024]{1,0:T(8,128)(2,1)S(1)}, bf16[128,1024]{1,0:T(8,128)(2,1)S(1)}, bf16[128,1024]{1,0:T(8,128)(2,1...) custom-call(s32[32]{0:T(128)S(1)} %get-tuple-element.34.slot_ref, ...), custom_call_target="tpu_custom_call" | custom-call | flops 18253611008 | bytes 8388608 | tf_op jit(solution)/shard_map/grads/pallas_call | solution.py:333
  101.1 2.0 %collective-permute-start.21 = (bf16[128,1024]{1,0:T(8,128)(2,1)S(1)}, bf16[128,1024]{1,0:T(8,128)(2,1)S(1)}, u32[]{:S(2)}, u32[]{:S(2)}) collective-permute-start(bf16[128,1024]{1,0:T(8,128)(2,1)S(1)} %get-tuple-element.26), channel_id=1, source_target_pairs={{0,16},{16,32},{32,48},{48,0},{1,17},{17,33},{33,49},{49,1},{2,18}... | collective-permute-start | bytes 786440 | tf_op jit(solution)/shard_map/ppermute | solution.py:41
  103.1 0.8 collective-permute-start.22
  104.1 2.7 %collective-permute-start.25 = (bf16[512,256]{1,0:T(8,128)(2,1)S(1)}, bf16[512,256]{1,0:T(8,128)(2,1)S(1)}, u32[]{:S(2)}, u32[]{:S(2)}) collective-permute-start(bf16[512,256]{1,0:T(8,128)(2,1)S(1)} %get-tuple-element.35), channel_id=1, source_target_pairs={{0,6},{2,0},{4,2},{6,4},{1,7},{3,1},{5,3},{7,5},{8,14},{10,8},{12,... | collective-permute-start | bytes 786440 | tf_op jit(solution)/shard_map/ppermute | solution.py:41
  106.9 0.8 collective-permute-start.27
  107.6 2.6 %collective-permute-done.20 = bf16[128,1024]{1,0:T(8,128)(2,1)S(1)} collective-permute-done((bf16[128,1024]{1,0:T(8,128)(2,1)S(1)}, bf16[128,1024]{1,0:T(8,128)(2,1)S(1)}, u32[]{:S(2)}, u32[]{:S(2)}) %collective-permute-start.20) | collective-permute-done | bytes 262176 | tf_op jit(solution)/shard_map/ppermute | solution.py:41
  110.2 1.2 collective-permute-start.26
  111.5 5.1 %collective-permute-done.21 = bf16[128,1024]{1,0:T(8,128)(2,1)S(1)} collective-permute-done((bf16[128,1024]{1,0:T(8,128)(2,1)S(1)}, bf16[128,1024]{1,0:T(8,128)(2,1)S(1)}, u32[]{:S(2)}, u32[]{:S(2)}) %collective-permute-start.21) | collective-permute-done | bytes 262176 | tf_op jit(solution)/shard_map/ppermute | solution.py:41
  116.8 2.3 %collective-permute-start.23 = (bf16[64,1024]{1,0:T(8,128)(2,1)S(1)}, bf16[64,1024]{1,0:T(8,128)(2,1)S(1)}, u32[]{:S(2)}, u32[]{:S(2)}) collective-permute-start(bf16[64,1024]{1,0:T(8,128)(2,1)S(1)} %broadcast_select_fusion.5), channel_id=1, source_target_pairs={{0,128},{64,192},{128,0},{192,64},{1,129},{65,193},{129,1},{193,65... | collective-permute-start | bytes 393224 | tf_op jit(solution)/shard_map/ppermute | solution.py:49
  119.0 3.0 %collective-permute-done.26 = bf16[512,256]{1,0:T(8,128)(2,1)S(1)} collective-permute-done((bf16[512,256]{1,0:T(8,128)(2,1)S(1)}, bf16[512,256]{1,0:T(8,128)(2,1)S(1)}, u32[]{:S(2)}, u32[]{:S(2)}) %collective-permute-start.26) | collective-permute-done | bytes 262176 | tf_op jit(solution)/shard_map/ppermute | solution.py:41
  122.3 2.3 %collective-permute-start.28 = (bf16[4,64,256]{2,1,0:T(8,128)(2,1)S(1)}, bf16[4,64,256]{2,1,0:T(8,128)(2,1)S(1)}, u32[]{:S(2)}, u32[]{:S(2)}) collective-permute-start(bf16[4,64,256]{2,1,0:T(8,128)(2,1)S(1)} %select_bitcast_fusion), channel_id=1, source_target_pairs={{0,64},{64,0},{128,192},{192,128},{1,65},{65,1},{129,193},{193,129... | collective-permute-start | bytes 393224 | tf_op jit(solution)/shard_map/ppermute | solution.py:53
  124.6 3.6 %collective-permute-done.28 = bf16[4,64,256]{2,1,0:T(8,128)(2,1)S(1)} collective-permute-done((bf16[4,64,256]{2,1,0:T(8,128)(2,1)S(1)}, bf16[4,64,256]{2,1,0:T(8,128)(2,1)S(1)}, u32[]{:S(2)}, u32[]{:S(2)}) %collective-permute-start.28) | collective-permute-done | bytes 131104 | tf_op jit(solution)/shard_map/ppermute | solution.py:53
  128.3 3.8 %collective-permute-start.31 = (bf16[64,256]{1,0:T(8,128)(2,1)S(1)}, bf16[64,256]{1,0:T(8,128)(2,1)S(1)}, u32[]{:S(2)}, u32[]{:S(2)}) collective-permute-start(bf16[64,256]{1,0:T(8,128)(2,1)S(1)} %get-tuple-element.48), channel_id=1, source_target_pairs={{0,8},{8,0},{1,9},{9,1},{2,10},{10,2},{3,11},{11,3},{4,12},{12,4},... | collective-permute-start | bytes 98312 | tf_op jit(solution)/shard_map/ppermute | solution.py:57
  132.1 1.6 %collective-permute-start.30 = (bf16[64,256]{1,0:T(8,128)(2,1)S(1)}, bf16[64,256]{1,0:T(8,128)(2,1)S(1)}, u32[]{:S(2)}, u32[]{:S(2)}) collective-permute-start(bf16[64,256]{1,0:T(8,128)(2,1)S(1)} %get-tuple-element.49), channel_id=1, source_target_pairs={{0,136},{8,128},{64,200},{72,192},{128,8},{136,0},{192,72},{200,64... | collective-permute-start | bytes 98312 | tf_op jit(solution)/shard_map/ppermute | solution.py:61
  133.7 1.2 collective-permute-start.29
  134.9 0.7 pad_maximum_fusion.4
  135.6 0.7 collective-permute-done.31
  136.3 1.8 %collective-permute-done.30 = bf16[64,256]{1,0:T(8,128)(2,1)S(1)} collective-permute-done((bf16[64,256]{1,0:T(8,128)(2,1)S(1)}, bf16[64,256]{1,0:T(8,128)(2,1)S(1)}, u32[]{:S(2)}, u32[]{:S(2)}) %collective-permute-start.30) | collective-permute-done | bytes 32800 | tf_op jit(solution)/shard_map/ppermute | solution.py:61
  138.2 0.7 collective-permute-done.29
  138.9 0.6 pad_maximum_fusion.9
  (98 shorter events, 5.0 us)
Async XLA Ops:
  0.6 13.9 %copy-start.5 = (s32[4]{0:T(128)S(1)}, s32[4]{0:T(128)}, u32[]{:S(2)}) copy-start(s32[4]{0:T(128)} %constant.176.clone) | copy-start | bytes 52
  0.6 14.8 %copy-start.1 = (bf16[64,2048]{1,0:T(8,128)(2,1)S(1)}, bf16[64,2048]{1,0:T(8,128)(2,1)}, u32[]{:S(2)}) copy-start(bf16[64,2048]{1,0:T(8,128)(2,1)} %param.11) | copy-start | bytes 786436
  0.7 14.1 %copy-start.4 = (s32[128]{0:T(128)S(1)}, s32[128]{0:T(128)}, u32[]{:S(2)}) copy-start(s32[128]{0:T(128)} %param.12) | copy-start | bytes 1540
  0.7 14.8 %copy-start.3 = (bf16[64,2048]{1,0:T(8,128)(2,1)S(1)}, bf16[64,2048]{1,0:T(8,128)(2,1)}, u32[]{:S(2)}) copy-start(bf16[64,2048]{1,0:T(8,128)(2,1)} %param.10) | copy-start | bytes 786436
  1.5 14.9 %collective-permute-start.2 = (bf16[64,256]{1,0:T(8,128)(2,1)S(1)}, bf16[64,256]{1,0:T(8,128)(2,1)S(1)}, u32[]{:S(2)}, u32[]{:S(2)}) collective-permute-start(bf16[64,256]{1,0:T(8,128)(2,1)S(1)} %pad_maximum_fusion.7), channel_id=1, source_target_pairs={{0,136},{8,128},{64,200},{72,192},{128,8},{136,0},{192,72},{200,64... | collective-permute-start | bytes 98312 | tf_op jit(solution)/shard_map/ppermute | solution.py:61
  7.0 9.4 %collective-permute-start = (bf16[64,256]{1,0:T(8,128)(2,1)S(1)}, bf16[64,256]{1,0:T(8,128)(2,1)S(1)}, u32[]{:S(2)}, u32[]{:S(2)}) collective-permute-start(bf16[64,256]{1,0:T(8,128)(2,1)S(1)} %pad_maximum_fusion.7), channel_id=1, source_target_pairs={{0,128},{64,192},{128,0},{192,64},{1,129},{65,193},{129,1},{193,65... | collective-permute-start | bytes 98312 | tf_op jit(solution)/shard_map/ppermute | solution.py:49
  8.5 8.0 %collective-permute-start.1 = (bf16[64,256]{1,0:T(8,128)(2,1)S(1)}, bf16[64,256]{1,0:T(8,128)(2,1)S(1)}, u32[]{:S(2)}, u32[]{:S(2)}) collective-permute-start(bf16[64,256]{1,0:T(8,128)(2,1)S(1)} %get-tuple-element.58), channel_id=1, source_target_pairs={{0,8},{8,0},{1,9},{9,1},{2,10},{10,2},{3,11},{11,3},{4,12},{12,4},... | collective-permute-start | bytes 98312 | tf_op jit(solution)/shard_map/ppermute | solution.py:57
  10.5 23.1 %collective-permute-start.7 = (bf16[64,1024]{1,0:T(8,128)(2,1)S(1)}, bf16[64,1024]{1,0:T(8,128)(2,1)S(1)}, u32[]{:S(2)}, u32[]{:S(2)}) collective-permute-start(bf16[64,1024]{1,0:T(8,128)(2,1)S(1)} %broadcast_select_fusion.13), channel_id=1, source_target_pairs={{0,128},{64,192},{128,0},{192,64},{1,129},{65,193},{129,1},{193,65... | collective-permute-start | bytes 393224 | tf_op jit(solution)/shard_map/ppermute | solution.py:49
  13.5 10.1 %collective-permute-start.8 = (bf16[64,1024]{1,0:T(8,128)(2,1)S(1)}, bf16[64,1024]{1,0:T(8,128)(2,1)S(1)}, u32[]{:S(2)}, u32[]{:S(2)}) collective-permute-start(bf16[64,1024]{1,0:T(8,128)(2,1)S(1)} %broadcast_select_fusion.9), channel_id=1, source_target_pairs={{0,128},{64,192},{128,0},{192,64},{1,129},{65,193},{129,1},{193,65... | collective-permute-start | bytes 393224 | tf_op jit(solution)/shard_map/ppermute | solution.py:49
  15.5 8.1 %copy-start.2 = (bf16[64,2048]{1,0:T(8,128)(2,1)S(1)}, bf16[64,2048]{1,0:T(8,128)(2,1)}, u32[]{:S(2)}) copy-start(bf16[64,2048]{1,0:T(8,128)(2,1)} %param.7) | copy-start | bytes 786436
  16.5 8.4 %collective-permute-start.3 = (bf16[4,64,256]{2,1,0:T(8,128)(2,1)S(1)}, bf16[4,64,256]{2,1,0:T(8,128)(2,1)S(1)}, u32[]{:S(2)}, u32[]{:S(2)}) collective-permute-start(bf16[4,64,256]{2,1,0:T(8,128)(2,1)S(1)} %pad_maximum_fusion.5), channel_id=1, source_target_pairs={{0,64},{64,0},{128,192},{192,128},{1,65},{65,1},{129,193},{193,129... | collective-permute-start | bytes 393224 | tf_op jit(solution)/shard_map/ppermute | solution.py:53
  24.9 9.6 %collective-permute-start.6 = (bf16[512,256]{1,0:T(8,128)(2,1)S(1)}, bf16[512,256]{1,0:T(8,128)(2,1)S(1)}, u32[]{:S(2)}, u32[]{:S(2)}) collective-permute-start(bf16[512,256]{1,0:T(8,128)(2,1)S(1)} %bitcast.47), channel_id=1, source_target_pairs={{0,4},{2,6},{4,0},{6,2},{1,5},{3,7},{5,1},{7,3},{8,12},{10,14},{12... | collective-permute-start | bytes 786440 | tf_op jit(solution)/shard_map/ppermute | solution.py:41
  28.3 15.3 %collective-permute-start.11 = (bf16[128,1024]{1,0:T(8,128)(2,1)S(1)}, bf16[128,1024]{1,0:T(8,128)(2,1)S(1)}, u32[]{:S(2)}, u32[]{:S(2)}) collective-permute-start(bf16[128,1024]{1,0:T(8,128)(2,1)S(1)} %pad_maximum_fusion.3.refs_0_), channel_id=1, source_target_pairs={{0,32},{16,48},{32,0},{48,16},{1,33},{17,49},{33,1},{49,17},{2,34}... | collective-permute-start | bytes 786440 | tf_op jit(solution)/shard_map/ppermute | solution.py:41
  31.4 12.2 %collective-permute-start.10 = (bf16[128,1024]{1,0:T(8,128)(2,1)S(1)}, bf16[128,1024]{1,0:T(8,128)(2,1)S(1)}, u32[]{:S(2)}, u32[]{:S(2)}) collective-permute-start(bf16[128,1024]{1,0:T(8,128)(2,1)S(1)} %pad_maximum_fusion.3.refs_0_), channel_id=1, source_target_pairs={{0,48},{16,0},{32,16},{48,32},{1,49},{17,1},{33,17},{49,33},{2,50}... | collective-permute-start | bytes 786440 | tf_op jit(solution)/shard_map/ppermute | solution.py:41
  32.5 6.6 %collective-permute-start.5 = (bf16[512,256]{1,0:T(8,128)(2,1)S(1)}, bf16[512,256]{1,0:T(8,128)(2,1)S(1)}, u32[]{:S(2)}, u32[]{:S(2)}) collective-permute-start(bf16[512,256]{1,0:T(8,128)(2,1)S(1)} %bitcast.48), channel_id=1, source_target_pairs={{0,6},{2,0},{4,2},{6,4},{1,7},{3,1},{5,3},{7,5},{8,14},{10,8},{12,... | collective-permute-start | bytes 786440 | tf_op jit(solution)/shard_map/ppermute | solution.py:41
  33.6 8.9 %collective-permute-start.4 = (bf16[512,256]{1,0:T(8,128)(2,1)S(1)}, bf16[512,256]{1,0:T(8,128)(2,1)S(1)}, u32[]{:S(2)}, u32[]{:S(2)}) collective-permute-start(bf16[512,256]{1,0:T(8,128)(2,1)S(1)} %bitcast.49), channel_id=1, source_target_pairs={{0,2},{2,4},{4,6},{6,0},{1,3},{3,5},{5,7},{7,1},{8,10},{10,12},{12... | collective-permute-start | bytes 786440 | tf_op jit(solution)/shard_map/ppermute | solution.py:41
  34.6 9.0 %collective-permute-start.9 = (bf16[128,1024]{1,0:T(8,128)(2,1)S(1)}, bf16[128,1024]{1,0:T(8,128)(2,1)S(1)}, u32[]{:S(2)}, u32[]{:S(2)}) collective-permute-start(bf16[128,1024]{1,0:T(8,128)(2,1)S(1)} %pad_maximum_fusion.3.refs_0_), channel_id=1, source_target_pairs={{0,16},{16,32},{32,48},{48,0},{1,17},{17,33},{33,49},{49,1},{2,18}... | collective-permute-start | bytes 786440 | tf_op jit(solution)/shard_map/ppermute | solution.py:41
  39.1 5.7 %collective-permute-start.15 = (f32[1,512]{1,0:T(1,128)S(1)}, f32[1,512]{1,0:T(1,128)S(1)}, u32[]{:S(2)}, u32[]{:S(2)}) collective-permute-start(f32[1,512]{1,0:T(1,128)S(1)} %select_n.361), channel_id=1, source_target_pairs={{0,128},{64,192},{128,0},{192,64},{1,129},{65,193},{129,1},{193,65... | collective-permute-start | bytes 6152 | tf_op jit(solution)/shard_map/ppermute | solution.py:49
  43.6 6.4 %collective-permute-start.16 = (bf16[2048,256]{1,0:T(8,128)(2,1)}, bf16[2048,256]{1,0:T(8,128)(2,1)S(1)}, u32[]{:S(2)}, u32[]{:S(2)}) collective-permute-start(bf16[2048,256]{1,0:T(8,128)(2,1)} %pad_maximum_fusion), channel_id=1, source_target_pairs={{0,1},{1,0},{2,3},{3,2},{4,5},{5,4},{6,7},{7,6},{8,9},{9,8},{10,11... | collective-permute-start | bytes 3145736 | tf_op jit(solution)/shard_map/ppermute | solution.py:45
  44.8 21.9 %collective-permute-start.14 = (bf16[128,1024]{1,0:T(8,128)(2,1)S(1)}, bf16[128,1024]{1,0:T(8,128)(2,1)S(1)}, u32[]{:S(2)}, u32[]{:S(2)}) collective-permute-start(bf16[128,1024]{1,0:T(8,128)(2,1)S(1)} %pad_maximum_fusion.2.refs_4_), channel_id=1, source_target_pairs={{0,32},{16,48},{32,0},{48,16},{1,33},{17,49},{33,1},{49,17},{2,34}... | collective-permute-start | bytes 786440 | tf_op jit(solution)/shard_map/ppermute | solution.py:41
  47.9 18.8 %collective-permute-start.13 = (bf16[128,1024]{1,0:T(8,128)(2,1)S(1)}, bf16[128,1024]{1,0:T(8,128)(2,1)S(1)}, u32[]{:S(2)}, u32[]{:S(2)}) collective-permute-start(bf16[128,1024]{1,0:T(8,128)(2,1)S(1)} %pad_maximum_fusion.2.refs_4_), channel_id=1, source_target_pairs={{0,48},{16,0},{32,16},{48,32},{1,49},{17,1},{33,17},{49,33},{2,50}... | collective-permute-start | bytes 786440 | tf_op jit(solution)/shard_map/ppermute | solution.py:41
  49.1 17.7 %collective-permute-start.12 = (bf16[128,1024]{1,0:T(8,128)(2,1)S(1)}, bf16[128,1024]{1,0:T(8,128)(2,1)S(1)}, u32[]{:S(2)}, u32[]{:S(2)}) collective-permute-start(bf16[128,1024]{1,0:T(8,128)(2,1)S(1)} %pad_maximum_fusion.2.refs_4_), channel_id=1, source_target_pairs={{0,16},{16,32},{32,48},{48,0},{1,17},{17,33},{33,49},{49,1},{2,18}... | collective-permute-start | bytes 786440 | tf_op jit(solution)/shard_map/ppermute | solution.py:41
  49.9 13.4 %copy-start = (bf16[2048,256]{1,0:T(8,128)(2,1)}, bf16[2048,256]{1,0:T(8,128)(2,1)S(1)}, u32[]{:S(2)}) copy-start(bf16[2048,256]{1,0:T(8,128)(2,1)S(1)} %collective-permute-done.16.refs_8_.refs_16_) | copy-start | bytes 3145732
  63.4 5.8 %collective-permute-start.19 = (f32[18,1,512]{2,1,0:T(1,128)S(1)}, f32[18,1,512]{2,1,0:T(1,128)S(1)}, u32[]{:S(2)}, u32[]{:S(2)}) collective-permute-start(f32[18,1,512]{2,1,0:T(1,128)S(1)} %lse.1.refs_8_), channel_id=1, source_target_pairs={{0,32},{16,48},{32,0},{48,16},{1,33},{17,49},{33,1},{49,17},{2,34}... | collective-permute-start | bytes 110600 | tf_op jit(solution)/shard_map/ppermute | solution.py:41
  64.1 5.1 %collective-permute-start.18 = (f32[18,1,512]{2,1,0:T(1,128)S(1)}, f32[18,1,512]{2,1,0:T(1,128)S(1)}, u32[]{:S(2)}, u32[]{:S(2)}) collective-permute-start(f32[18,1,512]{2,1,0:T(1,128)S(1)} %lse.1.refs_8_), channel_id=1, source_target_pairs={{0,48},{16,0},{32,16},{48,32},{1,49},{17,1},{33,17},{49,33},{2,50}... | collective-permute-start | bytes 110600 | tf_op jit(solution)/shard_map/ppermute | solution.py:41
  66.7 5.2 %collective-permute-start.17 = (f32[18,1,512]{2,1,0:T(1,128)S(1)}, f32[18,1,512]{2,1,0:T(1,128)S(1)}, u32[]{:S(2)}, u32[]{:S(2)}) collective-permute-start(f32[18,1,512]{2,1,0:T(1,128)S(1)} %lse.1.refs_8_), channel_id=1, source_target_pairs={{0,16},{16,32},{32,48},{48,0},{1,17},{17,33},{33,49},{49,1},{2,18}... | collective-permute-start | bytes 110600 | tf_op jit(solution)/shard_map/ppermute | solution.py:41
  100.7 3.2 %collective-permute-start.24 = (bf16[2048,256]{1,0:T(8,128)(2,1)}, bf16[2048,256]{1,0:T(8,128)(2,1)S(1)}, u32[]{:S(2)}, u32[]{:S(2)}) collective-permute-start(bf16[2048,256]{1,0:T(8,128)(2,1)} %get-tuple-element.29), channel_id=1, source_target_pairs={{0,1},{1,0},{2,3},{3,2},{4,5},{5,4},{6,7},{7,6},{8,9},{9,8},{10,11... | collective-permute-start | bytes 3145736 | tf_op jit(solution)/shard_map/ppermute | solution.py:45
  101.0 9.2 %collective-permute-start.20 = (bf16[128,1024]{1,0:T(8,128)(2,1)S(1)}, bf16[128,1024]{1,0:T(8,128)(2,1)S(1)}, u32[]{:S(2)}, u32[]{:S(2)}) collective-permute-start(bf16[128,1024]{1,0:T(8,128)(2,1)S(1)} %get-tuple-element.25), channel_id=1, source_target_pairs={{0,48},{16,0},{32,16},{48,32},{1,49},{17,1},{33,17},{49,33},{2,50}... | collective-permute-start | bytes 786440 | tf_op jit(solution)/shard_map/ppermute | solution.py:41
  101.1 15.4 %collective-permute-start.21 = (bf16[128,1024]{1,0:T(8,128)(2,1)S(1)}, bf16[128,1024]{1,0:T(8,128)(2,1)S(1)}, u32[]{:S(2)}, u32[]{:S(2)}) collective-permute-start(bf16[128,1024]{1,0:T(8,128)(2,1)S(1)} %get-tuple-element.26), channel_id=1, source_target_pairs={{0,16},{16,32},{32,48},{48,0},{1,17},{17,33},{33,49},{49,1},{2,18}... | collective-permute-start | bytes 786440 | tf_op jit(solution)/shard_map/ppermute | solution.py:41
  103.1 13.4 %collective-permute-start.22 = (bf16[128,1024]{1,0:T(8,128)(2,1)S(1)}, bf16[128,1024]{1,0:T(8,128)(2,1)S(1)}, u32[]{:S(2)}, u32[]{:S(2)}) collective-permute-start(bf16[128,1024]{1,0:T(8,128)(2,1)S(1)} %get-tuple-element.27), channel_id=1, source_target_pairs={{0,32},{16,48},{32,0},{48,16},{1,33},{17,49},{33,1},{49,17},{2,34}... | collective-permute-start | bytes 786440 | tf_op jit(solution)/shard_map/ppermute | solution.py:41
  104.1 14.9 %collective-permute-start.25 = (bf16[512,256]{1,0:T(8,128)(2,1)S(1)}, bf16[512,256]{1,0:T(8,128)(2,1)S(1)}, u32[]{:S(2)}, u32[]{:S(2)}) collective-permute-start(bf16[512,256]{1,0:T(8,128)(2,1)S(1)} %get-tuple-element.35), channel_id=1, source_target_pairs={{0,6},{2,0},{4,2},{6,4},{1,7},{3,1},{5,3},{7,5},{8,14},{10,8},{12,... | collective-permute-start | bytes 786440 | tf_op jit(solution)/shard_map/ppermute | solution.py:41
  106.9 12.2 %collective-permute-start.27 = (bf16[512,256]{1,0:T(8,128)(2,1)S(1)}, bf16[512,256]{1,0:T(8,128)(2,1)S(1)}, u32[]{:S(2)}, u32[]{:S(2)}) collective-permute-start(bf16[512,256]{1,0:T(8,128)(2,1)S(1)} %get-tuple-element.36), channel_id=1, source_target_pairs={{0,4},{2,6},{4,0},{6,2},{1,5},{3,7},{5,1},{7,3},{8,12},{10,14},{12... | collective-permute-start | bytes 786440 | tf_op jit(solution)/shard_map/ppermute | solution.py:41
  110.2 11.8 %collective-permute-start.26 = (bf16[512,256]{1,0:T(8,128)(2,1)S(1)}, bf16[512,256]{1,0:T(8,128)(2,1)S(1)}, u32[]{:S(2)}, u32[]{:S(2)}) collective-permute-start(bf16[512,256]{1,0:T(8,128)(2,1)S(1)} %get-tuple-element.37), channel_id=1, source_target_pairs={{0,2},{2,4},{4,6},{6,0},{1,3},{3,5},{5,7},{7,1},{8,10},{10,12},{12... | collective-permute-start | bytes 786440 | tf_op jit(solution)/shard_map/ppermute | solution.py:41
  116.8 7.8 %collective-permute-start.23 = (bf16[64,1024]{1,0:T(8,128)(2,1)S(1)}, bf16[64,1024]{1,0:T(8,128)(2,1)S(1)}, u32[]{:S(2)}, u32[]{:S(2)}) collective-permute-start(bf16[64,1024]{1,0:T(8,128)(2,1)S(1)} %broadcast_select_fusion.5), channel_id=1, source_target_pairs={{0,128},{64,192},{128,0},{192,64},{1,129},{65,193},{129,1},{193,65... | collective-permute-start | bytes 393224 | tf_op jit(solution)/shard_map/ppermute | solution.py:49
  122.3 6.0 %collective-permute-start.28 = (bf16[4,64,256]{2,1,0:T(8,128)(2,1)S(1)}, bf16[4,64,256]{2,1,0:T(8,128)(2,1)S(1)}, u32[]{:S(2)}, u32[]{:S(2)}) collective-permute-start(bf16[4,64,256]{2,1,0:T(8,128)(2,1)S(1)} %select_bitcast_fusion), channel_id=1, source_target_pairs={{0,64},{64,0},{128,192},{192,128},{1,65},{65,1},{129,193},{193,129... | collective-permute-start | bytes 393224 | tf_op jit(solution)/shard_map/ppermute | solution.py:53
  128.3 8.0 %collective-permute-start.31 = (bf16[64,256]{1,0:T(8,128)(2,1)S(1)}, bf16[64,256]{1,0:T(8,128)(2,1)S(1)}, u32[]{:S(2)}, u32[]{:S(2)}) collective-permute-start(bf16[64,256]{1,0:T(8,128)(2,1)S(1)} %get-tuple-element.48), channel_id=1, source_target_pairs={{0,8},{8,0},{1,9},{9,1},{2,10},{10,2},{3,11},{11,3},{4,12},{12,4},... | collective-permute-start | bytes 98312 | tf_op jit(solution)/shard_map/ppermute | solution.py:57
  132.1 6.1 %collective-permute-start.30 = (bf16[64,256]{1,0:T(8,128)(2,1)S(1)}, bf16[64,256]{1,0:T(8,128)(2,1)S(1)}, u32[]{:S(2)}, u32[]{:S(2)}) collective-permute-start(bf16[64,256]{1,0:T(8,128)(2,1)S(1)} %get-tuple-element.49), channel_id=1, source_target_pairs={{0,136},{8,128},{64,200},{72,192},{128,8},{136,0},{192,72},{200,64... | collective-permute-start | bytes 98312 | tf_op jit(solution)/shard_map/ppermute | solution.py:61
  133.7 5.2 %collective-permute-start.29 = (bf16[64,256]{1,0:T(8,128)(2,1)S(1)}, bf16[64,256]{1,0:T(8,128)(2,1)S(1)}, u32[]{:S(2)}, u32[]{:S(2)}) collective-permute-start(bf16[64,256]{1,0:T(8,128)(2,1)S(1)} %get-tuple-element.50), channel_id=1, source_target_pairs={{0,128},{64,192},{128,0},{192,64},{1,129},{65,193},{129,1},{193,65... | collective-permute-start | bytes 98312 | tf_op jit(solution)/shard_map/ppermute | solution.py:49

commit v4 on v3

--- a/solution.py
+++ b/solution.py
@@ -79,6 +79,16 @@
 def reduce_direct(pieces, axis):
     arrived = [send(piece, axis, offset) for piece, offset in zip(pieces[1:], OFFSETS[1:])]
     return add(pieces[0], *arrived)
+
+
+def reduce_ring(pieces, axis):
+    own, left, right, far = pieces
+    middle = far.shape[0] // 2
+    from_right = send(far[:middle], axis, -1)
+    from_left = send(far[middle:], axis, 1)
+    left = jnp.concatenate([add(left[:middle], from_right), left[middle:]])
+    right = jnp.concatenate([right[:middle], add(right[middle:], from_left)])
+    return add(own, send(left, axis, -1), send(right, axis, 1))
 
 
 def kv_copies(pieces, other, gathered, sems, outward):
@@ -415,10 +425,12 @@
     my_values, their_values = columns(values, group)
     mine = jnp.concatenate([my_keys, my_values], axis=1)
     theirs = jnp.concatenate([their_keys, their_values], axis=1)
-    near = jnp.stack([mine, swap_group(theirs), swap_z(mine), swap_both(theirs)])
+    near = [mine, swap_group(theirs), swap_z(mine), swap_both(theirs)]
+    my_g, their_g = columns(out_grad, group)
+    their_g, *near = lax.optimization_barrier((their_g, *near))
+    near = jnp.stack(near)
     blocks = jnp.concatenate(choose(near, swap_half(near), half == 1), axis=1)
     my_q, their_q = columns(queries, group)
-    my_g, their_g = columns(out_grad, group)
     q_rows = jnp.concatenate(choose(my_q, swap_group(their_q), group == 1))
     g_rows = jnp.concatenate(choose(my_g, swap_group(their_g), group == 1))
     pieces = gather_direct(blocks.reshape(PIECE, PAIR), "y")
@@ -443,7 +455,7 @@
     query_grad = jnp.concatenate(choose(my_dq, swap_group(their_dq), group == 1), axis=1)
 
     arrived = swap_core(d_other)
-    both = reduce_direct(
+    both = reduce_ring(
         [add(piece, arrived[i * PIECE : (i + 1) * PIECE]) for i, piece in enumerate(d_pieces)], "y"
     )
     both = both.reshape(4, 2, TOKENS, PAIR)

time: 141 us -> 139 us (0.986)
  waiting for transfers between devices: 34 us -> 29 us
  other arithmetic: 8.13 us -> 10.8 us
    ppermute x18 -> x19, waiting for transfers between devices: 19.4 us -> 14.7 us  [send(): return lax.ppermute(value, axis, ring_pairs(steps))]
    ppermute x2, waiting for transfers between devices: 0.01 us -> 2.86 us  [swap_core(): return lax.ppermute(value, 'core', [(0, 1), (1, 0)])]
    reduce_sum x4, other arithmetic: 0.53 us -> 3.15 us  [lookup(): jnp.sum(jnp.where(wanted[:, None] == places[None, :], table[None, :], 0),...]
    ppermute x2, starting transfers between devices: 3.24 us -> 1 us  [swap_half(): lax.ppermute(value, 'head', [(source, source ^ 1) for source in range(4)])]
    ppermute x18 -> x19, starting transfers between devices: 26.6 us -> 28.6 us  [send(): return lax.ppermute(value, axis, ring_pairs(steps))]
    ppermute x6, waiting for transfers between devices: 6.8 us -> 5.33 us  [swap_group(): lax.ppermute(value, 'head', [(source, source ^ 2) for source in range(4)])]
  transfers between devices with their start and end apart: 32 -> 33, of which waited for: 13 -> 13; matrix products, arithmetic and copies ran while one was open for 5% -> 7% of each run, Pallas kernels for 10% -> 10%
where the time goes in v4:
time: 139 us; the launch traced here: 138 us
  starting transfers between devices  53.5 us (38%)
  Pallas kernels  42.2 us (30%)
  waiting for transfers between devices  29 us (21%)
  other arithmetic  10.8 us (8%)
    pallas_call x1, Pallas kernels, call_grads(): pl.pallas_call(grad_kernel, out_shape=(flat,) * 4 + (piece,) * PIECES + (...  28.8 us
    ppermute x19, starting transfers between devices, send(): return lax.ppermute(value, axis, ring_pairs(steps))  28.6 us
    ppermute x19, waiting for transfers between devices, send(): return lax.ppermute(value, axis, ring_pairs(steps))  14.7 us
    pallas_call x1, Pallas kernels, call_lse(): pl.pallas_call(lse_kernel, out_shape=jax.ShapeDtypeStruct((2 * TILES + 2,...  13.4 us
    ppermute x6, starting transfers between devices, swap_group(): lax.ppermute(value, 'head', [(source, source ^ 2) for source in range(4)])  11.3 us
    ppermute x2, starting transfers between devices, swap_both(): lax.ppermute(value, ('head', 'zh'), [(source, source ^ 5) for source in r...  8.48 us
    ppermute x6, waiting for transfers between devices, swap_group(): lax.ppermute(value, 'head', [(source, source ^ 2) for source in range(4)])  5.33 us
    ppermute x2, waiting for transfers between devices, swap_half(): lax.ppermute(value, 'head', [(source, source ^ 1) for source in range(4)])  4.65 us
  transfers between devices with their start and end apart: 33, of which 13 were waited for; matrix products, arithmetic and copies ran while one was open for 7% of the time, Pallas kernels for 10%

profile of v4, /device:TPU:32, one launch (start us, length us, event | category | flops | bytes accessed | tf_op | source)
XLA Modules:
  0.0 137.8 jit_solution(17602937306315702533)
XLA Ops:
  0.7 0.8 broadcast_select_fusion.16
  1.5 5.5 %collective-permute-start.2 = (bf16[64,256]{1,0:T(8,128)(2,1)S(1)}, bf16[64,256]{1,0:T(8,128)(2,1)S(1)}, u32[]{:S(2)}, u32[]{:S(2)}) collective-permute-start(bf16[64,256]{1,0:T(8,128)(2,1)S(1)} %pad_maximum_fusion.9), channel_id=1, source_target_pairs={{0,136},{8,128},{64,200},{72,192},{128,8},{136,0},{192,72},{200,64... | collective-permute-start | bytes 98312 | tf_op jit(solution)/shard_map/ppermute | solution.py:61
  7.0 1.5 %collective-permute-start = (bf16[64,256]{1,0:T(8,128)(2,1)S(1)}, bf16[64,256]{1,0:T(8,128)(2,1)S(1)}, u32[]{:S(2)}, u32[]{:S(2)}) collective-permute-start(bf16[64,256]{1,0:T(8,128)(2,1)S(1)} %pad_maximum_fusion.9), channel_id=1, source_target_pairs={{0,128},{64,192},{128,0},{192,64},{1,129},{65,193},{129,1},{193,65... | collective-permute-start | bytes 98312 | tf_op jit(solution)/shard_map/ppermute | solution.py:49
  8.5 1.0 collective-permute-start.1
  9.5 1.0 broadcast_select_fusion.9
  10.5 2.0 %collective-permute-start.8 = (bf16[64,1024]{1,0:T(8,128)(2,1)S(1)}, bf16[64,1024]{1,0:T(8,128)(2,1)S(1)}, u32[]{:S(2)}, u32[]{:S(2)}) collective-permute-start(bf16[64,1024]{1,0:T(8,128)(2,1)S(1)} %broadcast_select_fusion.9), channel_id=1, source_target_pairs={{0,128},{64,192},{128,0},{192,64},{1,129},{65,193},{129,1},{193,65... | collective-permute-start | bytes 393224 | tf_op jit(solution)/shard_map/ppermute | solution.py:49
  12.5 0.7 select_reduce_fusion.5
  13.2 0.7 select_reduce_fusion.4
  14.0 0.8 select_reduce_fusion.2
  14.8 0.8 select_reduce_fusion.3
  15.9 1.0 broadcast_select_fusion.13
  18.3 1.5 %collective-permute-start.7 = (bf16[64,1024]{1,0:T(8,128)(2,1)S(1)}, bf16[64,1024]{1,0:T(8,128)(2,1)S(1)}, u32[]{:S(2)}, u32[]{:S(2)}) collective-permute-start(bf16[64,1024]{1,0:T(8,128)(2,1)S(1)} %broadcast_select_fusion.13), channel_id=1, source_target_pairs={{0,128},{64,192},{128,0},{192,64},{1,129},{65,193},{129,1},{193,65... | collective-permute-start | bytes 393224 | tf_op jit(solution)/shard_map/ppermute | solution.py:49
  19.8 3.5 %collective-permute-done.3 = bf16[4,64,256]{2,1,0:T(8,128)(2,1)S(1)} collective-permute-done((bf16[4,64,256]{2,1,0:T(8,128)(2,1)S(1)}, bf16[4,64,256]{2,1,0:T(8,128)(2,1)S(1)}, u32[]{:S(2)}, u32[]{:S(2)}) %collective-permute-start.3) | collective-permute-done | bytes 131104 | tf_op jit(solution)/shard_map/ppermute | solution.py:53
  23.4 3.3 %collective-permute-start.6 = (bf16[512,256]{1,0:T(8,128)(2,1)S(1)}, bf16[512,256]{1,0:T(8,128)(2,1)S(1)}, u32[]{:S(2)}, u32[]{:S(2)}) collective-permute-start(bf16[512,256]{1,0:T(8,128)(2,1)S(1)} %bitcast.46), channel_id=1, source_target_pairs={{0,4},{2,6},{4,0},{6,2},{1,5},{3,7},{5,1},{7,3},{8,12},{10,14},{12... | collective-permute-start | bytes 786440 | tf_op jit(solution)/shard_map/ppermute | solution.py:41
  26.7 3.1 %collective-permute-start.11 = (bf16[128,1024]{1,0:T(8,128)(2,1)S(1)}, bf16[128,1024]{1,0:T(8,128)(2,1)S(1)}, u32[]{:S(2)}, u32[]{:S(2)}) collective-permute-start(bf16[128,1024]{1,0:T(8,128)(2,1)S(1)} %pad_maximum_fusion.3.refs_0_), channel_id=1, source_target_pairs={{0,32},{16,48},{32,0},{48,16},{1,33},{17,49},{33,1},{49,17},{2,34}... | collective-permute-start | bytes 786440 | tf_op jit(solution)/shard_map/ppermute | solution.py:41
  29.8 1.1 collective-permute-start.10
  31.0 1.1 collective-permute-start.5
  32.0 1.0 collective-permute-start.4
  33.0 1.0 collective-permute-start.9
  34.0 3.3 %collective-permute-done.5.refs_6_.refs_14_ = bf16[512,256]{1,0:T(8,128)(2,1)S(1)} collective-permute-done((bf16[512,256]{1,0:T(8,128)(2,1)S(1)}, bf16[512,256]{1,0:T(8,128)(2,1)S(1)}, u32[]{:S(2)}, u32[]{:S(2)}) %collective-permute-start.5) | collective-permute-done | bytes 262176 | tf_op jit(solution)/shard_map/ppermute | solution.py:41
  37.3 3.0 %collective-permute-start.15 = (f32[1,512]{1,0:T(1,128)S(1)}, f32[1,512]{1,0:T(1,128)S(1)}, u32[]{:S(2)}, u32[]{:S(2)}) collective-permute-start(f32[1,512]{1,0:T(1,128)S(1)} %select_n.361), channel_id=1, source_target_pairs={{0,128},{64,192},{128,0},{192,64},{1,129},{65,193},{129,1},{193,65... | collective-permute-start | bytes 6152 | tf_op jit(solution)/shard_map/ppermute | solution.py:49
  40.4 1.1 pad_maximum_fusion
  42.7 3.1 %collective-permute-start.14 = (bf16[128,1024]{1,0:T(8,128)(2,1)S(1)}, bf16[128,1024]{1,0:T(8,128)(2,1)S(1)}, u32[]{:S(2)}, u32[]{:S(2)}) collective-permute-start(bf16[128,1024]{1,0:T(8,128)(2,1)S(1)} %pad_maximum_fusion.2.refs_4_), channel_id=1, source_target_pairs={{0,32},{16,48},{32,0},{48,16},{1,33},{17,49},{33,1},{49,17},{2,34}... | collective-permute-start | bytes 786440 | tf_op jit(solution)/shard_map/ppermute | solution.py:41
  45.8 1.1 collective-permute-start.13
  47.0 0.9 collective-permute-start.12
  47.9 13.4 %lse.1.refs_8_ = f32[18,1,512]{2,1,0:T(1,128)S(1)} custom-call(s32[32]{0:T(128)S(1)} %get-tuple-element.44.slot_ref, s32[32]{0:T(128)S(1)} %get-tuple-element.43.ids_ref, s32[20]{0:T(128)S(1)} %get-tuple-element.77.tile_ref, s32[20]{0:T(128)S(1)} %get-tuple-element.76.chunk_ref, s32[20]{0:T(128)S(1)} %get-tuple-element.75.start_ref, ...), custom_call_target="tpu_custom_call" | custom-call | flops 9126805504 | bytes 4194304 | tf_op jit(solution)/shard_map/lse/pallas_call | solution.py:318
  61.9 2.4 %collective-permute-start.18 = (f32[18,1,512]{2,1,0:T(1,128)S(1)}, f32[18,1,512]{2,1,0:T(1,128)S(1)}, u32[]{:S(2)}, u32[]{:S(2)}) collective-permute-start(f32[18,1,512]{2,1,0:T(1,128)S(1)} %lse.1.refs_8_), channel_id=1, source_target_pairs={{0,48},{16,0},{32,16},{48,32},{1,49},{17,1},{33,17},{49,33},{2,50}... | collective-permute-start | bytes 110600 | tf_op jit(solution)/shard_map/ppermute | solution.py:41
  64.6 2.5 %collective-permute-done.19.refs_11_ = f32[18,1,512]{2,1,0:T(1,128)S(1)} collective-permute-done((f32[18,1,512]{2,1,0:T(1,128)S(1)}, f32[18,1,512]{2,1,0:T(1,128)S(1)}, u32[]{:S(2)}, u32[]{:S(2)}) %collective-permute-start.19) | collective-permute-done | bytes 36896 | tf_op jit(solution)/shard_map/ppermute | solution.py:41
  67.1 2.5 %collective-permute-done.17.refs_9_ = f32[18,1,512]{2,1,0:T(1,128)S(1)} collective-permute-done((f32[18,1,512]{2,1,0:T(1,128)S(1)}, f32[18,1,512]{2,1,0:T(1,128)S(1)}, u32[]{:S(2)}, u32[]{:S(2)}) %collective-permute-start.17) | collective-permute-done | bytes 36896 | tf_op jit(solution)/shard_map/ppermute | solution.py:41
  69.5 28.8 %grads.1 = (bf16[128,1024]{1,0:T(8,128)(2,1)S(1)}, bf16[128,1024]{1,0:T(8,128)(2,1)S(1)}, bf16[128,1024]{1,0:T(8,128)(2,1)S(1)}, bf16[128,1024]{1,0:T(8,128)(2,1...) custom-call(s32[32]{0:T(128)S(1)} %get-tuple-element.44.slot_ref, ...), custom_call_target="tpu_custom_call" | custom-call | flops 18253611008 | bytes 8388608 | tf_op jit(solution)/shard_map/grads/pallas_call | solution.py:343
  98.6 2.9 %collective-permute-done.24 = bf16[2048,256]{1,0:T(8,128)(2,1)S(1)} collective-permute-done((bf16[2048,256]{1,0:T(8,128)(2,1)}, bf16[2048,256]{1,0:T(8,128)(2,1)S(1)}, u32[]{:S(2)}, u32[]{:S(2)}) %collective-permute-start.24) | collective-permute-done | bytes 1048608 | tf_op jit(solution)/shard_map/ppermute | solution.py:45
  101.7 1.3 collective-permute-start.27
  103.4 1.7 %collective-permute-start.21 = (bf16[128,1024]{1,0:T(8,128)(2,1)S(1)}, bf16[128,1024]{1,0:T(8,128)(2,1)S(1)}, u32[]{:S(2)}, u32[]{:S(2)}) collective-permute-start(bf16[128,1024]{1,0:T(8,128)(2,1)S(1)} %get-tuple-element.36), channel_id=1, source_target_pairs={{0,16},{16,32},{32,48},{48,0},{1,17},{17,33},{33,49},{49,1},{2,18}... | collective-permute-start | bytes 786440 | tf_op jit(solution)/shard_map/ppermute | solution.py:41
  105.1 1.4 collective-permute-start.22
  106.5 1.8 %collective-permute-start.25 = (bf16[256,256]{1,0:T(8,128)(2,1)S(1)}, bf16[256,256]{1,0:T(8,128)(2,1)S(1)}, u32[]{:S(2)}, u32[]{:S(2)}) collective-permute-start(bf16[256,256]{1,0:T(8,128)(2,1)S(1)} %get-tuple-element.54), channel_id=1, source_target_pairs={{0,6},{2,0},{4,2},{6,4},{1,7},{3,1},{5,3},{7,5},{8,14},{10,8},{12,... | collective-permute-start | bytes 393224 | tf_op jit(solution)/shard_map/ppermute | solution.py:41
  108.7 2.8 %collective-permute-done.25 = bf16[256,256]{1,0:T(8,128)(2,1)S(1)} collective-permute-done((bf16[256,256]{1,0:T(8,128)(2,1)S(1)}, bf16[256,256]{1,0:T(8,128)(2,1)S(1)}, u32[]{:S(2)}, u32[]{:S(2)}) %collective-permute-start.25) | collective-permute-done | bytes 131104 | tf_op jit(solution)/shard_map/ppermute | solution.py:41
  111.6 3.0 %collective-permute-start.26 = (bf16[512,256]{1,0:T(8,128)(2,1)S(1)}, bf16[512,256]{1,0:T(8,128)(2,1)S(1)}, u32[]{:S(2)}, u32[]{:S(2)}) collective-permute-start(bf16[512,256]{1,0:T(8,128)(2,1)S(1)} %pad_maximum_fusion.5), channel_id=1, source_target_pairs={{0,6},{2,0},{4,2},{6,4},{1,7},{3,1},{5,3},{7,5},{8,14},{10,8},{12,... | collective-permute-start | bytes 786440 | tf_op jit(solution)/shard_map/ppermute | solution.py:41
  114.6 3.4 %collective-permute-done.21 = bf16[128,1024]{1,0:T(8,128)(2,1)S(1)} collective-permute-done((bf16[128,1024]{1,0:T(8,128)(2,1)S(1)}, bf16[128,1024]{1,0:T(8,128)(2,1)S(1)}, u32[]{:S(2)}, u32[]{:S(2)}) %collective-permute-start.21) | collective-permute-done | bytes 262176 | tf_op jit(solution)/shard_map/ppermute | solution.py:41
  118.2 2.4 %collective-permute-start.23 = (bf16[64,1024]{1,0:T(8,128)(2,1)S(1)}, bf16[64,1024]{1,0:T(8,128)(2,1)S(1)}, u32[]{:S(2)}, u32[]{:S(2)}) collective-permute-start(bf16[64,1024]{1,0:T(8,128)(2,1)S(1)} %broadcast_select_fusion.5), channel_id=1, source_target_pairs={{0,128},{64,192},{128,0},{192,64},{1,129},{65,193},{129,1},{193,65... | collective-permute-start | bytes 393224 | tf_op jit(solution)/shard_map/ppermute | solution.py:49
  121.2 3.5 %collective-permute-done.23 = bf16[64,1024]{1,0:T(8,128)(2,1)S(1)} collective-permute-done((bf16[64,1024]{1,0:T(8,128)(2,1)S(1)}, bf16[64,1024]{1,0:T(8,128)(2,1)S(1)}, u32[]{:S(2)}, u32[]{:S(2)}) %collective-permute-start.23) | collective-permute-done | bytes 131104 | tf_op jit(solution)/shard_map/ppermute | solution.py:49
  124.7 1.1 collective-permute-done.29
  125.9 2.7 %collective-permute-start.32 = (bf16[64,256]{1,0:T(8,128)(2,1)S(1)}, bf16[64,256]{1,0:T(8,128)(2,1)S(1)}, u32[]{:S(2)}, u32[]{:S(2)}) collective-permute-start(bf16[64,256]{1,0:T(8,128)(2,1)S(1)} %get-tuple-element.60), channel_id=1, source_target_pairs={{0,8},{8,0},{1,9},{9,1},{2,10},{10,2},{3,11},{11,3},{4,12},{12,4},... | collective-permute-start | bytes 98312 | tf_op jit(solution)/shard_map/ppermute | solution.py:57
  128.7 3.0 %collective-permute-start.31 = (bf16[64,256]{1,0:T(8,128)(2,1)S(1)}, bf16[64,256]{1,0:T(8,128)(2,1)S(1)}, u32[]{:S(2)}, u32[]{:S(2)}) collective-permute-start(bf16[64,256]{1,0:T(8,128)(2,1)S(1)} %get-tuple-element.61), channel_id=1, source_target_pairs={{0,136},{8,128},{64,200},{72,192},{128,8},{136,0},{192,72},{200,64... | collective-permute-start | bytes 98312 | tf_op jit(solution)/shard_map/ppermute | solution.py:61
  131.7 0.9 collective-permute-start.30
  132.5 0.7 pad_maximum_fusion.4
  133.3 0.7 collective-permute-done.32
  133.9 0.8 collective-permute-done.31
  134.7 1.8 %collective-permute-done.30 = bf16[64,256]{1,0:T(8,128)(2,1)S(1)} collective-permute-done((bf16[64,256]{1,0:T(8,128)(2,1)S(1)}, bf16[64,256]{1,0:T(8,128)(2,1)S(1)}, u32[]{:S(2)}, u32[]{:S(2)}) %collective-permute-start.30) | collective-permute-done | bytes 32800 | tf_op jit(solution)/shard_map/ppermute | solution.py:49
  (103 shorter events, 7.4 us)
Async XLA Ops:
  0.6 16.3 %copy-start.1 = (bf16[64,2048]{1,0:T(8,128)(2,1)S(1)}, bf16[64,2048]{1,0:T(8,128)(2,1)}, u32[]{:S(2)}) copy-start(bf16[64,2048]{1,0:T(8,128)(2,1)} %param.11) | copy-start | bytes 786436
  0.6 16.3 %copy-start.3 = (bf16[64,2048]{1,0:T(8,128)(2,1)S(1)}, bf16[64,2048]{1,0:T(8,128)(2,1)}, u32[]{:S(2)}) copy-start(bf16[64,2048]{1,0:T(8,128)(2,1)} %param.10) | copy-start | bytes 786436
  1.5 16.1 %collective-permute-start.2 = (bf16[64,256]{1,0:T(8,128)(2,1)S(1)}, bf16[64,256]{1,0:T(8,128)(2,1)S(1)}, u32[]{:S(2)}, u32[]{:S(2)}) collective-permute-start(bf16[64,256]{1,0:T(8,128)(2,1)S(1)} %pad_maximum_fusion.9), channel_id=1, source_target_pairs={{0,136},{8,128},{64,200},{72,192},{128,8},{136,0},{192,72},{200,64... | collective-permute-start | bytes 98312 | tf_op jit(solution)/shard_map/ppermute | solution.py:61
  7.0 10.7 %collective-permute-start = (bf16[64,256]{1,0:T(8,128)(2,1)S(1)}, bf16[64,256]{1,0:T(8,128)(2,1)S(1)}, u32[]{:S(2)}, u32[]{:S(2)}) collective-permute-start(bf16[64,256]{1,0:T(8,128)(2,1)S(1)} %pad_maximum_fusion.9), channel_id=1, source_target_pairs={{0,128},{64,192},{128,0},{192,64},{1,129},{65,193},{129,1},{193,65... | collective-permute-start | bytes 98312 | tf_op jit(solution)/shard_map/ppermute | solution.py:49
  8.5 9.2 %collective-permute-start.1 = (bf16[64,256]{1,0:T(8,128)(2,1)S(1)}, bf16[64,256]{1,0:T(8,128)(2,1)S(1)}, u32[]{:S(2)}, u32[]{:S(2)}) collective-permute-start(bf16[64,256]{1,0:T(8,128)(2,1)S(1)} %pad_maximum_fusion.8), channel_id=1, source_target_pairs={{0,8},{8,0},{1,9},{9,1},{2,10},{10,2},{3,11},{11,3},{4,12},{12,4},... | collective-permute-start | bytes 98312 | tf_op jit(solution)/shard_map/ppermute | solution.py:57
  10.5 9.4 %collective-permute-start.8 = (bf16[64,1024]{1,0:T(8,128)(2,1)S(1)}, bf16[64,1024]{1,0:T(8,128)(2,1)S(1)}, u32[]{:S(2)}, u32[]{:S(2)}) collective-permute-start(bf16[64,1024]{1,0:T(8,128)(2,1)S(1)} %broadcast_select_fusion.9), channel_id=1, source_target_pairs={{0,128},{64,192},{128,0},{192,64},{1,129},{65,193},{129,1},{193,65... | collective-permute-start | bytes 393224 | tf_op jit(solution)/shard_map/ppermute | solution.py:49
  17.0 2.8 %copy-start.2 = (bf16[64,2048]{1,0:T(8,128)(2,1)S(1)}, bf16[64,2048]{1,0:T(8,128)(2,1)}, u32[]{:S(2)}) copy-start(bf16[64,2048]{1,0:T(8,128)(2,1)} %param.7) | copy-start | bytes 786436
  17.7 5.7 %collective-permute-start.3 = (bf16[4,64,256]{2,1,0:T(8,128)(2,1)S(1)}, bf16[4,64,256]{2,1,0:T(8,128)(2,1)S(1)}, u32[]{:S(2)}, u32[]{:S(2)}) collective-permute-start(bf16[4,64,256]{2,1,0:T(8,128)(2,1)S(1)} %pad_maximum_fusion.7), channel_id=1, source_target_pairs={{0,64},{64,0},{128,192},{192,128},{1,65},{65,1},{129,193},{193,129... | collective-permute-start | bytes 393224 | tf_op jit(solution)/shard_map/ppermute | solution.py:53
  18.3 13.7 %collective-permute-start.7 = (bf16[64,1024]{1,0:T(8,128)(2,1)S(1)}, bf16[64,1024]{1,0:T(8,128)(2,1)S(1)}, u32[]{:S(2)}, u32[]{:S(2)}) collective-permute-start(bf16[64,1024]{1,0:T(8,128)(2,1)S(1)} %broadcast_select_fusion.13), channel_id=1, source_target_pairs={{0,128},{64,192},{128,0},{192,64},{1,129},{65,193},{129,1},{193,65... | collective-permute-start | bytes 393224 | tf_op jit(solution)/shard_map/ppermute | solution.py:49
  23.4 9.6 %collective-permute-start.6 = (bf16[512,256]{1,0:T(8,128)(2,1)S(1)}, bf16[512,256]{1,0:T(8,128)(2,1)S(1)}, u32[]{:S(2)}, u32[]{:S(2)}) collective-permute-start(bf16[512,256]{1,0:T(8,128)(2,1)S(1)} %bitcast.46), channel_id=1, source_target_pairs={{0,4},{2,6},{4,0},{6,2},{1,5},{3,7},{5,1},{7,3},{8,12},{10,14},{12... | collective-permute-start | bytes 786440 | tf_op jit(solution)/shard_map/ppermute | solution.py:41
  26.7 14.8 %collective-permute-start.11 = (bf16[128,1024]{1,0:T(8,128)(2,1)S(1)}, bf16[128,1024]{1,0:T(8,128)(2,1)S(1)}, u32[]{:S(2)}, u32[]{:S(2)}) collective-permute-start(bf16[128,1024]{1,0:T(8,128)(2,1)S(1)} %pad_maximum_fusion.3.refs_0_), channel_id=1, source_target_pairs={{0,32},{16,48},{32,0},{48,16},{1,33},{17,49},{33,1},{49,17},{2,34}... | collective-permute-start | bytes 786440 | tf_op jit(solution)/shard_map/ppermute | solution.py:41
  29.8 11.7 %collective-permute-start.10 = (bf16[128,1024]{1,0:T(8,128)(2,1)S(1)}, bf16[128,1024]{1,0:T(8,128)(2,1)S(1)}, u32[]{:S(2)}, u32[]{:S(2)}) collective-permute-start(bf16[128,1024]{1,0:T(8,128)(2,1)S(1)} %pad_maximum_fusion.3.refs_0_), channel_id=1, source_target_pairs={{0,48},{16,0},{32,16},{48,32},{1,49},{17,1},{33,17},{49,33},{2,50}... | collective-permute-start | bytes 786440 | tf_op jit(solution)/shard_map/ppermute | solution.py:41
  31.0 6.4 %collective-permute-start.5 = (bf16[512,256]{1,0:T(8,128)(2,1)S(1)}, bf16[512,256]{1,0:T(8,128)(2,1)S(1)}, u32[]{:S(2)}, u32[]{:S(2)}) collective-permute-start(bf16[512,256]{1,0:T(8,128)(2,1)S(1)} %bitcast.47), channel_id=1, source_target_pairs={{0,6},{2,0},{4,2},{6,4},{1,7},{3,1},{5,3},{7,5},{8,14},{10,8},{12,... | collective-permute-start | bytes 786440 | tf_op jit(solution)/shard_map/ppermute | solution.py:41
  32.0 8.4 %collective-permute-start.4 = (bf16[512,256]{1,0:T(8,128)(2,1)S(1)}, bf16[512,256]{1,0:T(8,128)(2,1)S(1)}, u32[]{:S(2)}, u32[]{:S(2)}) collective-permute-start(bf16[512,256]{1,0:T(8,128)(2,1)S(1)} %bitcast.48), channel_id=1, source_target_pairs={{0,2},{2,4},{4,6},{6,0},{1,3},{3,5},{5,7},{7,1},{8,10},{10,12},{12... | collective-permute-start | bytes 786440 | tf_op jit(solution)/shard_map/ppermute | solution.py:41
  33.0 8.4 %collective-permute-start.9 = (bf16[128,1024]{1,0:T(8,128)(2,1)S(1)}, bf16[128,1024]{1,0:T(8,128)(2,1)S(1)}, u32[]{:S(2)}, u32[]{:S(2)}) collective-permute-start(bf16[128,1024]{1,0:T(8,128)(2,1)S(1)} %pad_maximum_fusion.3.refs_0_), channel_id=1, source_target_pairs={{0,16},{16,32},{32,48},{48,0},{1,17},{17,33},{33,49},{49,1},{2,18}... | collective-permute-start | bytes 786440 | tf_op jit(solution)/shard_map/ppermute | solution.py:41
  37.3 5.3 %collective-permute-start.15 = (f32[1,512]{1,0:T(1,128)S(1)}, f32[1,512]{1,0:T(1,128)S(1)}, u32[]{:S(2)}, u32[]{:S(2)}) collective-permute-start(f32[1,512]{1,0:T(1,128)S(1)} %select_n.361), channel_id=1, source_target_pairs={{0,128},{64,192},{128,0},{192,64},{1,129},{65,193},{129,1},{193,65... | collective-permute-start | bytes 6152 | tf_op jit(solution)/shard_map/ppermute | solution.py:49
  41.5 6.4 %collective-permute-start.16 = (bf16[2048,256]{1,0:T(8,128)(2,1)}, bf16[2048,256]{1,0:T(8,128)(2,1)S(1)}, u32[]{:S(2)}, u32[]{:S(2)}) collective-permute-start(bf16[2048,256]{1,0:T(8,128)(2,1)} %pad_maximum_fusion), channel_id=1, source_target_pairs={{0,1},{1,0},{2,3},{3,2},{4,5},{5,4},{6,7},{7,6},{8,9},{9,8},{10,11... | collective-permute-start | bytes 3145736 | tf_op jit(solution)/shard_map/ppermute | solution.py:45
  42.7 21.6 %collective-permute-start.14 = (bf16[128,1024]{1,0:T(8,128)(2,1)S(1)}, bf16[128,1024]{1,0:T(8,128)(2,1)S(1)}, u32[]{:S(2)}, u32[]{:S(2)}) collective-permute-start(bf16[128,1024]{1,0:T(8,128)(2,1)S(1)} %pad_maximum_fusion.2.refs_4_), channel_id=1, source_target_pairs={{0,32},{16,48},{32,0},{48,16},{1,33},{17,49},{33,1},{49,17},{2,34}... | collective-permute-start | bytes 786440 | tf_op jit(solution)/shard_map/ppermute | solution.py:41
  45.8 18.7 %collective-permute-start.13 = (bf16[128,1024]{1,0:T(8,128)(2,1)S(1)}, bf16[128,1024]{1,0:T(8,128)(2,1)S(1)}, u32[]{:S(2)}, u32[]{:S(2)}) collective-permute-start(bf16[128,1024]{1,0:T(8,128)(2,1)S(1)} %pad_maximum_fusion.2.refs_4_), channel_id=1, source_target_pairs={{0,48},{16,0},{32,16},{48,32},{1,49},{17,1},{33,17},{49,33},{2,50}... | collective-permute-start | bytes 786440 | tf_op jit(solution)/shard_map/ppermute | solution.py:41
  47.0 17.6 %collective-permute-start.12 = (bf16[128,1024]{1,0:T(8,128)(2,1)S(1)}, bf16[128,1024]{1,0:T(8,128)(2,1)S(1)}, u32[]{:S(2)}, u32[]{:S(2)}) collective-permute-start(bf16[128,1024]{1,0:T(8,128)(2,1)S(1)} %pad_maximum_fusion.2.refs_4_), channel_id=1, source_target_pairs={{0,16},{16,32},{32,48},{48,0},{1,17},{17,33},{33,49},{49,1},{2,18}... | collective-permute-start | bytes 786440 | tf_op jit(solution)/shard_map/ppermute | solution.py:41
  47.9 13.4 %copy-start = (bf16[2048,256]{1,0:T(8,128)(2,1)}, bf16[2048,256]{1,0:T(8,128)(2,1)S(1)}, u32[]{:S(2)}) copy-start(bf16[2048,256]{1,0:T(8,128)(2,1)S(1)} %collective-permute-done.16.refs_8_.refs_16_) | copy-start | bytes 3145732
  61.3 5.8 %collective-permute-start.19 = (f32[18,1,512]{2,1,0:T(1,128)S(1)}, f32[18,1,512]{2,1,0:T(1,128)S(1)}, u32[]{:S(2)}, u32[]{:S(2)}) collective-permute-start(f32[18,1,512]{2,1,0:T(1,128)S(1)} %lse.1.refs_8_), channel_id=1, source_target_pairs={{0,32},{16,48},{32,0},{48,16},{1,33},{17,49},{33,1},{49,17},{2,34}... | collective-permute-start | bytes 110600 | tf_op jit(solution)/shard_map/ppermute | solution.py:41
  61.9 5.1 %collective-permute-start.18 = (f32[18,1,512]{2,1,0:T(1,128)S(1)}, f32[18,1,512]{2,1,0:T(1,128)S(1)}, u32[]{:S(2)}, u32[]{:S(2)}) collective-permute-start(f32[18,1,512]{2,1,0:T(1,128)S(1)} %lse.1.refs_8_), channel_id=1, source_target_pairs={{0,48},{16,0},{32,16},{48,32},{1,49},{17,1},{33,17},{49,33},{2,50}... | collective-permute-start | bytes 110600 | tf_op jit(solution)/shard_map/ppermute | solution.py:41
  64.3 5.2 %collective-permute-start.17 = (f32[18,1,512]{2,1,0:T(1,128)S(1)}, f32[18,1,512]{2,1,0:T(1,128)S(1)}, u32[]{:S(2)}, u32[]{:S(2)}) collective-permute-start(f32[18,1,512]{2,1,0:T(1,128)S(1)} %lse.1.refs_8_), channel_id=1, source_target_pairs={{0,16},{16,32},{32,48},{48,0},{1,17},{17,33},{33,49},{49,1},{2,18}... | collective-permute-start | bytes 110600 | tf_op jit(solution)/shard_map/ppermute | solution.py:41
  98.3 3.2 %collective-permute-start.24 = (bf16[2048,256]{1,0:T(8,128)(2,1)}, bf16[2048,256]{1,0:T(8,128)(2,1)S(1)}, u32[]{:S(2)}, u32[]{:S(2)}) collective-permute-start(bf16[2048,256]{1,0:T(8,128)(2,1)} %get-tuple-element.39), channel_id=1, source_target_pairs={{0,1},{1,0},{2,3},{3,2},{4,5},{5,4},{6,7},{7,6},{8,9},{9,8},{10,11... | collective-permute-start | bytes 3145736 | tf_op jit(solution)/shard_map/ppermute | solution.py:45
  101.7 6.8 %collective-permute-start.27 = (bf16[256,256]{1,0:T(8,128)(2,1)S(1)}, bf16[256,256]{1,0:T(8,128)(2,1)S(1)}, u32[]{:S(2)}, u32[]{:S(2)}) collective-permute-start(bf16[256,256]{1,0:T(8,128)(2,1)S(1)} %get-tuple-element.55), channel_id=1, source_target_pairs={{0,2},{2,4},{4,6},{6,0},{1,3},{3,5},{5,7},{7,1},{8,10},{10,12},{12... | collective-permute-start | bytes 393224 | tf_op jit(solution)/shard_map/ppermute | solution.py:41
  103.1 11.5 %collective-permute-start.20 = (bf16[128,1024]{1,0:T(8,128)(2,1)S(1)}, bf16[128,1024]{1,0:T(8,128)(2,1)S(1)}, u32[]{:S(2)}, u32[]{:S(2)}) collective-permute-start(bf16[128,1024]{1,0:T(8,128)(2,1)S(1)} %get-tuple-element.35), channel_id=1, source_target_pairs={{0,48},{16,0},{32,16},{48,32},{1,49},{17,1},{33,17},{49,33},{2,50}... | collective-permute-start | bytes 786440 | tf_op jit(solution)/shard_map/ppermute | solution.py:41
  103.4 14.6 %collective-permute-start.21 = (bf16[128,1024]{1,0:T(8,128)(2,1)S(1)}, bf16[128,1024]{1,0:T(8,128)(2,1)S(1)}, u32[]{:S(2)}, u32[]{:S(2)}) collective-permute-start(bf16[128,1024]{1,0:T(8,128)(2,1)S(1)} %get-tuple-element.36), channel_id=1, source_target_pairs={{0,16},{16,32},{32,48},{48,0},{1,17},{17,33},{33,49},{49,1},{2,18}... | collective-permute-start | bytes 786440 | tf_op jit(solution)/shard_map/ppermute | solution.py:41
  105.1 12.9 %collective-permute-start.22 = (bf16[128,1024]{1,0:T(8,128)(2,1)S(1)}, bf16[128,1024]{1,0:T(8,128)(2,1)S(1)}, u32[]{:S(2)}, u32[]{:S(2)}) collective-permute-start(bf16[128,1024]{1,0:T(8,128)(2,1)S(1)} %get-tuple-element.37), channel_id=1, source_target_pairs={{0,32},{16,48},{32,0},{48,16},{1,33},{17,49},{33,1},{49,17},{2,34}... | collective-permute-start | bytes 786440 | tf_op jit(solution)/shard_map/ppermute | solution.py:41
  106.5 5.0 %collective-permute-start.25 = (bf16[256,256]{1,0:T(8,128)(2,1)S(1)}, bf16[256,256]{1,0:T(8,128)(2,1)S(1)}, u32[]{:S(2)}, u32[]{:S(2)}) collective-permute-start(bf16[256,256]{1,0:T(8,128)(2,1)S(1)} %get-tuple-element.54), channel_id=1, source_target_pairs={{0,6},{2,0},{4,2},{6,4},{1,7},{3,1},{5,3},{7,5},{8,14},{10,8},{12,... | collective-permute-start | bytes 393224 | tf_op jit(solution)/shard_map/ppermute | solution.py:41
  108.6 12.0 %collective-permute-start.28 = (bf16[512,256]{1,0:T(8,128)(2,1)S(1)}, bf16[512,256]{1,0:T(8,128)(2,1)S(1)}, u32[]{:S(2)}, u32[]{:S(2)}) collective-permute-start(bf16[512,256]{1,0:T(8,128)(2,1)S(1)} %pad_maximum_fusion.6), channel_id=1, source_target_pairs={{0,2},{2,4},{4,6},{6,0},{1,3},{3,5},{5,7},{7,1},{8,10},{10,12},{12... | collective-permute-start | bytes 786440 | tf_op jit(solution)/shard_map/ppermute | solution.py:41
  111.6 9.1 %collective-permute-start.26 = (bf16[512,256]{1,0:T(8,128)(2,1)S(1)}, bf16[512,256]{1,0:T(8,128)(2,1)S(1)}, u32[]{:S(2)}, u32[]{:S(2)}) collective-permute-start(bf16[512,256]{1,0:T(8,128)(2,1)S(1)} %pad_maximum_fusion.5), channel_id=1, source_target_pairs={{0,6},{2,0},{4,2},{6,4},{1,7},{3,1},{5,3},{7,5},{8,14},{10,8},{12,... | collective-permute-start | bytes 786440 | tf_op jit(solution)/shard_map/ppermute | solution.py:41
  118.2 6.5 %collective-permute-start.23 = (bf16[64,1024]{1,0:T(8,128)(2,1)S(1)}, bf16[64,1024]{1,0:T(8,128)(2,1)S(1)}, u32[]{:S(2)}, u32[]{:S(2)}) collective-permute-start(bf16[64,1024]{1,0:T(8,128)(2,1)S(1)} %broadcast_select_fusion.5), channel_id=1, source_target_pairs={{0,128},{64,192},{128,0},{192,64},{1,129},{65,193},{129,1},{193,65... | collective-permute-start | bytes 393224 | tf_op jit(solution)/shard_map/ppermute | solution.py:49
  120.8 5.1 %collective-permute-start.29 = (bf16[4,64,256]{2,1,0:T(8,128)(2,1)S(1)}, bf16[4,64,256]{2,1,0:T(8,128)(2,1)S(1)}, u32[]{:S(2)}, u32[]{:S(2)}) collective-permute-start(bf16[4,64,256]{2,1,0:T(8,128)(2,1)S(1)} %select_bitcast_fusion), channel_id=1, source_target_pairs={{0,64},{64,0},{128,192},{192,128},{1,65},{65,1},{129,193},{193,129... | collective-permute-start | bytes 393224 | tf_op jit(solution)/shard_map/ppermute | solution.py:53
  125.9 8.0 %collective-permute-start.32 = (bf16[64,256]{1,0:T(8,128)(2,1)S(1)}, bf16[64,256]{1,0:T(8,128)(2,1)S(1)}, u32[]{:S(2)}, u32[]{:S(2)}) collective-permute-start(bf16[64,256]{1,0:T(8,128)(2,1)S(1)} %get-tuple-element.60), channel_id=1, source_target_pairs={{0,8},{8,0},{1,9},{9,1},{2,10},{10,2},{3,11},{11,3},{4,12},{12,4},... | collective-permute-start | bytes 98312 | tf_op jit(solution)/shard_map/ppermute | solution.py:57
  128.7 6.0 %collective-permute-start.31 = (bf16[64,256]{1,0:T(8,128)(2,1)S(1)}, bf16[64,256]{1,0:T(8,128)(2,1)S(1)}, u32[]{:S(2)}, u32[]{:S(2)}) collective-permute-start(bf16[64,256]{1,0:T(8,128)(2,1)S(1)} %get-tuple-element.61), channel_id=1, source_target_pairs={{0,136},{8,128},{64,200},{72,192},{128,8},{136,0},{192,72},{200,64... | collective-permute-start | bytes 98312 | tf_op jit(solution)/shard_map/ppermute | solution.py:61
  131.7 4.8 %collective-permute-start.30 = (bf16[64,256]{1,0:T(8,128)(2,1)S(1)}, bf16[64,256]{1,0:T(8,128)(2,1)S(1)}, u32[]{:S(2)}, u32[]{:S(2)}) collective-permute-start(bf16[64,256]{1,0:T(8,128)(2,1)S(1)} %get-tuple-element.62), channel_id=1, source_target_pairs={{0,128},{64,192},{128,0},{192,64},{1,129},{65,193},{129,1},{193,65... | collective-permute-start | bytes 98312 | tf_op jit(solution)/shard_map/ppermute | solution.py:49

commit v5 on v4

--- a/solution.py
+++ b/solution.py
@@ -436,7 +436,8 @@
     pieces = gather_direct(blocks.reshape(PIECE, PAIR), "y")
     q_rows = gather_direct(q_rows, "x")
     across = jnp.concatenate(pieces)
-    across, g_rows, *q_rows = lax.optimization_barrier((across, g_rows, *q_rows))
+    g_rows, q_rows[1] = lax.optimization_barrier((g_rows, q_rows[1]))
+    across, *q_rows = lax.optimization_barrier((across, *q_rows))
     pieces.append(swap_core(across))
     row_delta = jnp.sum(
         (wide(out_grad) * wide(outputs)).reshape(TOKENS, 2 * HEADS_HERE, HEAD_DIM), axis=2

time: 139 us -> 139 us (level)
    ppermute x19, waiting for transfers between devices: 14.7 us -> 18.4 us  [send(): return lax.ppermute(value, axis, ring_pairs(steps))]
    ppermute x2, waiting for transfers between devices: 4.65 us -> 1.16 us  [swap_half(): lax.ppermute(value, 'head', [(source, source ^ 1) for source in range(4)])]
  transfers between devices with their start and end apart: 33 -> 33, of which waited for: 13 -> 15; matrix products, arithmetic and copies ran while one was open for 7% -> 7% of each run, Pallas kernels for 10% -> 10%
where the time goes in v5:
time: 139 us; the launch traced here: 138 us
  starting transfers between devices  53.2 us (38%)
  Pallas kernels  42.2 us (30%)
  waiting for transfers between devices  29.6 us (21%)
  other arithmetic  10.8 us (8%)
    pallas_call x1, Pallas kernels, call_grads(): pl.pallas_call(grad_kernel, out_shape=(flat,) * 4 + (piece,) * PIECES + (...  28.8 us
    ppermute x19, starting transfers between devices, send(): return lax.ppermute(value, axis, ring_pairs(steps))  27.5 us
    ppermute x19, waiting for transfers between devices, send(): return lax.ppermute(value, axis, ring_pairs(steps))  18.4 us
    pallas_call x1, Pallas kernels, call_lse(): pl.pallas_call(lse_kernel, out_shape=jax.ShapeDtypeStruct((2 * TILES + 2,...  13.4 us
    ppermute x6, starting transfers between devices, swap_group(): lax.ppermute(value, 'head', [(source, source ^ 2) for source in range(4)])  12 us
    ppermute x2, starting transfers between devices, swap_both(): lax.ppermute(value, ('head', 'zh'), [(source, source ^ 5) for source in r...  8.05 us
    ppermute x6, waiting for transfers between devices, swap_group(): lax.ppermute(value, 'head', [(source, source ^ 2) for source in range(4)])  5 us
    ppermute x2, starting transfers between devices, swap_z(): return lax.ppermute(value, 'zh', [(0, 1), (1, 0)])  4.48 us
  transfers between devices with their start and end apart: 33, of which 15 were waited for; matrix products, arithmetic and copies ran while one was open for 7% of the time, Pallas kernels for 10%

profile of v5, /device:TPU:32, one launch (start us, length us, event | category | flops | bytes accessed | tf_op | source)
XLA Modules:
  0.0 138.1 jit_solution(8720628637905653804)
XLA Ops:
  0.7 0.8 broadcast_select_fusion.16
  1.5 5.5 %collective-permute-start.2 = (bf16[64,256]{1,0:T(8,128)(2,1)S(1)}, bf16[64,256]{1,0:T(8,128)(2,1)S(1)}, u32[]{:S(2)}, u32[]{:S(2)}) collective-permute-start(bf16[64,256]{1,0:T(8,128)(2,1)S(1)} %pad_maximum_fusion.9), channel_id=1, source_target_pairs={{0,136},{8,128},{64,200},{72,192},{128,8},{136,0},{192,72},{200,64... | collective-permute-start | bytes 98312 | tf_op jit(solution)/shard_map/ppermute | solution.py:61
  7.0 1.5 %collective-permute-start = (bf16[64,256]{1,0:T(8,128)(2,1)S(1)}, bf16[64,256]{1,0:T(8,128)(2,1)S(1)}, u32[]{:S(2)}, u32[]{:S(2)}) collective-permute-start(bf16[64,256]{1,0:T(8,128)(2,1)S(1)} %pad_maximum_fusion.9), channel_id=1, source_target_pairs={{0,128},{64,192},{128,0},{192,64},{1,129},{65,193},{129,1},{193,65... | collective-permute-start | bytes 98312 | tf_op jit(solution)/shard_map/ppermute | solution.py:49
  8.5 1.0 collective-permute-start.1
  9.5 1.0 broadcast_select_fusion.12
  10.5 2.0 %collective-permute-start.7 = (bf16[64,1024]{1,0:T(8,128)(2,1)S(1)}, bf16[64,1024]{1,0:T(8,128)(2,1)S(1)}, u32[]{:S(2)}, u32[]{:S(2)}) collective-permute-start(bf16[64,1024]{1,0:T(8,128)(2,1)S(1)} %broadcast_select_fusion.12), channel_id=1, source_target_pairs={{0,128},{64,192},{128,0},{192,64},{1,129},{65,193},{129,1},{193,65... | collective-permute-start | bytes 393224 | tf_op jit(solution)/shard_map/ppermute | solution.py:49
  12.5 0.7 select_reduce_fusion.5
  13.2 0.7 select_reduce_fusion.4
  14.0 0.8 select_reduce_fusion.2
  14.8 0.8 select_reduce_fusion.3
  15.9 1.0 broadcast_select_fusion.13
  17.7 0.6 collective-permute-start.3
  18.3 1.5 %collective-permute-start.8 = (bf16[64,1024]{1,0:T(8,128)(2,1)S(1)}, bf16[64,1024]{1,0:T(8,128)(2,1)S(1)}, u32[]{:S(2)}, u32[]{:S(2)}) collective-permute-start(bf16[64,1024]{1,0:T(8,128)(2,1)S(1)} %broadcast_select_fusion.13), channel_id=1, source_target_pairs={{0,128},{64,192},{128,0},{192,64},{1,129},{65,193},{129,1},{193,65... | collective-permute-start | bytes 393224 | tf_op jit(solution)/shard_map/ppermute | solution.py:49
  19.9 3.1 %collective-permute-start.11 = (bf16[128,1024]{1,0:T(8,128)(2,1)S(1)}, bf16[128,1024]{1,0:T(8,128)(2,1)S(1)}, u32[]{:S(2)}, u32[]{:S(2)}) collective-permute-start(bf16[128,1024]{1,0:T(8,128)(2,1)S(1)} %pad_maximum_fusion.2.refs_0_), channel_id=1, source_target_pairs={{0,32},{16,48},{32,0},{48,16},{1,33},{17,49},{33,1},{49,17},{2,34}... | collective-permute-start | bytes 786440 | tf_op jit(solution)/shard_map/ppermute | solution.py:41
  23.6 3.3 %collective-permute-start.6 = (bf16[512,256]{1,0:T(8,128)(2,1)S(1)}, bf16[512,256]{1,0:T(8,128)(2,1)S(1)}, u32[]{:S(2)}, u32[]{:S(2)}) collective-permute-start(bf16[512,256]{1,0:T(8,128)(2,1)S(1)} %bitcast.46), channel_id=1, source_target_pairs={{0,4},{2,6},{4,0},{6,2},{1,5},{3,7},{5,1},{7,3},{8,12},{10,14},{12... | collective-permute-start | bytes 786440 | tf_op jit(solution)/shard_map/ppermute | solution.py:41
  26.9 1.1 collective-permute-start.5
  28.0 1.0 collective-permute-start.4
  29.0 4.7 %collective-permute-done.9.refs_1_ = bf16[128,1024]{1,0:T(8,128)(2,1)S(1)} collective-permute-done((bf16[128,1024]{1,0:T(8,128)(2,1)S(1)}, bf16[128,1024]{1,0:T(8,128)(2,1)S(1)}, u32[]{:S(2)}, u32[]{:S(2)}) %collective-permute-start.9) | collective-permute-done | bytes 262176 | tf_op jit(solution)/shard_map/ppermute | solution.py:41
  34.3 2.8 %collective-permute-start.15 = (f32[1,512]{1,0:T(1,128)S(1)}, f32[1,512]{1,0:T(1,128)S(1)}, u32[]{:S(2)}, u32[]{:S(2)}) collective-permute-start(f32[1,512]{1,0:T(1,128)S(1)} %select_n.361), channel_id=1, source_target_pairs={{0,128},{64,192},{128,0},{192,64},{1,129},{65,193},{129,1},{193,65... | collective-permute-start | bytes 6152 | tf_op jit(solution)/shard_map/ppermute | solution.py:49
  37.4 1.1 pad_maximum_fusion
  38.5 2.4 %collective-permute-done.10.refs_2_ = bf16[128,1024]{1,0:T(8,128)(2,1)S(1)} collective-permute-done((bf16[128,1024]{1,0:T(8,128)(2,1)S(1)}, bf16[128,1024]{1,0:T(8,128)(2,1)S(1)}, u32[]{:S(2)}, u32[]{:S(2)}) %collective-permute-start.10) | collective-permute-done | bytes 262176 | tf_op jit(solution)/shard_map/ppermute | solution.py:41
  42.0 2.4 %collective-permute-start.14 = (bf16[128,1024]{1,0:T(8,128)(2,1)S(1)}, bf16[128,1024]{1,0:T(8,128)(2,1)S(1)}, u32[]{:S(2)}, u32[]{:S(2)}) collective-permute-start(bf16[128,1024]{1,0:T(8,128)(2,1)S(1)} %pad_maximum_fusion.3.refs_4_), channel_id=1, source_target_pairs={{0,32},{16,48},{32,0},{48,16},{1,33},{17,49},{33,1},{49,17},{2,34}... | collective-permute-start | bytes 786440 | tf_op jit(solution)/shard_map/ppermute | solution.py:41
  44.4 1.2 collective-permute-start.13
  45.6 0.9 collective-permute-start.12
  46.4 13.4 %lse.1.refs_8_ = f32[18,1,512]{2,1,0:T(1,128)S(1)} custom-call(s32[32]{0:T(128)S(1)} %get-tuple-element.46.slot_ref, s32[32]{0:T(128)S(1)} %get-tuple-element.45.ids_ref, s32[20]{0:T(128)S(1)} %get-tuple-element.79.tile_ref, s32[20]{0:T(128)S(1)} %get-tuple-element.78.chunk_ref, s32[20]{0:T(128)S(1)} %get-tuple-element.77.start_ref, ...), custom_call_target="tpu_custom_call" | custom-call | flops 9126805504 | bytes 4194304 | tf_op jit(solution)/shard_map/lse/pallas_call | solution.py:318
  59.8 1.3 collective-permute-start.19
  61.2 1.5 %collective-permute-start.18 = (f32[18,1,512]{2,1,0:T(1,128)S(1)}, f32[18,1,512]{2,1,0:T(1,128)S(1)}, u32[]{:S(2)}, u32[]{:S(2)}) collective-permute-start(f32[18,1,512]{2,1,0:T(1,128)S(1)} %lse.1.refs_8_), channel_id=1, source_target_pairs={{0,48},{16,0},{32,16},{48,32},{1,49},{17,1},{33,17},{49,33},{2,50}... | collective-permute-start | bytes 110600 | tf_op jit(solution)/shard_map/ppermute | solution.py:41
  63.2 2.4 %collective-permute-done.19.refs_11_ = f32[18,1,512]{2,1,0:T(1,128)S(1)} collective-permute-done((f32[18,1,512]{2,1,0:T(1,128)S(1)}, f32[18,1,512]{2,1,0:T(1,128)S(1)}, u32[]{:S(2)}, u32[]{:S(2)}) %collective-permute-start.19) | collective-permute-done | bytes 36896 | tf_op jit(solution)/shard_map/ppermute | solution.py:41
  65.6 2.2 %collective-permute-done.17.refs_9_ = f32[18,1,512]{2,1,0:T(1,128)S(1)} collective-permute-done((f32[18,1,512]{2,1,0:T(1,128)S(1)}, f32[18,1,512]{2,1,0:T(1,128)S(1)}, u32[]{:S(2)}, u32[]{:S(2)}) %collective-permute-start.17) | collective-permute-done | bytes 36896 | tf_op jit(solution)/shard_map/ppermute | solution.py:41
  67.8 28.8 %grads.1 = (bf16[128,1024]{1,0:T(8,128)(2,1)S(1)}, bf16[128,1024]{1,0:T(8,128)(2,1)S(1)}, bf16[128,1024]{1,0:T(8,128)(2,1)S(1)}, bf16[128,1024]{1,0:T(8,128)(2,1...) custom-call(s32[32]{0:T(128)S(1)} %get-tuple-element.46.slot_ref, ...), custom_call_target="tpu_custom_call" | custom-call | flops 18253611008 | bytes 8388608 | tf_op jit(solution)/shard_map/grads/pallas_call | solution.py:343
  97.0 2.9 %collective-permute-done.24 = bf16[2048,256]{1,0:T(8,128)(2,1)S(1)} collective-permute-done((bf16[2048,256]{1,0:T(8,128)(2,1)}, bf16[2048,256]{1,0:T(8,128)(2,1)S(1)}, u32[]{:S(2)}, u32[]{:S(2)}) %collective-permute-start.24) | collective-permute-done | bytes 1048608 | tf_op jit(solution)/shard_map/ppermute | solution.py:45
  100.0 1.7 %collective-permute-start.27 = (bf16[256,256]{1,0:T(8,128)(2,1)S(1)}, bf16[256,256]{1,0:T(8,128)(2,1)S(1)}, u32[]{:S(2)}, u32[]{:S(2)}) collective-permute-start(bf16[256,256]{1,0:T(8,128)(2,1)S(1)} %get-tuple-element.57), channel_id=1, source_target_pairs={{0,2},{2,4},{4,6},{6,0},{1,3},{3,5},{5,7},{7,1},{8,10},{10,12},{12... | collective-permute-start | bytes 393224 | tf_op jit(solution)/shard_map/ppermute | solution.py:41
  102.1 1.7 %collective-permute-start.21 = (bf16[128,1024]{1,0:T(8,128)(2,1)S(1)}, bf16[128,1024]{1,0:T(8,128)(2,1)S(1)}, u32[]{:S(2)}, u32[]{:S(2)}) collective-permute-start(bf16[128,1024]{1,0:T(8,128)(2,1)S(1)} %get-tuple-element.38), channel_id=1, source_target_pairs={{0,16},{16,32},{32,48},{48,0},{1,17},{17,33},{33,49},{49,1},{2,18}... | collective-permute-start | bytes 786440 | tf_op jit(solution)/shard_map/ppermute | solution.py:41
  103.7 1.4 collective-permute-start.22
  105.1 1.7 %collective-permute-start.25 = (bf16[256,256]{1,0:T(8,128)(2,1)S(1)}, bf16[256,256]{1,0:T(8,128)(2,1)S(1)}, u32[]{:S(2)}, u32[]{:S(2)}) collective-permute-start(bf16[256,256]{1,0:T(8,128)(2,1)S(1)} %get-tuple-element.56), channel_id=1, source_target_pairs={{0,6},{2,0},{4,2},{6,4},{1,7},{3,1},{5,3},{7,5},{8,14},{10,8},{12,... | collective-permute-start | bytes 393224 | tf_op jit(solution)/shard_map/ppermute | solution.py:41
  107.4 2.8 %collective-permute-done.25 = bf16[256,256]{1,0:T(8,128)(2,1)S(1)} collective-permute-done((bf16[256,256]{1,0:T(8,128)(2,1)S(1)}, bf16[256,256]{1,0:T(8,128)(2,1)S(1)}, u32[]{:S(2)}, u32[]{:S(2)}) %collective-permute-start.25) | collective-permute-done | bytes 131104 | tf_op jit(solution)/shard_map/ppermute | solution.py:41
  110.3 2.9 %collective-permute-start.26 = (bf16[512,256]{1,0:T(8,128)(2,1)S(1)}, bf16[512,256]{1,0:T(8,128)(2,1)S(1)}, u32[]{:S(2)}, u32[]{:S(2)}) collective-permute-start(bf16[512,256]{1,0:T(8,128)(2,1)S(1)} %pad_maximum_fusion.5), channel_id=1, source_target_pairs={{0,6},{2,0},{4,2},{6,4},{1,7},{3,1},{5,3},{7,5},{8,14},{10,8},{12,... | collective-permute-start | bytes 786440 | tf_op jit(solution)/shard_map/ppermute | solution.py:41
  113.2 3.5 %collective-permute-done.21 = bf16[128,1024]{1,0:T(8,128)(2,1)S(1)} collective-permute-done((bf16[128,1024]{1,0:T(8,128)(2,1)S(1)}, bf16[128,1024]{1,0:T(8,128)(2,1)S(1)}, u32[]{:S(2)}, u32[]{:S(2)}) %collective-permute-start.21) | collective-permute-done | bytes 262176 | tf_op jit(solution)/shard_map/ppermute | solution.py:41
  116.9 3.8 %collective-permute-start.23 = (bf16[64,1024]{1,0:T(8,128)(2,1)S(1)}, bf16[64,1024]{1,0:T(8,128)(2,1)S(1)}, u32[]{:S(2)}, u32[]{:S(2)}) collective-permute-start(bf16[64,1024]{1,0:T(8,128)(2,1)S(1)} %broadcast_select_fusion.5), channel_id=1, source_target_pairs={{0,128},{64,192},{128,0},{192,64},{1,129},{65,193},{129,1},{193,65... | collective-permute-start | bytes 393224 | tf_op jit(solution)/shard_map/ppermute | solution.py:49
  121.1 3.6 %collective-permute-done.23 = bf16[64,1024]{1,0:T(8,128)(2,1)S(1)} collective-permute-done((bf16[64,1024]{1,0:T(8,128)(2,1)S(1)}, bf16[64,1024]{1,0:T(8,128)(2,1)S(1)}, u32[]{:S(2)}, u32[]{:S(2)}) %collective-permute-start.23) | collective-permute-done | bytes 131104 | tf_op jit(solution)/shard_map/ppermute | solution.py:49
  124.7 1.2 collective-permute-done.29
  126.0 3.5 %collective-permute-start.32 = (bf16[64,256]{1,0:T(8,128)(2,1)S(1)}, bf16[64,256]{1,0:T(8,128)(2,1)S(1)}, u32[]{:S(2)}, u32[]{:S(2)}) collective-permute-start(bf16[64,256]{1,0:T(8,128)(2,1)S(1)} %get-tuple-element.62), channel_id=1, source_target_pairs={{0,8},{8,0},{1,9},{9,1},{2,10},{10,2},{3,11},{11,3},{4,12},{12,4},... | collective-permute-start | bytes 98312 | tf_op jit(solution)/shard_map/ppermute | solution.py:57
  129.4 2.6 %collective-permute-start.31 = (bf16[64,256]{1,0:T(8,128)(2,1)S(1)}, bf16[64,256]{1,0:T(8,128)(2,1)S(1)}, u32[]{:S(2)}, u32[]{:S(2)}) collective-permute-start(bf16[64,256]{1,0:T(8,128)(2,1)S(1)} %get-tuple-element.63), channel_id=1, source_target_pairs={{0,136},{8,128},{64,200},{72,192},{128,8},{136,0},{192,72},{200,64... | collective-permute-start | bytes 98312 | tf_op jit(solution)/shard_map/ppermute | solution.py:61
  132.6 0.7 pad_maximum_fusion.4
  133.9 1.6 %collective-permute-done.31 = bf16[64,256]{1,0:T(8,128)(2,1)S(1)} collective-permute-done((bf16[64,256]{1,0:T(8,128)(2,1)S(1)}, bf16[64,256]{1,0:T(8,128)(2,1)S(1)}, u32[]{:S(2)}, u32[]{:S(2)}) %collective-permute-start.31) | collective-permute-done | bytes 32800 | tf_op jit(solution)/shard_map/ppermute | solution.py:61
  135.5 1.4 collective-permute-done.30
  136.9 0.6 pad_maximum_fusion.11
  137.5 0.6 pad_maximum_fusion.10
  (103 shorter events, 7.6 us)
Async XLA Ops:
  0.6 16.3 %copy-start.1 = (bf16[64,2048]{1,0:T(8,128)(2,1)S(1)}, bf16[64,2048]{1,0:T(8,128)(2,1)}, u32[]{:S(2)}) copy-start(bf16[64,2048]{1,0:T(8,128)(2,1)} %param.11) | copy-start | bytes 786436
  0.6 16.3 %copy-start.3 = (bf16[64,2048]{1,0:T(8,128)(2,1)S(1)}, bf16[64,2048]{1,0:T(8,128)(2,1)}, u32[]{:S(2)}) copy-start(bf16[64,2048]{1,0:T(8,128)(2,1)} %param.10) | copy-start | bytes 786436
  1.5 16.1 %collective-permute-start.2 = (bf16[64,256]{1,0:T(8,128)(2,1)S(1)}, bf16[64,256]{1,0:T(8,128)(2,1)S(1)}, u32[]{:S(2)}, u32[]{:S(2)}) collective-permute-start(bf16[64,256]{1,0:T(8,128)(2,1)S(1)} %pad_maximum_fusion.9), channel_id=1, source_target_pairs={{0,136},{8,128},{64,200},{72,192},{128,8},{136,0},{192,72},{200,64... | collective-permute-start | bytes 98312 | tf_op jit(solution)/shard_map/ppermute | solution.py:61
  7.0 10.7 %collective-permute-start = (bf16[64,256]{1,0:T(8,128)(2,1)S(1)}, bf16[64,256]{1,0:T(8,128)(2,1)S(1)}, u32[]{:S(2)}, u32[]{:S(2)}) collective-permute-start(bf16[64,256]{1,0:T(8,128)(2,1)S(1)} %pad_maximum_fusion.9), channel_id=1, source_target_pairs={{0,128},{64,192},{128,0},{192,64},{1,129},{65,193},{129,1},{193,65... | collective-permute-start | bytes 98312 | tf_op jit(solution)/shard_map/ppermute | solution.py:49
  8.5 9.2 %collective-permute-start.1 = (bf16[64,256]{1,0:T(8,128)(2,1)S(1)}, bf16[64,256]{1,0:T(8,128)(2,1)S(1)}, u32[]{:S(2)}, u32[]{:S(2)}) collective-permute-start(bf16[64,256]{1,0:T(8,128)(2,1)S(1)} %pad_maximum_fusion.8), channel_id=1, source_target_pairs={{0,8},{8,0},{1,9},{9,1},{2,10},{10,2},{3,11},{11,3},{4,12},{12,4},... | collective-permute-start | bytes 98312 | tf_op jit(solution)/shard_map/ppermute | solution.py:57
  10.5 9.4 %collective-permute-start.7 = (bf16[64,1024]{1,0:T(8,128)(2,1)S(1)}, bf16[64,1024]{1,0:T(8,128)(2,1)S(1)}, u32[]{:S(2)}, u32[]{:S(2)}) collective-permute-start(bf16[64,1024]{1,0:T(8,128)(2,1)S(1)} %broadcast_select_fusion.12), channel_id=1, source_target_pairs={{0,128},{64,192},{128,0},{192,64},{1,129},{65,193},{129,1},{193,65... | collective-permute-start | bytes 393224 | tf_op jit(solution)/shard_map/ppermute | solution.py:49
  17.0 2.8 %copy-start.2 = (bf16[64,2048]{1,0:T(8,128)(2,1)S(1)}, bf16[64,2048]{1,0:T(8,128)(2,1)}, u32[]{:S(2)}) copy-start(bf16[64,2048]{1,0:T(8,128)(2,1)} %param.7) | copy-start | bytes 786436
  17.7 5.9 %collective-permute-start.3 = (bf16[4,64,256]{2,1,0:T(8,128)(2,1)S(1)}, bf16[4,64,256]{2,1,0:T(8,128)(2,1)S(1)}, u32[]{:S(2)}, u32[]{:S(2)}) collective-permute-start(bf16[4,64,256]{2,1,0:T(8,128)(2,1)S(1)} %pad_maximum_fusion.7), channel_id=1, source_target_pairs={{0,64},{64,0},{128,192},{192,128},{1,65},{65,1},{129,193},{193,129... | collective-permute-start | bytes 393224 | tf_op jit(solution)/shard_map/ppermute | solution.py:53
  18.3 9.6 %collective-permute-start.8 = (bf16[64,1024]{1,0:T(8,128)(2,1)S(1)}, bf16[64,1024]{1,0:T(8,128)(2,1)S(1)}, u32[]{:S(2)}, u32[]{:S(2)}) collective-permute-start(bf16[64,1024]{1,0:T(8,128)(2,1)S(1)} %broadcast_select_fusion.13), channel_id=1, source_target_pairs={{0,128},{64,192},{128,0},{192,64},{1,129},{65,193},{129,1},{193,65... | collective-permute-start | bytes 393224 | tf_op jit(solution)/shard_map/ppermute | solution.py:49
  19.9 18.6 %collective-permute-start.11 = (bf16[128,1024]{1,0:T(8,128)(2,1)S(1)}, bf16[128,1024]{1,0:T(8,128)(2,1)S(1)}, u32[]{:S(2)}, u32[]{:S(2)}) collective-permute-start(bf16[128,1024]{1,0:T(8,128)(2,1)S(1)} %pad_maximum_fusion.2.refs_0_), channel_id=1, source_target_pairs={{0,32},{16,48},{32,0},{48,16},{1,33},{17,49},{33,1},{49,17},{2,34}... | collective-permute-start | bytes 786440 | tf_op jit(solution)/shard_map/ppermute | solution.py:41
  23.0 10.7 %collective-permute-start.9 = (bf16[128,1024]{1,0:T(8,128)(2,1)S(1)}, bf16[128,1024]{1,0:T(8,128)(2,1)S(1)}, u32[]{:S(2)}, u32[]{:S(2)}) collective-permute-start(bf16[128,1024]{1,0:T(8,128)(2,1)S(1)} %pad_maximum_fusion.2.refs_0_), channel_id=1, source_target_pairs={{0,16},{16,32},{32,48},{48,0},{1,17},{17,33},{33,49},{49,1},{2,18}... | collective-permute-start | bytes 786440 | tf_op jit(solution)/shard_map/ppermute | solution.py:41
  23.6 10.7 %collective-permute-start.6 = (bf16[512,256]{1,0:T(8,128)(2,1)S(1)}, bf16[512,256]{1,0:T(8,128)(2,1)S(1)}, u32[]{:S(2)}, u32[]{:S(2)}) collective-permute-start(bf16[512,256]{1,0:T(8,128)(2,1)S(1)} %bitcast.46), channel_id=1, source_target_pairs={{0,4},{2,6},{4,0},{6,2},{1,5},{3,7},{5,1},{7,3},{8,12},{10,14},{12... | collective-permute-start | bytes 786440 | tf_op jit(solution)/shard_map/ppermute | solution.py:41
  26.9 10.4 %collective-permute-start.5 = (bf16[512,256]{1,0:T(8,128)(2,1)S(1)}, bf16[512,256]{1,0:T(8,128)(2,1)S(1)}, u32[]{:S(2)}, u32[]{:S(2)}) collective-permute-start(bf16[512,256]{1,0:T(8,128)(2,1)S(1)} %bitcast.47), channel_id=1, source_target_pairs={{0,6},{2,0},{4,2},{6,4},{1,7},{3,1},{5,3},{7,5},{8,14},{10,8},{12,... | collective-permute-start | bytes 786440 | tf_op jit(solution)/shard_map/ppermute | solution.py:41
  28.0 9.4 %collective-permute-start.4 = (bf16[512,256]{1,0:T(8,128)(2,1)S(1)}, bf16[512,256]{1,0:T(8,128)(2,1)S(1)}, u32[]{:S(2)}, u32[]{:S(2)}) collective-permute-start(bf16[512,256]{1,0:T(8,128)(2,1)S(1)} %bitcast.48), channel_id=1, source_target_pairs={{0,2},{2,4},{4,6},{6,0},{1,3},{3,5},{5,7},{7,1},{8,10},{10,12},{12... | collective-permute-start | bytes 786440 | tf_op jit(solution)/shard_map/ppermute | solution.py:41
  33.7 7.1 %collective-permute-start.10 = (bf16[128,1024]{1,0:T(8,128)(2,1)S(1)}, bf16[128,1024]{1,0:T(8,128)(2,1)S(1)}, u32[]{:S(2)}, u32[]{:S(2)}) collective-permute-start(bf16[128,1024]{1,0:T(8,128)(2,1)S(1)} %pad_maximum_fusion.2.refs_0_), channel_id=1, source_target_pairs={{0,48},{16,0},{32,16},{48,32},{1,49},{17,1},{33,17},{49,33},{2,50}... | collective-permute-start | bytes 786440 | tf_op jit(solution)/shard_map/ppermute | solution.py:41
  34.3 7.6 %collective-permute-start.15 = (f32[1,512]{1,0:T(1,128)S(1)}, f32[1,512]{1,0:T(1,128)S(1)}, u32[]{:S(2)}, u32[]{:S(2)}) collective-permute-start(f32[1,512]{1,0:T(1,128)S(1)} %select_n.361), channel_id=1, source_target_pairs={{0,128},{64,192},{128,0},{192,64},{1,129},{65,193},{129,1},{193,65... | collective-permute-start | bytes 6152 | tf_op jit(solution)/shard_map/ppermute | solution.py:49
  40.9 5.6 %collective-permute-start.16 = (bf16[2048,256]{1,0:T(8,128)(2,1)}, bf16[2048,256]{1,0:T(8,128)(2,1)S(1)}, u32[]{:S(2)}, u32[]{:S(2)}) collective-permute-start(bf16[2048,256]{1,0:T(8,128)(2,1)} %pad_maximum_fusion), channel_id=1, source_target_pairs={{0,1},{1,0},{2,3},{3,2},{4,5},{5,4},{6,7},{7,6},{8,9},{9,8},{10,11... | collective-permute-start | bytes 3145736 | tf_op jit(solution)/shard_map/ppermute | solution.py:45
  42.0 20.6 %collective-permute-start.14 = (bf16[128,1024]{1,0:T(8,128)(2,1)S(1)}, bf16[128,1024]{1,0:T(8,128)(2,1)S(1)}, u32[]{:S(2)}, u32[]{:S(2)}) collective-permute-start(bf16[128,1024]{1,0:T(8,128)(2,1)S(1)} %pad_maximum_fusion.3.refs_4_), channel_id=1, source_target_pairs={{0,32},{16,48},{32,0},{48,16},{1,33},{17,49},{33,1},{49,17},{2,34}... | collective-permute-start | bytes 786440 | tf_op jit(solution)/shard_map/ppermute | solution.py:41
  44.4 18.8 %collective-permute-start.13 = (bf16[128,1024]{1,0:T(8,128)(2,1)S(1)}, bf16[128,1024]{1,0:T(8,128)(2,1)S(1)}, u32[]{:S(2)}, u32[]{:S(2)}) collective-permute-start(bf16[128,1024]{1,0:T(8,128)(2,1)S(1)} %pad_maximum_fusion.3.refs_4_), channel_id=1, source_target_pairs={{0,48},{16,0},{32,16},{48,32},{1,49},{17,1},{33,17},{49,33},{2,50}... | collective-permute-start | bytes 786440 | tf_op jit(solution)/shard_map/ppermute | solution.py:41
  45.6 17.6 %collective-permute-start.12 = (bf16[128,1024]{1,0:T(8,128)(2,1)S(1)}, bf16[128,1024]{1,0:T(8,128)(2,1)S(1)}, u32[]{:S(2)}, u32[]{:S(2)}) collective-permute-start(bf16[128,1024]{1,0:T(8,128)(2,1)S(1)} %pad_maximum_fusion.3.refs_4_), channel_id=1, source_target_pairs={{0,16},{16,32},{32,48},{48,0},{1,17},{17,33},{33,49},{49,1},{2,18}... | collective-permute-start | bytes 786440 | tf_op jit(solution)/shard_map/ppermute | solution.py:41
  46.4 13.4 %copy-start = (bf16[2048,256]{1,0:T(8,128)(2,1)}, bf16[2048,256]{1,0:T(8,128)(2,1)S(1)}, u32[]{:S(2)}) copy-start(bf16[2048,256]{1,0:T(8,128)(2,1)S(1)} %collective-permute-done.16.refs_8_.refs_16_) | copy-start | bytes 3145732
  59.8 5.7 %collective-permute-start.19 = (f32[18,1,512]{2,1,0:T(1,128)S(1)}, f32[18,1,512]{2,1,0:T(1,128)S(1)}, u32[]{:S(2)}, u32[]{:S(2)}) collective-permute-start(f32[18,1,512]{2,1,0:T(1,128)S(1)} %lse.1.refs_8_), channel_id=1, source_target_pairs={{0,32},{16,48},{32,0},{48,16},{1,33},{17,49},{33,1},{49,17},{2,34}... | collective-permute-start | bytes 110600 | tf_op jit(solution)/shard_map/ppermute | solution.py:41
  61.2 4.4 %collective-permute-start.18 = (f32[18,1,512]{2,1,0:T(1,128)S(1)}, f32[18,1,512]{2,1,0:T(1,128)S(1)}, u32[]{:S(2)}, u32[]{:S(2)}) collective-permute-start(f32[18,1,512]{2,1,0:T(1,128)S(1)} %lse.1.refs_8_), channel_id=1, source_target_pairs={{0,48},{16,0},{32,16},{48,32},{1,49},{17,1},{33,17},{49,33},{2,50}... | collective-permute-start | bytes 110600 | tf_op jit(solution)/shard_map/ppermute | solution.py:41
  62.6 5.2 %collective-permute-start.17 = (f32[18,1,512]{2,1,0:T(1,128)S(1)}, f32[18,1,512]{2,1,0:T(1,128)S(1)}, u32[]{:S(2)}, u32[]{:S(2)}) collective-permute-start(f32[18,1,512]{2,1,0:T(1,128)S(1)} %lse.1.refs_8_), channel_id=1, source_target_pairs={{0,16},{16,32},{32,48},{48,0},{1,17},{17,33},{33,49},{49,1},{2,18}... | collective-permute-start | bytes 110600 | tf_op jit(solution)/shard_map/ppermute | solution.py:41
  96.6 3.2 %collective-permute-start.24 = (bf16[2048,256]{1,0:T(8,128)(2,1)}, bf16[2048,256]{1,0:T(8,128)(2,1)S(1)}, u32[]{:S(2)}, u32[]{:S(2)}) collective-permute-start(bf16[2048,256]{1,0:T(8,128)(2,1)} %get-tuple-element.41), channel_id=1, source_target_pairs={{0,1},{1,0},{2,3},{3,2},{4,5},{5,4},{6,7},{7,6},{8,9},{9,8},{10,11... | collective-permute-start | bytes 3145736 | tf_op jit(solution)/shard_map/ppermute | solution.py:45
  100.0 6.9 %collective-permute-start.27 = (bf16[256,256]{1,0:T(8,128)(2,1)S(1)}, bf16[256,256]{1,0:T(8,128)(2,1)S(1)}, u32[]{:S(2)}, u32[]{:S(2)}) collective-permute-start(bf16[256,256]{1,0:T(8,128)(2,1)S(1)} %get-tuple-element.57), channel_id=1, source_target_pairs={{0,2},{2,4},{4,6},{6,0},{1,3},{3,5},{5,7},{7,1},{8,10},{10,12},{12... | collective-permute-start | bytes 393224 | tf_op jit(solution)/shard_map/ppermute | solution.py:41
  101.7 11.5 %collective-permute-start.20 = (bf16[128,1024]{1,0:T(8,128)(2,1)S(1)}, bf16[128,1024]{1,0:T(8,128)(2,1)S(1)}, u32[]{:S(2)}, u32[]{:S(2)}) collective-permute-start(bf16[128,1024]{1,0:T(8,128)(2,1)S(1)} %get-tuple-element.37), channel_id=1, source_target_pairs={{0,48},{16,0},{32,16},{48,32},{1,49},{17,1},{33,17},{49,33},{2,50}... | collective-permute-start | bytes 786440 | tf_op jit(solution)/shard_map/ppermute | solution.py:41
  102.1 14.6 %collective-permute-start.21 = (bf16[128,1024]{1,0:T(8,128)(2,1)S(1)}, bf16[128,1024]{1,0:T(8,128)(2,1)S(1)}, u32[]{:S(2)}, u32[]{:S(2)}) collective-permute-start(bf16[128,1024]{1,0:T(8,128)(2,1)S(1)} %get-tuple-element.38), channel_id=1, source_target_pairs={{0,16},{16,32},{32,48},{48,0},{1,17},{17,33},{33,49},{49,1},{2,18}... | collective-permute-start | bytes 786440 | tf_op jit(solution)/shard_map/ppermute | solution.py:41
  103.7 12.9 %collective-permute-start.22 = (bf16[128,1024]{1,0:T(8,128)(2,1)S(1)}, bf16[128,1024]{1,0:T(8,128)(2,1)S(1)}, u32[]{:S(2)}, u32[]{:S(2)}) collective-permute-start(bf16[128,1024]{1,0:T(8,128)(2,1)S(1)} %get-tuple-element.39), channel_id=1, source_target_pairs={{0,32},{16,48},{32,0},{48,16},{1,33},{17,49},{33,1},{49,17},{2,34}... | collective-permute-start | bytes 786440 | tf_op jit(solution)/shard_map/ppermute | solution.py:41
  105.1 5.0 %collective-permute-start.25 = (bf16[256,256]{1,0:T(8,128)(2,1)S(1)}, bf16[256,256]{1,0:T(8,128)(2,1)S(1)}, u32[]{:S(2)}, u32[]{:S(2)}) collective-permute-start(bf16[256,256]{1,0:T(8,128)(2,1)S(1)} %get-tuple-element.56), channel_id=1, source_target_pairs={{0,6},{2,0},{4,2},{6,4},{1,7},{3,1},{5,3},{7,5},{8,14},{10,8},{12,... | collective-permute-start | bytes 393224 | tf_op jit(solution)/shard_map/ppermute | solution.py:41
  107.0 13.7 %collective-permute-start.28 = (bf16[512,256]{1,0:T(8,128)(2,1)S(1)}, bf16[512,256]{1,0:T(8,128)(2,1)S(1)}, u32[]{:S(2)}, u32[]{:S(2)}) collective-permute-start(bf16[512,256]{1,0:T(8,128)(2,1)S(1)} %pad_maximum_fusion.6), channel_id=1, source_target_pairs={{0,2},{2,4},{4,6},{6,0},{1,3},{3,5},{5,7},{7,1},{8,10},{10,12},{12... | collective-permute-start | bytes 786440 | tf_op jit(solution)/shard_map/ppermute | solution.py:41
  110.3 10.4 %collective-permute-start.26 = (bf16[512,256]{1,0:T(8,128)(2,1)S(1)}, bf16[512,256]{1,0:T(8,128)(2,1)S(1)}, u32[]{:S(2)}, u32[]{:S(2)}) collective-permute-start(bf16[512,256]{1,0:T(8,128)(2,1)S(1)} %pad_maximum_fusion.5), channel_id=1, source_target_pairs={{0,6},{2,0},{4,2},{6,4},{1,7},{3,1},{5,3},{7,5},{8,14},{10,8},{12,... | collective-permute-start | bytes 786440 | tf_op jit(solution)/shard_map/ppermute | solution.py:41
  116.9 7.8 %collective-permute-start.23 = (bf16[64,1024]{1,0:T(8,128)(2,1)S(1)}, bf16[64,1024]{1,0:T(8,128)(2,1)S(1)}, u32[]{:S(2)}, u32[]{:S(2)}) collective-permute-start(bf16[64,1024]{1,0:T(8,128)(2,1)S(1)} %broadcast_select_fusion.5), channel_id=1, source_target_pairs={{0,128},{64,192},{128,0},{192,64},{1,129},{65,193},{129,1},{193,65... | collective-permute-start | bytes 393224 | tf_op jit(solution)/shard_map/ppermute | solution.py:49
  120.8 5.1 %collective-permute-start.29 = (bf16[4,64,256]{2,1,0:T(8,128)(2,1)S(1)}, bf16[4,64,256]{2,1,0:T(8,128)(2,1)S(1)}, u32[]{:S(2)}, u32[]{:S(2)}) collective-permute-start(bf16[4,64,256]{2,1,0:T(8,128)(2,1)S(1)} %select_bitcast_fusion), channel_id=1, source_target_pairs={{0,64},{64,0},{128,192},{192,128},{1,65},{65,1},{129,193},{193,129... | collective-permute-start | bytes 393224 | tf_op jit(solution)/shard_map/ppermute | solution.py:53
  126.0 7.9 %collective-permute-start.32 = (bf16[64,256]{1,0:T(8,128)(2,1)S(1)}, bf16[64,256]{1,0:T(8,128)(2,1)S(1)}, u32[]{:S(2)}, u32[]{:S(2)}) collective-permute-start(bf16[64,256]{1,0:T(8,128)(2,1)S(1)} %get-tuple-element.62), channel_id=1, source_target_pairs={{0,8},{8,0},{1,9},{9,1},{2,10},{10,2},{3,11},{11,3},{4,12},{12,4},... | collective-permute-start | bytes 98312 | tf_op jit(solution)/shard_map/ppermute | solution.py:57
  129.4 6.0 %collective-permute-start.31 = (bf16[64,256]{1,0:T(8,128)(2,1)S(1)}, bf16[64,256]{1,0:T(8,128)(2,1)S(1)}, u32[]{:S(2)}, u32[]{:S(2)}) collective-permute-start(bf16[64,256]{1,0:T(8,128)(2,1)S(1)} %get-tuple-element.63), channel_id=1, source_target_pairs={{0,136},{8,128},{64,200},{72,192},{128,8},{136,0},{192,72},{200,64... | collective-permute-start | bytes 98312 | tf_op jit(solution)/shard_map/ppermute | solution.py:61
  132.0 4.8 %collective-permute-start.30 = (bf16[64,256]{1,0:T(8,128)(2,1)S(1)}, bf16[64,256]{1,0:T(8,128)(2,1)S(1)}, u32[]{:S(2)}, u32[]{:S(2)}) collective-permute-start(bf16[64,256]{1,0:T(8,128)(2,1)S(1)} %get-tuple-element.64), channel_id=1, source_target_pairs={{0,128},{64,192},{128,0},{192,64},{1,129},{65,193},{129,1},{193,65... | collective-permute-start | bytes 98312 | tf_op jit(solution)/shard_map/ppermute | solution.py:49
